TPU v7x, 128 devices: a whole 4x4x4 slice. The times are simulated.
128 devices in a mesh: dp: 4 (over y), fsdp: 32 (over x, z, core).
Axes of the slice: x: 4, y: 4, z: 4, core: 2. Of those that a mesh axis runs over, the one named last changes fastest.
Arguments:
- tokens: bfloat16 [65536, 768], P(('dp', 'fsdp')), may hold values from -24 to 24
- segment_ids: int32 [128, 512], P(('dp', 'fsdp')), may hold values from 0 to 2, never falling along the last dimension, each value on 1 to 384 neighbouring positions
- qkv_weight: bfloat16 [768, 576], P(('dp', 'fsdp')), may hold values from -0.4375 to 0.4375
- out_weight: bfloat16 [768, 768], P(('dp', 'fsdp')), may hold values from -1.75 to 1.75
- up_weight: bfloat16 [768, 768], P(('dp', 'fsdp')), may hold values from -0.4375 to 0.4375
- down_weight: bfloat16 [3072, 192], P(('dp', 'fsdp')), may hold values from -0.21875 to 0.21875
- qv_bias: bfloat16 [2, 768], P(None, ('dp', 'fsdp')), may hold values from -3 to 3
- out_bias: bfloat16 [2, 768], P(None, ('dp', 'fsdp')), may hold values from -3 to 3
- up_bias: bfloat16 [3072], P(('dp', 'fsdp')), may hold values from -3 to 3
- norm_gain: bfloat16 [2, 768], P(None, ('dp', 'fsdp')), may hold values from 0.099609375 to 1.8984375
- norm_shift: bfloat16 [2, 768], P(None, ('dp', 'fsdp')), may hold values from -3 to 3
- cotangent: bfloat16 [65536, 768], P(('dp', 'fsdp')), may hold values from -6 to 6
Outputs:
- output: bfloat16 [65536, 768], P(('dp', 'fsdp'))
- grad_tokens: float32 [65536, 768], P(('dp', 'fsdp'))
- grad_qkv_weight: float32 [768, 576], P(('dp', 'fsdp'))
- grad_out_weight: float32 [768, 768], P(('dp', 'fsdp'))
- grad_up_weight: float32 [768, 768], P(('dp', 'fsdp'))
- grad_down_weight: float32 [3072, 192], P(('dp', 'fsdp'))
- grad_qv_bias: float32 [2, 768], P(None, ('dp', 'fsdp'))
- grad_out_bias: float32 [2, 768], P(None, ('dp', 'fsdp'))
- grad_up_bias: float32 [3072], P(('dp', 'fsdp'))
- grad_norm_gain: float32 [2, 768], P(None, ('dp', 'fsdp'))
- grad_norm_shift: float32 [2, 768], P(None, ('dp', 'fsdp'))
Inputs may be any that keep to these rules, and one draw needn't show every extreme that they name: `segment_ids`: each row holds one device's tokens; ids never fall along a row, each of the ids 0, 1, 2 covers 1 to 384 tokens of every row, and one sequence of every row has exactly that many.
All inputs are finite; a program needn't handle non-finite values.
Results may differ from a plain program's by a relative error of at most 0.012.
The roundings to bfloat16 on the way count: a program that leaves them out, or rounds other values in their place, can miss the bound.
Values may be sent and summed in bfloat16 or wider, within the bound.
No kernel may reach another device: no remote copies, remote signals or barrier semaphores. Data moves between devices by JAX's collectives and lax.ppermute only.
A program may use at most 128 MiB of HBM per device.

v0:
```python
import jax
import jax.numpy as jnp
from jax import lax
from jax.sharding import PartitionSpec as P

D = 768
HEADS = 12
G = 4
HEAD = 64
DG = 192


def normalize(rows_in, gain_row, shift_row):
    centered = rows_in - jnp.mean(rows_in, axis=-1, keepdims=True)
    spread = jnp.mean(centered * centered, axis=-1, keepdims=True)
    return centered * lax.rsqrt(spread + 1e-05) * gain_row + shift_row


def gelu_exact(values):
    return jax.nn.gelu(values, approximate=False)


def grouped_dot(inputs, weight):
    row_count = inputs.shape[0]
    out_width = weight.shape[1]
    grouped_in = inputs.reshape(row_count, G, -1)
    block_weights = weight.reshape(G, -1, out_width)
    product = jnp.einsum(
        "tgi,gic->tgc", grouped_in, block_weights, preferred_element_type=jnp.float32
    )
    return product.reshape(row_count, G * out_width)


def grouped_back(inputs, weight, gradient):
    row_count = inputs.shape[0]
    out_width = weight.shape[1]
    grouped_in = inputs.reshape(row_count, G, -1)
    block_weights = weight.reshape(G, -1, out_width)
    grouped_grad = gradient.reshape(row_count, G, out_width)
    weight_grad = jnp.einsum(
        "tgi,tgc->gic", grouped_in, grouped_grad, preferred_element_type=jnp.float32
    )
    input_grad = jnp.einsum(
        "tgc,gic->tgi", grouped_grad, block_weights, preferred_element_type=jnp.float32
    )
    return (weight_grad.reshape(weight.shape), input_grad.reshape(row_count, -1))


def local(
    tokens,
    segment_ids,
    qkv_weight,
    out_weight,
    up_weight,
    down_weight,
    qv_bias,
    out_bias,
    up_bias,
    norm_gain,
    norm_shift,
    cotangent,
):
    gathered = (
        lax.all_gather(qkv_weight, ("dp", "fsdp"), axis=0, tiled=True),
        lax.all_gather(out_weight, ("dp", "fsdp"), axis=0, tiled=True),
        lax.all_gather(up_weight, ("dp", "fsdp"), axis=0, tiled=True),
        lax.all_gather(down_weight, ("dp", "fsdp"), axis=0, tiled=True),
        lax.all_gather(qv_bias, ("dp", "fsdp"), axis=1, tiled=True),
        lax.all_gather(out_bias, ("dp", "fsdp"), axis=1, tiled=True),
        lax.all_gather(up_bias, ("dp", "fsdp"), axis=0, tiled=True),
        lax.all_gather(norm_gain, ("dp", "fsdp"), axis=1, tiled=True),
        lax.all_gather(norm_shift, ("dp", "fsdp"), axis=1, tiled=True),
    )
    qkv_full, out_full, up_full, down_full, qv_full, outb_full, upb_full, gain_full, shift_full = (
        gathered
    )
    row_count = tokens.shape[0]
    scale = HEAD ** (-0.5)
    qv_float = qv_full.astype(jnp.float32)
    bias_out = outb_full.astype(jnp.float32)
    gain_float = gain_full.astype(jnp.float32)
    shift_float = shift_full.astype(jnp.float32)
    packed = grouped_dot(tokens, qkv_full).reshape(row_count, G, 3, DG)
    queries = (packed[:, :, 0].reshape(row_count, D) + qv_float[0]).astype(jnp.bfloat16)
    keys_low = packed[:, :, 1].reshape(row_count, D).astype(jnp.bfloat16)
    values = (packed[:, :, 2].reshape(row_count, D) + qv_float[1]).astype(jnp.bfloat16)
    query_heads = queries.reshape(row_count, HEADS, HEAD)
    key_heads = keys_low.reshape(row_count, HEADS, HEAD)
    value_heads = values.reshape(row_count, HEADS, HEAD)
    scores = (
        jnp.einsum("qhd,khd->hqk", query_heads, key_heads, preferred_element_type=jnp.float32)
        * scale
    )
    same_seq = segment_ids[0][:, None] == segment_ids[0][None, :]
    scores = jnp.where(same_seq[None], scores, -1000000000.0)
    row_max = jnp.max(scores, axis=-1, keepdims=True)
    exponent = jnp.exp(scores - row_max)
    attn_probs = exponent / jnp.sum(exponent, axis=-1, keepdims=True)
    probs_low = attn_probs.astype(jnp.bfloat16)
    context = jnp.einsum("hqk,khd->qhd", probs_low, value_heads, preferred_element_type=jnp.float32)
    context = context.reshape(row_count, D).astype(jnp.bfloat16)
    attended = jnp.dot(context, out_full, preferred_element_type=jnp.float32) + bias_out[0]
    sum_first = tokens.astype(jnp.float32) + attended
    first_norm, first_back = jax.vjp(normalize, sum_first, gain_float[0], shift_float[0])
    first_low = first_norm.astype(jnp.bfloat16)
    upper_in = grouped_dot(first_low, up_full) + upb_full.astype(jnp.float32)
    active = gelu_exact(upper_in).astype(jnp.bfloat16)
    branch = grouped_dot(active, down_full) + bias_out[1]
    sum_second = first_norm + branch
    result, second_back = jax.vjp(normalize, sum_second, gain_float[1], shift_float[1])
    output = result.astype(jnp.bfloat16)
    qkv_back, out_back, up_back, down_back = (
        lax.all_gather(qkv_weight, ("dp", "fsdp"), axis=0, tiled=True),
        lax.all_gather(out_weight, ("dp", "fsdp"), axis=0, tiled=True),
        lax.all_gather(up_weight, ("dp", "fsdp"), axis=0, tiled=True),
        lax.all_gather(down_weight, ("dp", "fsdp"), axis=0, tiled=True),
    )
    d_second, grad_gain_two, grad_shift_two = second_back(cotangent.astype(jnp.float32))
    d_branch = d_second.astype(jnp.bfloat16)
    grad_outb_two = jnp.sum(d_branch.astype(jnp.float32), axis=0)
    grad_down, d_active = grouped_back(active, down_back, d_branch)
    unused_value, gelu_back = jax.vjp(gelu_exact, upper_in)
    d_upper = gelu_back(d_active)[0].astype(jnp.bfloat16)
    grad_upb = jnp.sum(d_upper.astype(jnp.float32), axis=0)
    grad_up, d_hidden = grouped_back(first_low, up_back, d_upper)
    d_first = d_second + d_hidden
    d_sum_first, grad_gain_one, grad_shift_one = first_back(d_first)
    d_attended = d_sum_first.astype(jnp.bfloat16)
    grad_out = jnp.einsum("tc,td->cd", context, d_attended, preferred_element_type=jnp.float32)
    d_context = jnp.einsum(
        "td,cd->tc", d_attended, out_back, preferred_element_type=jnp.float32
    ).astype(jnp.bfloat16)
    d_context_heads = d_context.reshape(row_count, HEADS, HEAD)
    d_probs = jnp.einsum(
        "qhd,khd->hqk", d_context_heads, value_heads, preferred_element_type=jnp.float32
    )
    d_values = jnp.einsum(
        "hqk,qhd->khd", probs_low, d_context_heads, preferred_element_type=jnp.float32
    )
    d_values = d_values.reshape(row_count, D).astype(jnp.bfloat16)
    d_scores = attn_probs * (d_probs - jnp.sum(d_probs * attn_probs, axis=-1, keepdims=True))
    d_scores = d_scores.astype(jnp.bfloat16)
    d_queries = (
        jnp.einsum("hqk,khd->qhd", d_scores, key_heads, preferred_element_type=jnp.float32) * scale
    )
    d_queries = d_queries.reshape(row_count, D).astype(jnp.bfloat16)
    d_keys = (
        jnp.einsum("hqk,qhd->khd", d_scores, query_heads, preferred_element_type=jnp.float32)
        * scale
    )
    d_keys = d_keys.reshape(row_count, D).astype(jnp.bfloat16)
    d_packed = jnp.stack(
        [
            d_queries.reshape(row_count, G, DG),
            d_keys.reshape(row_count, G, DG),
            d_values.reshape(row_count, G, DG),
        ],
        axis=2,
    )
    d_packed = d_packed.reshape(row_count, G * 3 * DG)
    grad_qkv, d_tokens_in = grouped_back(tokens, qkv_back, d_packed)
    grad_tokens = d_sum_first + d_tokens_in
    grad_qvb = jnp.stack(
        [
            jnp.sum(d_queries.astype(jnp.float32), axis=0),
            jnp.sum(d_values.astype(jnp.float32), axis=0),
        ]
    )
    grad_outb = jnp.stack([jnp.sum(d_attended.astype(jnp.float32), axis=0), grad_outb_two])
    grad_gain = jnp.stack([grad_gain_one, grad_gain_two])
    grad_shift = jnp.stack([grad_shift_one, grad_shift_two])
    summed = (
        lax.psum_scatter(grad_qkv, ("dp", "fsdp"), scatter_dimension=0, tiled=True),
        lax.psum_scatter(grad_out, ("dp", "fsdp"), scatter_dimension=0, tiled=True),
        lax.psum_scatter(grad_up, ("dp", "fsdp"), scatter_dimension=0, tiled=True),
        lax.psum_scatter(grad_down, ("dp", "fsdp"), scatter_dimension=0, tiled=True),
        lax.psum_scatter(grad_qvb, ("dp", "fsdp"), scatter_dimension=1, tiled=True),
        lax.psum_scatter(grad_outb, ("dp", "fsdp"), scatter_dimension=1, tiled=True),
        lax.psum_scatter(grad_upb, ("dp", "fsdp"), scatter_dimension=0, tiled=True),
        lax.psum_scatter(grad_gain, ("dp", "fsdp"), scatter_dimension=1, tiled=True),
        lax.psum_scatter(grad_shift, ("dp", "fsdp"), scatter_dimension=1, tiled=True),
    )
    own_qkv, own_out, own_up, own_down, own_qvb, own_outb, own_upb, own_gain, own_shift = summed
    return (
        output,
        grad_tokens,
        own_qkv,
        own_out,
        own_up,
        own_down,
        own_qvb,
        own_outb,
        own_upb,
        own_gain,
        own_shift,
    )


def solution(mesh):
    in_specs = (
        P(("dp", "fsdp"), None),
        P(("dp", "fsdp"), None),
        P(("dp", "fsdp"), None),
        P(("dp", "fsdp"), None),
        P(("dp", "fsdp"), None),
        P(("dp", "fsdp"), None),
        P(None, ("dp", "fsdp")),
        P(None, ("dp", "fsdp")),
        P(("dp", "fsdp")),
        P(None, ("dp", "fsdp")),
        P(None, ("dp", "fsdp")),
        P(("dp", "fsdp"), None),
    )
    out_specs = (
        P(("dp", "fsdp"), None),
        P(("dp", "fsdp"), None),
        P(("dp", "fsdp"), None),
        P(("dp", "fsdp"), None),
        P(("dp", "fsdp"), None),
        P(("dp", "fsdp"), None),
        P(None, ("dp", "fsdp")),
        P(None, ("dp", "fsdp")),
        P(("dp", "fsdp")),
        P(None, ("dp", "fsdp")),
        P(None, ("dp", "fsdp")),
    )
    return jax.shard_map(local, mesh=mesh, in_specs=in_specs, out_specs=out_specs, check_vma=False)
```

profile of v0, /device:TPU:0, one launch (start us, length us, event | category | flops | bytes accessed | tf_op | source)
XLA Modules:
  0.0 977.3 jit_solution(5132997014274182251)
XLA Ops:
  10.9 38.6 %all-gather = bf16[128,6,576]{2,1,0:T(8,128)(2,1)S(1)} all-gather(bf16[1,6,576]{2,1,0:T(8,128)(2,1)} %bitcast.225), channel_id=1, replica_groups=mesh['dp'=4,'fsdp'=32] {'dp','fsdp'}, dimensions={0}, use_global_device_ids=true | all-gather | bytes 891648 | tf_op jit(solution)/shard_map/all_gather | solution.py:64
  53.0 64.8 %all-reduce = bf16[3072]{0:T(1024)(128)(2,1)S(1)} all-reduce(bf16[3072]{0:T(1024)(128)(2,1)S(1)} %dynamic-update-slice), channel_id=1, replica_groups=mesh['dp'=4,'fsdp'=32] {'dp','fsdp'}, use_global_device_ids=true, to_apply=%add | all-reduce | flops 3072 | bytes 12288
  118.4 28.3 %all-gather.1 = bf16[128,6,2]{1,2,0:T(2,128)(2,1)S(1)} all-gather(bf16[1,6,2]{1,2,0:T(2,128)(2,1)S(1)} %bitcast.227), channel_id=1, replica_groups=mesh['dp'=4,'fsdp'=32] {'dp','fsdp'}, dimensions={0}, use_global_device_ids=true | all-gather | bytes 3096 | tf_op jit(solution)/shard_map/all_gather | solution.py:68
  146.8 29.1 %all-gather.3 = bf16[128,6,2]{1,2,0:T(2,128)(2,1)S(1)} all-gather(bf16[1,6,2]{1,2,0:T(2,128)(2,1)S(1)} %bitcast.228), channel_id=1, replica_groups=mesh['dp'=4,'fsdp'=32] {'dp','fsdp'}, dimensions={0}, use_global_device_ids=true | all-gather | bytes 3096 | tf_op jit(solution)/shard_map/all_gather | solution.py:69
  176.0 30.1 %all-gather.4 = bf16[128,6,2]{1,2,0:T(2,128)(2,1)S(1)} all-gather(bf16[1,6,2]{1,2,0:T(2,128)(2,1)S(1)} %bitcast.229), channel_id=1, replica_groups=mesh['dp'=4,'fsdp'=32] {'dp','fsdp'}, dimensions={0}, use_global_device_ids=true | all-gather | bytes 3096 | tf_op jit(solution)/shard_map/all_gather | solution.py:71
  206.1 29.4 %all-gather.5 = bf16[128,6,2]{1,2,0:T(2,128)(2,1)S(1)} all-gather(bf16[1,6,2]{1,2,0:T(2,128)(2,1)S(1)} %bitcast.230), channel_id=1, replica_groups=mesh['dp'=4,'fsdp'=32] {'dp','fsdp'}, dimensions={0}, use_global_device_ids=true | all-gather | bytes 3096 | tf_op jit(solution)/shard_map/all_gather | solution.py:72
  238.4 7.7 fusion.57
  246.0 7.2 fusion.37
  262.3 17.9 %fusion.13 = (bf16[512,4,768]{2,0,1:T(8,128)(2,1)}, f32[512,4,768]{2,0,1:T(8,128)}, f32[4,512,768]{2,1,0:T(8,128)}) fusion(f32[4,768]{1,0:T(4,128)} %reshape.264, bf16[512,4,192]{0,2,1:T(8,128)(2,1)S(1)} %bitcast.205, bf16[4,192,768]{2,1,0:T(8,128)(2,1)S(1)} %reshape.250), kind=kOutput, calls=%fused_computation.23 | convolution fusion | flops 707788800 | bytes 17707008 | tf_op jit(solution)/shard_map/tgi,gic->tgc/dot_general | solution.py:28
  280.3 4.7 fusion.60
  294.3 9.5 convert_reduce_fusion
  316.6 7.6 convert_reduce_fusion.4
  324.2 9.0 multiply_reduce_fusion
  333.3 6.9 multiply_convert_fusion
  347.2 4.2 fusion.64
  358.9 349.8 %fusion.51 = (f32[8,768]{1,0:T(8,128)S(1)}, f32[8,768]{1,0:T(8,128)S(1)}) fusion(f32[768,768]{1,0:T(8,128)} %fusion.63, f32[768,768]{1,0:T(8,128)} %bitcast.190), kind=kCustom, calls=%all-reduce-scatter.2 | all-reduce-scatter fusion | flops 1572865 | bytes 4767744
  722.4 15.6 %collective-permute-start.22 = (f32[8,768]{1,0:T(8,128)S(1)}, f32[8,768]{1,0:T(8,128)}, u32[]{:S(2)}, u32[]{:S(2)}) collective-permute-start(f32[8,768]{1,0:T(8,128)S(1)} %get-tuple-element.65), channel_id=1, source_target_pairs={{0,23},{1,24},{2,25},{3,26},{4,27},{5,28},{6,29},{7,30},{8,31},{9,... | collective-permute-start | bytes 73736
  766.3 4.0 collective-permute-start.11
  780.0 4.3 collective-permute-start.6
  788.6 4.5 collective-permute-start.3
  813.0 3.6 collective-permute-start.54
  823.6 62.7 %all-reduce.11 = (f32[2,768]{1,0:T(2,128)S(1)}, f32[2,768]{1,0:T(2,128)S(1)}, f32[3072]{0:T(1024)S(1)}, f32[2,768]{1,0:T(2,128)S(1)}, f32[2,768]{1,0:T(2,128)S(1)}) all-reduce(f32[2,768]{1,0:T(2,128)S(1)} %pad_maximum_fusion.1, f32[2,768]{1,0:T(2,128)S(1)} %pad_maximum_fusion.2, ...), channel_id=6, replica_groups=mesh['dp'=4,'fsdp'=32] {'dp','fsdp'}, use_global_device_ids=true, to_apply=%region_17.18.clone | all-reduce | flops 9216 | bytes 73728
  886.2 4.5 collective-permute-start.51
  893.9 4.0 collective-permute-start.49
  897.9 4.1 collective-permute-start.48
  902.0 4.7 collective-permute-start.47
  909.6 4.3 collective-permute-start.45
  916.9 4.7 collective-permute-start.43
  926.4 3.6 collective-permute-start.40
  932.0 3.7 collective-permute-start.38
  941.4 3.9 collective-permute-start.35
  953.6 10.8 %concatenate = f32[262,768]{1,0:T(8,128)S(1)} concatenate(f32[6,768]{1,0:T(8,128)S(1)} %collective-permute-done.31, f32[8,768]{1,0:T(8,128)S(1)} %collective-permute-done.30, f32[8,768]{1,0:T(8,128)S(1)} %collective-permute-done.29, f32[8,768]{1,0:T(8,128)S(1)} %collective-permute-done.28, f32[8,768]{1,0:T(8,128)S(1)} %collective-permute-done.27, f32[8,768]{1,0:T(8,128)S(1)} %copy-done.31, ...), dimensions={0} | concatenate | bytes 1609728
  (334 shorter events, 174.0 us)
Async XLA Ops:
  7.2 246.1 %all-gather.13.cloned.1.call-start = ((), (), s32[]{:S(2)}) async-start(), calls=%async_computation.2 | async-start | bytes 1585152 | tf_op jit(solution)/shard_map/all_gather | solution.py:65
  7.9 251.8 %all-gather.15.cloned.1.call-start = ((), (), s32[]{:S(2)}) async-start(), calls=%async_computation.3 | async-start | bytes 1585152 | tf_op jit(solution)/shard_map/all_gather | solution.py:66
  8.7 271.6 %all-gather.11.cloned.1.call-start = ((), (), s32[]{:S(2)}) async-start(), calls=%async_computation.1 | async-start | bytes 1585152 | tf_op jit(solution)/shard_map/all_gather | solution.py:67
  9.4 959.8 %all-reduce.15.cloned.1.call-start = ((), (), s32[]{:S(2)}) async-start(), calls=%async_computation.5 | async-start | bytes 3932160
  347.1 623.4 %reduce-scatter.12.cloned.1.call-start = ((), (), s32[]{:S(2)}) async-start(), calls=%async_computation.4 | async-start | bytes 3170304
  716.6 21.5 %collective-permute-start.26 = (f32[8,768]{1,0:T(8,128)S(1)}, f32[8,768]{1,0:T(8,128)S(1)}, u32[]{:S(2)}, u32[]{:S(2)}) collective-permute-start(f32[8,768]{1,0:T(8,128)S(1)} %get-tuple-element.65), channel_id=1, source_target_pairs={{0,27},{1,28},{2,29},{3,30},{4,31},{5,32},{6,33},{7,34},{8,35},{9,... | collective-permute-start | bytes 73736
  717.9 23.1 %collective-permute-start.25 = (f32[8,768]{1,0:T(8,128)S(1)}, f32[8,768]{1,0:T(8,128)S(1)}, u32[]{:S(2)}, u32[]{:S(2)}) collective-permute-start(f32[8,768]{1,0:T(8,128)S(1)} %get-tuple-element.65), channel_id=1, source_target_pairs={{0,26},{1,27},{2,28},{3,29},{4,30},{5,31},{6,32},{7,33},{8,34},{9,... | collective-permute-start | bytes 73736
  719.2 24.3 %collective-permute-start.24 = (f32[8,768]{1,0:T(8,128)S(1)}, f32[8,768]{1,0:T(8,128)S(1)}, u32[]{:S(2)}, u32[]{:S(2)}) collective-permute-start(f32[8,768]{1,0:T(8,128)S(1)} %get-tuple-element.65), channel_id=1, source_target_pairs={{0,25},{1,26},{2,27},{3,28},{4,29},{5,30},{6,31},{7,32},{8,33},{9,... | collective-permute-start | bytes 73736
  720.5 25.3 %collective-permute-start.23 = (f32[8,768]{1,0:T(8,128)S(1)}, f32[8,768]{1,0:T(8,128)}, u32[]{:S(2)}, u32[]{:S(2)}) collective-permute-start(f32[8,768]{1,0:T(8,128)S(1)} %get-tuple-element.65), channel_id=1, source_target_pairs={{0,24},{1,25},{2,26},{3,27},{4,28},{5,29},{6,30},{7,31},{8,32},{9,... | collective-permute-start | bytes 73736
  722.4 25.3 %collective-permute-start.22 = (f32[8,768]{1,0:T(8,128)S(1)}, f32[8,768]{1,0:T(8,128)}, u32[]{:S(2)}, u32[]{:S(2)}) collective-permute-start(f32[8,768]{1,0:T(8,128)S(1)} %get-tuple-element.65), channel_id=1, source_target_pairs={{0,23},{1,24},{2,25},{3,26},{4,27},{5,28},{6,29},{7,30},{8,31},{9,... | collective-permute-start | bytes 73736
  747.6 16.0 %collective-permute-start.17 = (f32[8,768]{1,0:T(8,128)S(1)}, f32[8,768]{1,0:T(8,128)}, u32[]{:S(2)}, u32[]{:S(2)}) collective-permute-start(f32[8,768]{1,0:T(8,128)S(1)} %get-tuple-element.65), channel_id=1, source_target_pairs={{0,18},{1,19},{2,20},{3,21},{4,22},{5,23},{6,24},{7,25},{8,26},{9,... | collective-permute-start | bytes 73736
  749.5 16.7 %collective-permute-start.16 = (f32[8,768]{1,0:T(8,128)S(1)}, f32[8,768]{1,0:T(8,128)}, u32[]{:S(2)}, u32[]{:S(2)}) collective-permute-start(f32[8,768]{1,0:T(8,128)S(1)} %get-tuple-element.65), channel_id=1, source_target_pairs={{0,17},{1,18},{2,19},{3,20},{4,21},{5,22},{6,23},{7,24},{8,25},{9,... | collective-permute-start | bytes 73736
  753.0 17.3 %collective-permute-start.15 = (f32[8,768]{1,0:T(8,128)S(1)}, f32[8,768]{1,0:T(8,128)}, u32[]{:S(2)}, u32[]{:S(2)}) collective-permute-start(f32[8,768]{1,0:T(8,128)S(1)} %get-tuple-element.65), channel_id=1, source_target_pairs={{0,16},{1,17},{2,18},{3,19},{4,20},{5,21},{6,22},{7,23},{8,24},{9,... | collective-permute-start | bytes 73736
  755.2 16.4 %collective-permute-start.14 = (f32[8,768]{1,0:T(8,128)S(1)}, f32[8,768]{1,0:T(8,128)}, u32[]{:S(2)}, u32[]{:S(2)}) collective-permute-start(f32[8,768]{1,0:T(8,128)S(1)} %get-tuple-element.65), channel_id=1, source_target_pairs={{0,15},{1,16},{2,17},{3,18},{4,19},{5,20},{6,21},{7,22},{8,23},{9,... | collective-permute-start | bytes 73736
  777.2 16.0 %collective-permute-start.7 = (f32[8,768]{1,0:T(8,128)S(1)}, f32[8,768]{1,0:T(8,128)S(1)}, u32[]{:S(2)}, u32[]{:S(2)}) collective-permute-start(f32[8,768]{1,0:T(8,128)S(1)} %get-tuple-element.65), channel_id=1, source_target_pairs={{0,8},{1,9},{2,10},{3,11},{4,12},{5,13},{6,14},{7,15},{8,16},{9,17... | collective-permute-start | bytes 73736
  810.2 76.0 %collective-permute-start.56 = (f32[8,768]{1,0:T(8,128)S(1)}, f32[8,768]{1,0:T(8,128)S(1)}, u32[]{:S(2)}, u32[]{:S(2)}) collective-permute-start(f32[8,768]{1,0:T(8,128)S(1)} %get-tuple-element.66), channel_id=1, source_target_pairs={{0,25},{1,26},{2,27},{3,28},{4,29},{5,30},{6,31},{7,32},{8,33},{9,... | collective-permute-start | bytes 73736
  811.5 79.2 %collective-permute-start.55 = (f32[8,768]{1,0:T(8,128)S(1)}, f32[8,768]{1,0:T(8,128)S(1)}, u32[]{:S(2)}, u32[]{:S(2)}) collective-permute-start(f32[8,768]{1,0:T(8,128)S(1)} %get-tuple-element.66), channel_id=1, source_target_pairs={{0,24},{1,25},{2,26},{3,27},{4,28},{5,29},{6,30},{7,31},{8,32},{9,... | collective-permute-start | bytes 73736
  813.0 81.0 %collective-permute-start.54 = (f32[8,768]{1,0:T(8,128)S(1)}, f32[8,768]{1,0:T(8,128)S(1)}, u32[]{:S(2)}, u32[]{:S(2)}) collective-permute-start(f32[8,768]{1,0:T(8,128)S(1)} %get-tuple-element.66), channel_id=1, source_target_pairs={{0,23},{1,24},{2,25},{3,26},{4,27},{5,28},{6,29},{7,30},{8,31},{9,... | collective-permute-start | bytes 73736
  816.6 81.3 %collective-permute-start.53 = (f32[8,768]{1,0:T(8,128)S(1)}, f32[8,768]{1,0:T(8,128)S(1)}, u32[]{:S(2)}, u32[]{:S(2)}) collective-permute-start(f32[8,768]{1,0:T(8,128)S(1)} %get-tuple-element.66), channel_id=1, source_target_pairs={{0,22},{1,23},{2,24},{3,25},{4,26},{5,27},{6,28},{7,29},{8,30},{9,... | collective-permute-start | bytes 73736
  819.7 82.3 %collective-permute-start.52 = (f32[8,768]{1,0:T(8,128)S(1)}, f32[8,768]{1,0:T(8,128)S(1)}, u32[]{:S(2)}, u32[]{:S(2)}) collective-permute-start(f32[8,768]{1,0:T(8,128)S(1)} %get-tuple-element.66), channel_id=1, source_target_pairs={{0,21},{1,22},{2,23},{3,24},{4,25},{5,26},{6,27},{7,28},{8,29},{9,... | collective-permute-start | bytes 73736
  886.2 21.1 %collective-permute-start.51 = (f32[8,768]{1,0:T(8,128)S(1)}, f32[8,768]{1,0:T(8,128)S(1)}, u32[]{:S(2)}, u32[]{:S(2)}) collective-permute-start(f32[8,768]{1,0:T(8,128)S(1)} %get-tuple-element.66), channel_id=1, source_target_pairs={{0,20},{1,21},{2,22},{3,23},{4,24},{5,25},{6,26},{7,27},{8,28},{9,... | collective-permute-start | bytes 73736
  890.7 18.9 %collective-permute-start.50 = (f32[8,768]{1,0:T(8,128)S(1)}, f32[8,768]{1,0:T(8,128)S(1)}, u32[]{:S(2)}, u32[]{:S(2)}) collective-permute-start(f32[8,768]{1,0:T(8,128)S(1)} %get-tuple-element.66), channel_id=1, source_target_pairs={{0,19},{1,20},{2,21},{3,22},{4,23},{5,24},{6,25},{7,26},{8,27},{9,... | collective-permute-start | bytes 73736
  893.9 19.9 %collective-permute-start.49 = (f32[8,768]{1,0:T(8,128)S(1)}, f32[8,768]{1,0:T(8,128)S(1)}, u32[]{:S(2)}, u32[]{:S(2)}) collective-permute-start(f32[8,768]{1,0:T(8,128)S(1)} %get-tuple-element.66), channel_id=1, source_target_pairs={{0,18},{1,19},{2,20},{3,21},{4,22},{5,23},{6,24},{7,25},{8,26},{9,... | collective-permute-start | bytes 73736
  897.9 19.0 %collective-permute-start.48 = (f32[8,768]{1,0:T(8,128)S(1)}, f32[8,768]{1,0:T(8,128)S(1)}, u32[]{:S(2)}, u32[]{:S(2)}) collective-permute-start(f32[8,768]{1,0:T(8,128)S(1)} %get-tuple-element.66), channel_id=1, source_target_pairs={{0,17},{1,18},{2,19},{3,20},{4,21},{5,22},{6,23},{7,24},{8,25},{9,... | collective-permute-start | bytes 73736
  902.0 19.6 %collective-permute-start.47 = (f32[8,768]{1,0:T(8,128)S(1)}, f32[8,768]{1,0:T(8,128)S(1)}, u32[]{:S(2)}, u32[]{:S(2)}) collective-permute-start(f32[8,768]{1,0:T(8,128)S(1)} %get-tuple-element.66), channel_id=1, source_target_pairs={{0,16},{1,17},{2,18},{3,19},{4,20},{5,21},{6,22},{7,23},{8,24},{9,... | collective-permute-start | bytes 73736
  907.3 16.9 %collective-permute-start.46 = (f32[8,768]{1,0:T(8,128)S(1)}, f32[8,768]{1,0:T(8,128)S(1)}, u32[]{:S(2)}, u32[]{:S(2)}) collective-permute-start(f32[8,768]{1,0:T(8,128)S(1)} %get-tuple-element.66), channel_id=1, source_target_pairs={{0,15},{1,16},{2,17},{3,18},{4,19},{5,20},{6,21},{7,22},{8,23},{9,... | collective-permute-start | bytes 73736
  909.6 16.7 %collective-permute-start.45 = (f32[8,768]{1,0:T(8,128)S(1)}, f32[8,768]{1,0:T(8,128)S(1)}, u32[]{:S(2)}, u32[]{:S(2)}) collective-permute-start(f32[8,768]{1,0:T(8,128)S(1)} %get-tuple-element.66), channel_id=1, source_target_pairs={{0,14},{1,15},{2,16},{3,17},{4,18},{5,19},{6,20},{7,21},{8,22},{9,... | collective-permute-start | bytes 73736
  913.9 16.1 %collective-permute-start.44 = (f32[8,768]{1,0:T(8,128)S(1)}, f32[8,768]{1,0:T(8,128)S(1)}, u32[]{:S(2)}, u32[]{:S(2)}) collective-permute-start(f32[8,768]{1,0:T(8,128)S(1)} %get-tuple-element.66), channel_id=1, source_target_pairs={{0,13},{1,14},{2,15},{3,16},{4,17},{5,18},{6,19},{7,20},{8,21},{9,... | collective-permute-start | bytes 73736
  938.9 25.5 %collective-permute-start.36 = (f32[8,768]{1,0:T(8,128)S(1)}, f32[8,768]{1,0:T(8,128)S(1)}, u32[]{:S(2)}, u32[]{:S(2)}) collective-permute-start(f32[8,768]{1,0:T(8,128)S(1)} %get-tuple-element.66), channel_id=1, source_target_pairs={{0,5},{1,6},{2,7},{3,8},{4,9},{5,10},{6,11},{7,12},{8,13},{9,14},{... | collective-permute-start | bytes 73736
  941.4 23.1 %collective-permute-start.35 = (f32[8,768]{1,0:T(8,128)S(1)}, f32[8,768]{1,0:T(8,128)S(1)}, u32[]{:S(2)}, u32[]{:S(2)}) collective-permute-start(f32[8,768]{1,0:T(8,128)S(1)} %get-tuple-element.66), channel_id=1, source_target_pairs={{0,4},{1,5},{2,6},{3,7},{4,8},{5,9},{6,10},{7,11},{8,12},{9,13},{1... | collective-permute-start | bytes 73736
  945.3 19.2 %collective-permute-start.34 = (f32[8,768]{1,0:T(8,128)S(1)}, f32[8,768]{1,0:T(8,128)S(1)}, u32[]{:S(2)}, u32[]{:S(2)}) collective-permute-start(f32[8,768]{1,0:T(8,128)S(1)} %get-tuple-element.66), channel_id=1, source_target_pairs={{0,3},{1,4},{2,5},{3,6},{4,7},{5,8},{6,9},{7,10},{8,11},{9,12},{10... | collective-permute-start | bytes 73736
  946.6 17.9 %collective-permute-start.33 = (f32[8,768]{1,0:T(8,128)S(1)}, f32[8,768]{1,0:T(8,128)S(1)}, u32[]{:S(2)}, u32[]{:S(2)}) collective-permute-start(f32[8,768]{1,0:T(8,128)S(1)} %get-tuple-element.66), channel_id=1, source_target_pairs={{0,2},{1,3},{2,4},{3,5},{4,6},{5,7},{6,8},{7,9},{8,10},{9,11},{10,... | collective-permute-start | bytes 73736
  (95 other events, 2794.9 us)
Sparse Core Ops, SparseCore 0:
  10.8 66.6 all-gather.12
  80.3 61.5 all-gather.14
  144.8 61.5 all-gather.10
  347.2 148.1 all-reduce.14
  500.6 208.2 reduce-scatter.11
where the time goes:
time: 990 us; the launch traced here: 977 us
  blocking collectives  633 us (64%)
  starting transfers between devices  171 us (17%)
  matrix products  88 us (9%)
  local copies, waits for them, and re-layouts  49.1 us (5%)
  other arithmetic  18.4 us (2%)
  between operations  15.7 us (2%)
    unnamed x3, blocking collectives  477 us
    unnamed x66, starting transfers between devices  171 us
    all_gather x1, blocking collectives, local(): lax.all_gather(qkv_weight, ('dp', 'fsdp'), axis=0, tiled=True)  38.6 us
    all_gather x1, blocking collectives, local(): lax.all_gather(norm_gain, ('dp', 'fsdp'), axis=1, tiled=True)  30.1 us
    unnamed x132, local copies, waits for them, and re-layouts  29.4 us
    all_gather x1, blocking collectives, local(): lax.all_gather(norm_shift, ('dp', 'fsdp'), axis=1, tiled=True)  29.4 us
    all_gather x1, blocking collectives, local(): lax.all_gather(out_bias, ('dp', 'fsdp'), axis=1, tiled=True)  29.1 us
    all_gather x1, blocking collectives, local(): lax.all_gather(qv_bias, ('dp', 'fsdp'), axis=1, tiled=True)  28.3 us
  transfers between devices with their start and end apart: 69, of which 0 were waited for; matrix products, arithmetic and copies ran while one was open for 45% of the time, Pallas kernels for 0%

commit v1 on v0

v1 whole, which is shorter than its diff:
```python
import jax
import jax.numpy as jnp
import numpy as np
from jax import lax
from jax.experimental import pallas as pl
from jax.experimental.pallas import tpu as pltpu
from jax.sharding import PartitionSpec as P

AXES = ("dp", "fsdp")
D = 768
F = 3072
G = 4
DG = 192
QKV = 3 * DG
HEADS = 12
HEAD = 64
TOK = 512
LONG = 384
CHIPS = 64
ROWS = 24
EPS = 1e-05
BAND = 64
BANDS = D // BAND
BF = jnp.bfloat16
F32 = jnp.float32
MIB = 1 << 20

SIDE = 18
CUT = 576
UP_AT = 64
OUT_AT = 320


def orders():
    weights, downs, hidden = (np.zeros((2, 192, 192), np.float32) for _ in range(3))
    for core in range(2):
        for device in range(8):
            chip, half = device // 2, device % 2
            base = (half != core) * 96 + chip * ROWS
            for row in range(6):
                for kind in range(4):
                    weights[core, kind * 48 + device * 6 + row, base + kind * 6 + row] = 1
            for row in range(ROWS):
                downs[core, device * ROWS + row, base + row] = 1
                hidden[core, device * ROWS + row, base + SIDE + row // 4] = 1
    return np.concatenate([weights, downs, hidden], axis=1)


def dot(left, right, over_left, over_right):
    return lax.dot_general(
        left, right, (((over_left,), (over_right,)), ((), ())), preferred_element_type=F32
    )


def iota(shape, axis):
    return lax.broadcasted_iota(jnp.int32, shape, axis)


def pack_kernel(qkv, out, up, down, qv, outb, upb, gain, shift, packed, tile, square):
    tile[...] = jnp.zeros_like(tile)
    tile[0:6, 0:CUT] = qkv[...].astype(F32)
    tile[6:12, 0:CUT] = out[:, 0:CUT].astype(F32)
    tile[12:18, 0:CUT] = up[:, 0:CUT].astype(F32)
    square[...] = jnp.zeros_like(square)
    for place, rows in enumerate((qv, outb, gain, shift)):
        square[2 * place : 2 * place + 2, 0:6] = rows[...].astype(F32)
    columns = square[...].T
    spread = jnp.where(iota((8, ROWS), 1) // 4 == iota((8, ROWS), 0), upb[...].astype(F32), 0.0)
    lanes = (iota((ROWS, 128), 1) - 8 == iota((ROWS, 128), 0) % 4).astype(F32)
    hidden = jnp.dot(spread, lanes, preferred_element_type=F32)
    tile[SIDE:ROWS, 0:128] = (columns[0:8] + hidden)[0:6]
    tile[SIDE:ROWS, UP_AT : UP_AT + DG] = up[:, CUT:D].astype(F32)
    tile[SIDE:ROWS, OUT_AT : OUT_AT + DG] = out[:, CUT:D].astype(F32)
    tile[:, CUT:D] = down[...].astype(F32)
    whole = tile[...].astype(BF)
    twice = jnp.concatenate([whole, whole], axis=0)
    for pair in range(CHIPS // 2):
        packed[2 * ROWS * pair : 2 * ROWS * (pair + 1), :] = twice


def each(count, step):
    def body(i, nothing):
        step(i)
        return nothing

    lax.fori_loop(0, count, body, 0)


def part(i, size):
    return pl.ds(pl.multiple_of(i * size, size), size)


def halves(chunk):
    return jnp.sum(chunk.reshape(BAND // 8, 8, TOK), axis=0)


def means(count, bands):
    def body(i, sums):
        return tuple(kept + halves(chunk) for kept, chunk in zip(sums, bands(part(i, BAND)), strict=True))

    sums = lax.fori_loop(0, BANDS, body, (jnp.zeros((8, TOK), F32),) * count)
    return [jnp.sum(total, axis=0, keepdims=True) * (1.0 / D) for total in sums]


def lane_sum(chunk):
    return jnp.sum(chunk, axis=1, keepdims=True)


def main_kernel(
    tokens, segments, cotangent, mine, other, order,
    output, grad_tokens, keep, send,
    w_qkv, w_out, w_up, w_down, side, up_bias,
    turn, x_t, c_t, q_t, k_t, v_t, ctx_t, low_t, probs, probs_small,
    first_low, hat, active, slope, second, branch_pad, packed_t,
    g_qkv, g_out, g_up, g_down, g_side,
):
    core = lax.rem(lax.axis_index("fsdp"), 2)
    lane48 = iota((48, 128), 1)

    def place_block(i):
        rows = part(i, 96)
        both = jnp.concatenate([mine[rows, :], other[rows, :]], axis=0)
        placed = jnp.dot(order[core, 0:192, :], both[:, 0:640], preferred_element_type=F32).astype(BF)
        down_rows = jnp.dot(order[core, 192:384, :], both[:, 512:768], preferred_element_type=F32)
        units = part(i, 192)
        w_down[units, :] = down_rows.astype(BF)
        hidden = jnp.dot(order[core, 384:576, :], both[:, 0:128], preferred_element_type=F32)
        pick = iota((192, 128), 1) - 8 == iota((192, 128), 0) % 4
        up_bias[units, :] = lane_sum(jnp.where(pick, hidden, 0.0))
        here = part(i, 48)
        last = placed[144:192]
        w_qkv[here, :] = placed[0:48, 0:CUT]
        w_out[here, 0:512] = placed[48:96, 0:512]
        w_out[here, 512:640] = jnp.where(lane48 < 64, placed[48:96, 512:640], last[:, 256:384])
        w_out[here, 640:768] = last[:, 384:512]
        w_up[here, 0:512] = placed[96:144, 0:512]
        w_up[here, 512:640] = jnp.where(lane48 < 64, placed[96:144, 512:640], last[:, 0:128])
        w_up[here, 640:768] = last[:, 128:256]
        side[here, :] = last[:, 0:128].astype(F32)

    each(16, place_block)

    ids = segments[...]
    count0 = jnp.sum((ids == 0).astype(jnp.int32))
    count1 = jnp.sum((ids == 1).astype(jnp.int32))
    count2 = TOK - count0 - count1
    start = jnp.where(count0 == LONG, 0, jnp.where(count1 == LONG, count0, count0 + count1))
    border = jnp.where(count0 == LONG, count1, jnp.where(count1 == LONG, count2, count0))

    def turn_rows(i):
        place = iota((64, TOK), 1) + start
        place = jnp.where(place >= TOK, place - TOK, place)
        turn[part(i, 64), :] = jnp.where(iota((64, TOK), 0) + i * 64 == place, 1.0, 0.0).astype(BF)

    each(8, turn_rows)

    def turn_features(i):
        x_t[part(i, 256), :] = dot(tokens[:, part(i, 256)], turn[...], 0, 0).astype(BF)
        c_t[part(i, 256), :] = dot(cotangent[:, part(i, 256)], turn[...], 0, 0).astype(BF)

    each(3, turn_features)

    together = (iota((128, 128), 0) < border) == (iota((128, 128), 1) < border)
    spans = ((slice(0, LONG), probs), (slice(LONG, TOK), probs_small))

    def attend(g):
        rows = part(g, DG)
        packed = dot(w_qkv[rows, :], x_t[rows, :], 0, 0)
        q_t[rows, :] = ((packed[0:DG] + side[rows, 0:1]).astype(BF).astype(F32) * 0.125).astype(BF)
        k_t[rows, :] = packed[DG : 2 * DG].astype(BF)
        v_t[rows, :] = (packed[2 * DG :] + side[rows, 1:2]).astype(BF)
        for third in range(3):
            head = g * 3 + third
            rows = part(head, HEAD)
            for cols, kept in spans:
                scores = dot(k_t[rows, cols], q_t[rows, cols], 0, 0)
                if kept is probs_small:
                    scores = jnp.where(together, scores, -1000000000.0)
                power = jnp.exp(scores - jnp.max(scores, axis=0, keepdims=True))
                share = power * (1.0 / jnp.sum(power, axis=0, keepdims=True))
                kept[head] = share
                ctx_t[rows, cols] = dot(v_t[rows, cols], share.astype(BF), 1, 0).astype(BF)

    each(G, attend)

    def project(i):
        rows = part(i, 128)
        attended = dot(w_out[:, rows], ctx_t[...], 0, 0) + side[rows, 2:3]
        second[rows, :] = x_t[rows, :].astype(F32) + attended

    each(6, project)
    (mean_one,) = means(1, lambda rows: (second[rows, :],))
    (spread_one,) = means(1, lambda rows: ((second[rows, :] - mean_one) ** 2,))
    rs_one = lax.rsqrt(spread_one + EPS)

    def norm_one(i):
        rows = part(i, BAND)
        hats = (second[rows, :] - mean_one) * rs_one
        hat[rows, :] = hats
        result = hats * side[rows, 4:5] + side[rows, 6:7]
        second[rows, :] = result
        first_low[rows, :] = result.astype(BF)

    each(BANDS, norm_one)

    def feed(g):
        rows = part(g, DG)
        for third in range(3):
            units = part(g * 3 + third, 256)
            upper = dot(w_up[rows, 256 * third : 256 * third + 256], first_low[rows, :], 0, 0) + up_bias[units, :]
            below = 0.5 + 0.5 * lax.erf(upper * 0.7071067811865476)
            density = jnp.exp(-0.5 * upper * upper) * 0.3989422804014327
            active[units, :] = (upper * below).astype(BF)
            slope[units, :] = below + upper * density
        units = part(g, D)
        branch = dot(w_down[units, :], active[units, :], 0, 0)[64:256]
        second[rows, :] += branch + side[rows, 3:4]

    each(G, feed)

    (mean_two,) = means(1, lambda rows: (second[rows, :],))
    (spread_two,) = means(1, lambda rows: ((second[rows, :] - mean_two) ** 2,))
    rs_two = lax.rsqrt(spread_two + EPS)

    def norm_two(rows):
        hats = (second[rows, :] - mean_two) * rs_two
        second[rows, :] = hats
        low_t[rows, :] = (hats * side[rows, 5:6] + side[rows, 7:8]).astype(BF)
        slopes = c_t[rows, :].astype(F32)
        g_side[rows, 5:6] = lane_sum(slopes * hats)
        g_side[rows, 7:8] = lane_sum(slopes)
        slopes = slopes * side[rows, 5:6]
        return slopes, slopes * hats

    lean, tilt = means(2, norm_two)

    def write_output(i):
        output[:, part(i, 256)] = dot(turn[...], low_t[part(i, 256), :], 1, 1).astype(BF)

    each(3, write_output)

    def norm_two_back(i):
        rows = part(i, BAND)
        slopes = c_t[rows, :].astype(F32) * side[rows, 5:6]
        back = rs_two * (slopes - lean - second[rows, :] * tilt)
        second[rows, :] = back
        low = back.astype(BF)
        g_side[rows, 3:4] = lane_sum(low.astype(F32))
        low_t[rows, :] = low

    each(BANDS, norm_two_back)
    for g in range(G):
        branch_pad[g, 0:64, :] = jnp.zeros((64, TOK), BF)
        branch_pad[g, 64:256, :] = low_t[DG * g : DG * (g + 1), :]

    def feed_back(g):
        rows = part(g, DG)
        for third in range(3):
            units = part(g * 3 + third, 256)
            span = slice(256 * third, 256 * third + 256)
            d_active = dot(w_down[units, :], branch_pad[g], 1, 0)
            d_upper = (d_active * slope[units, :]).astype(BF)
            up_bias[units, :] = lane_sum(d_upper.astype(F32))
            g_down[units, :] = dot(active[units, :], branch_pad[g], 1, 1).astype(BF)
            g_up[rows, span] = dot(first_low[rows, :], d_upper, 1, 1).astype(BF)
            active[units, :] = d_upper
        second[rows, :] += dot(w_up[rows, :], active[part(g, D), :], 1, 0)

    each(G, feed_back)

    def norm_one_sums(rows):
        slopes, hats = second[rows, :], hat[rows, :]
        g_side[rows, 4:5] = lane_sum(slopes * hats)
        g_side[rows, 6:7] = lane_sum(slopes)
        slopes = slopes * side[rows, 4:5]
        return slopes, slopes * hats

    lean_one, tilt_one = means(2, norm_one_sums)

    def norm_one_back(i):
        rows = part(i, BAND)
        back = rs_one * (second[rows, :] * side[rows, 4:5] - lean_one - hat[rows, :] * tilt_one)
        second[rows, :] = back
        low = back.astype(BF)
        g_side[rows, 2:3] = lane_sum(low.astype(F32))
        low_t[rows, :] = low

    each(BANDS, norm_one_back)

    def project_back(i):
        rows = part(i, 128)
        g_out[rows, :] = dot(ctx_t[rows, :], low_t[...], 1, 1).astype(BF)
        c_t[rows, :] = dot(w_out[rows, :], low_t[...], 1, 0).astype(BF)

    each(6, project_back)

    def attend_back(g):
        for third in range(3):
            head = g * 3 + third
            rows = part(head, HEAD)
            at = HEAD * third
            for cols, kept in spans:
                d_out = c_t[rows, cols]
                share = kept[head]
                d_share = dot(v_t[rows, cols], d_out, 0, 0)
                packed_t[2 * DG + at : 2 * DG + at + HEAD, cols] = dot(d_out, share.astype(BF), 1, 1).astype(BF)
                d_scores = share * (d_share - jnp.sum(d_share * share, axis=0, keepdims=True))
                d_scores = d_scores.astype(BF)
                packed_t[at : at + HEAD, cols] = (0.125 * dot(k_t[rows, cols], d_scores, 1, 0)).astype(BF)
                packed_t[DG + at : DG + at + HEAD, cols] = dot(q_t[rows, cols], d_scores, 1, 1).astype(BF)
        rows = part(g, DG)
        g_qkv[rows, :] = dot(x_t[rows, :], packed_t[...], 1, 1).astype(BF)
        total = second[rows, :] + dot(w_qkv[rows, :], packed_t[...], 1, 0)
        g_side[rows, 0:1] = lane_sum(packed_t[0:DG, :].astype(F32))
        g_side[rows, 1:2] = lane_sum(packed_t[2 * DG :, :].astype(F32))
        high = total.astype(BF)
        low_t[rows, :] = high
        first_low[rows, :] = (total - high.astype(F32)).astype(BF)

    each(G, attend_back)

    def write_grad(i):
        rows = part(i, 256)
        grad_tokens[:, rows] = dot(turn[...], low_t[rows, :], 1, 1) + dot(turn[...], first_low[rows, :], 1, 1)

    each(3, write_grad)

    def tile_block(i):
        here = part(i, 48)
        units = part(i, 192)
        pick = iota((192, 128), 1) - 8 == iota((192, 128), 0) % 4
        hidden = jnp.where(pick, up_bias[units, :], 0.0).astype(BF)
        bias = jnp.where(lane48 < 8, g_side[here, :], 0.0).astype(BF)
        zero = jnp.zeros((48, 128), BF)
        out_cut, up_cut = g_out[here, 512:640], g_up[here, 512:640]
        last = jnp.concatenate(
            [
                jnp.where(lane48 < 64, bias, up_cut),
                g_up[here, 640:768],
                jnp.where(lane48 < 64, zero, out_cut),
                g_out[here, 640:768],
                zero,
            ],
            axis=1,
        )
        stacked = jnp.concatenate(
            [
                jnp.concatenate([g_qkv[here, :], zero[:, 0:64]], axis=1),
                jnp.concatenate([g_out[here, 0:512], jnp.where(lane48 < 64, out_cut, zero)], axis=1),
                jnp.concatenate([g_up[here, 0:512], jnp.where(lane48 < 64, up_cut, zero)], axis=1),
                last,
            ],
            axis=0,
        )
        placed = dot(order[core, 0:192, :], stacked, 0, 0)
        downs = dot(order[core, 192:384, :], g_down[units, :], 0, 0)
        biases = dot(order[core, 384:576, :], hidden, 0, 0)
        rows = part(i, 96)
        for target, begin in ((keep, 0), (send, 96)):
            span = slice(begin, begin + 96)
            target[rows, 0:128] = (placed[span, 0:128] + biases[span]).astype(BF)
            target[rows, 128:512] = placed[span, 128:512].astype(BF)
            target[rows, 512:640] = (placed[span, 512:640] + downs[span, 0:128]).astype(BF)
            target[rows, 640:768] = downs[span, 128:256].astype(BF)

    each(16, tile_block)


def add_kernel(left, right, total):
    total[...] = (left[...].astype(F32) + right[...].astype(F32)).astype(BF)


def sum_kernel(parts, qkv, out, up, down, qv, outb, upb, gain, shift, square):
    total = jnp.zeros((2 * ROWS, D), F32)
    for pair in range(CHIPS // 2):
        total += parts[2 * ROWS * pair : 2 * ROWS * (pair + 1), :].astype(F32)
    total = total[0:ROWS] + total[ROWS:]
    qkv[...] = total[0:6, 0:CUT]
    out[:, 0:CUT] = total[6:12, 0:CUT]
    out[:, CUT:D] = total[SIDE:ROWS, OUT_AT : OUT_AT + DG]
    up[:, 0:CUT] = total[12:18, 0:CUT]
    up[:, CUT:D] = total[SIDE:ROWS, UP_AT : UP_AT + DG]
    down[...] = total[:, CUT:D]
    square[...] = jnp.zeros_like(square)
    square[0:6, :] = total[SIDE:ROWS, 0:128]
    columns = square[...].T
    for place, rows in enumerate((qv, outb, gain, shift)):
        rows[...] = columns[2 * place : 2 * place + 2, 0:6]
    lanes = (iota((128, ROWS), 0) - 8 == iota((128, ROWS), 1) % 4).astype(F32)
    spread = jnp.dot(square[0:8, :], lanes, preferred_element_type=F32, precision=lax.Precision.HIGHEST)
    spread = jnp.where(iota((8, ROWS), 1) // 4 == iota((8, ROWS), 0), spread, 0.0)
    upb[...] = jnp.sum(spread, axis=0, keepdims=True)


def call(kernel, shapes, scratch, limit, name):
    return pl.pallas_call(
        kernel,
        out_shape=[jax.ShapeDtypeStruct(*shape) for shape in shapes],
        scratch_shapes=[pltpu.VMEM(*shape) for shape in scratch],
        compiler_params=pltpu.CompilerParams(vmem_limit_bytes=limit * MIB),
        name=name,
    )


def same_core(n_dp, n_fsdp):
    return [[y * n_fsdp + i for y in range(n_dp) for i in range(core, n_fsdp, 2)] for core in range(2)]


def swap(array):
    return lax.ppermute(array, "fsdp", [(i, i ^ 1) for i in range(32)])


def local(
    tokens, segment_ids, qkv_weight, out_weight, up_weight, down_weight,
    qv_bias, out_bias, up_bias, norm_gain, norm_shift, cotangent,
):
    groups = same_core(4, 32)
    wide = (CHIPS * ROWS, D)
    packed = call(
        pack_kernel, [(wide, BF)], [((ROWS, D), F32), ((128, 128), F32)], 32, "pack"
    )(qkv_weight, out_weight, up_weight, down_weight, qv_bias, out_bias, up_bias.reshape(1, ROWS),
      norm_gain, norm_shift)[0]
    mine = lax.all_to_all(packed, AXES, 0, 0, axis_index_groups=groups, tiled=True)
    other = swap(mine)
    order = jnp.asarray(orders(), BF)
    square = (D, TOK)
    output, grad_tokens, keep, send = call(
        main_kernel,
        [((TOK, D), BF), ((TOK, D), F32), (wide, BF), (wide, BF)],
        [
            ((D, QKV), BF), ((D, D), BF), ((D, D), BF), ((F, 256), BF), ((D, 128), F32), ((F, 1), F32),
            ((TOK, TOK), BF), (square, BF), (square, BF), (square, BF), (square, BF), (square, BF), (square, BF),
            (square, BF), ((HEADS, LONG, LONG), F32), ((HEADS, 128, 128), F32),
            (square, BF), (square, F32), ((F, TOK), BF), ((F, TOK), F32), (square, F32),
            ((G, 256, TOK), BF), ((QKV, TOK), BF),
            ((D, QKV), BF), ((D, D), BF), ((D, D), BF), ((F, 256), BF), ((D, 128), F32),
        ],
        64,
        "layer",
    )(tokens, segment_ids, cotangent, mine, other, order)
    chip = call(add_kernel, [(wide, BF)], [], 32, "chip_sum")(keep, swap(send))[0]
    parts = lax.all_to_all(chip, AXES, 0, 0, axis_index_groups=groups, tiled=True)
    qkv, out, up, down, qv, outb, upb, gain, shift = call(
        sum_kernel,
        [((6, QKV), F32), ((6, D), F32), ((6, D), F32), ((ROWS, DG), F32), ((2, 6), F32), ((2, 6), F32),
         ((1, ROWS), F32), ((2, 6), F32), ((2, 6), F32)],
        [((128, 128), F32)],
        32,
        "slice_sum",
    )(parts)
    return output, grad_tokens, qkv, out, up, down, qv, outb, upb.reshape(ROWS), gain, shift


def solution(mesh):
    rows, columns, flat = P(AXES, None), P(None, AXES), P(AXES)
    in_specs = (rows, rows, rows, rows, rows, rows, columns, columns, flat, columns, columns, rows)
    out_specs = (rows, rows, rows, rows, rows, rows, columns, columns, flat, columns, columns)
    return jax.shard_map(local, mesh=mesh, in_specs=in_specs, out_specs=out_specs, check_vma=False)
```

time: 990 us -> 167 us (0.17); the launches traced: 977 us -> 167 us
  blocking collectives: 633 us -> 82.5 us
  starting transfers between devices: 171 us -> 0.14 us
  matrix products: 88 us -> 0 us
  Pallas kernels: 0 us -> 64.9 us
  local copies, waits for them, and re-layouts: 49.1 us -> 9.18 us
  other arithmetic: 18.4 us -> 0 us
  between operations: 15.7 us -> 0.68 us
    unnamed x3 -> x0, blocking collectives: 477 us -> none
    unnamed x66 -> x0, starting transfers between devices: 171 us -> none
    all_gather x5 -> x0, blocking collectives: 155 us -> none  [the longest x1 38.6 us: local(): lax.all_gather(qkv_weight, ('dp', 'fsdp'), axis=0, tiled=True)]
    all_to_all x0 -> x2, blocking collectives: none -> 82.5 us  [the longest x1 44.3 us: local(): lax.all_to_all(packed, AXES, 0, 0, axis_index_groups=groups, tiled=True)]
    dot_general x16 -> x0, matrix products: 77.4 us -> none  [the longest x3 23.4 us: grouped_dot(): jnp.einsum('tgi,gic->tgc', grouped_in, block_weights, preferred_element_t...]
    pallas_call x0 -> x4, Pallas kernels: none -> 64.9 us  [the longest x1 63.2 us: local(): call(main_kernel, [((TOK, D), BF), ((TOK, D), F32), (wide, BF), (wide, BF...]
    unnamed x132 -> x22, local copies, waits for them, and re-layouts: 29.4 us -> 9.18 us
    reshape x9 -> x0, local copies, waits for them, and re-layouts: 10.1 us -> none  [the longest x2 5.01 us: grouped_back(): input_grad.reshape(row_count, -1)]
  transfers between devices with their start and end apart: 69 -> 2, of which waited for: 0 -> 2; matrix products, arithmetic and copies ran while one was open for 45% -> 0% of each run, Pallas kernels for 0% -> 0%
where the time goes in v1:
time: 167 us
  blocking collectives  82.5 us (49%)
  Pallas kernels  64.9 us (39%)
  waiting for transfers between devices  9.27 us (6%)
  local copies, waits for them, and re-layouts  9.18 us (5%)
    pallas_call x1, Pallas kernels, local(): call(main_kernel, [((TOK, D), BF), ((TOK, D), F32), (wide, BF), (wide, BF...  63.2 us
    all_to_all x1, blocking collectives, local(): lax.all_to_all(packed, AXES, 0, 0, axis_index_groups=groups, tiled=True)  44.3 us
    all_to_all x1, blocking collectives, local(): lax.all_to_all(chip, AXES, 0, 0, axis_index_groups=groups, tiled=True)  38.2 us
    ppermute x2, waiting for transfers between devices, swap(): return lax.ppermute(array, 'fsdp', [(i, i ^ 1) for i in range(32)])  9.27 us
    unnamed x22, local copies, waits for them, and re-layouts  9.18 us
  transfers between devices with their start and end apart: 2, of which 2 were waited for; matrix products, arithmetic and copies ran while one was open for 0% of the time, Pallas kernels for 0%

profile of v1, /device:TPU:0, one launch (start us, length us, event | category | flops | bytes accessed | tf_op | source)
XLA Modules:
  0.0 166.7 jit_solution(14756160629412678911)
XLA Ops:
  0.6 0.0 copy-start.1
  0.7 0.7 copy-done.1
  1.4 0.0 copy-start.2
  1.4 0.7 copy-done.2
  2.1 0.0 copy-start.3
  2.1 0.7 copy-done.3
  2.8 0.0 copy-start.4
  2.8 0.7 copy-done.4
  3.5 0.0 copy-start.5
  3.5 0.7 copy-done.5
  4.1 0.0 copy-start.6
  4.1 0.7 copy-done.6
  4.8 0.0 copy-start.7
  4.8 0.7 copy-done.7
  5.4 0.0 copy-start.8
  5.4 0.7 copy-done.8
  6.1 0.0 copy-start.9
  6.1 0.7 copy-done.9
  6.8 0.2 pack.1
  7.0 44.3 %all_to_all.22 = bf16[64,24,768]{2,1,0:T(8,128)(2,1)S(1)} all-to-all(bf16[64,24,768]{2,1,0:T(8,128)(2,1)S(1)} %bitcast.8), channel_id=1, replica_groups={{0,2,4,6,8,10,12,14,16,18,20,22,24,26,28,30,32,34,36,38,40,42,44,46,48,..., dimensions={0} | all-to-all | bytes 4718592 | tf_op jit(solution)/shard_map/all_to_all | solution.py:423
  51.3 0.0 copy-start.10
  51.3 1.4 copy-done.10
  52.7 0.0 collective-permute-start
  52.7 4.7 %collective-permute-done.other = bf16[1536,768]{1,0:T(8,128)(2,1)} collective-permute-done((bf16[1536,768]{1,0:T(8,128)(2,1)S(1)}, bf16[1536,768]{1,0:T(8,128)(2,1)}, u32[]{:S(2)}, u32[]{:S(2)}) %collective-permute-start) | collective-permute-done | bytes 2359328 | tf_op jit(solution)/shard_map/ppermute | solution.py:410
  57.4 63.2 %layer.1 = (bf16[512,768]{1,0:T(8,128)(2,1)}, f32[512,768]{1,0:T(8,128)}, bf16[1536,768]{1,0:T(8,128)(2,1)}, bf16[1536,768]{1,0:T(8,128)(2,1)}) custom-call(bf16[512,768]{1,0:T(8,128)(2,1)} %tokens.1, s32[1,512]{1,0:T(1,128)} %segments.1, bf16[512,768]{1,0:T(8,128)(2,1)} %cotangent.1, bf16[1536,768]{1,0:T(8,128)(2,1)} %bitcast.11, ...), custom_call_target="tpu_custom_call" | custom-call | tf_op jit(solution)/shard_map/layer/pallas_call | solution.py:427
  120.6 0.1 collective-permute-start.1
  120.8 4.6 %collective-permute-done.1.right = bf16[1536,768]{1,0:T(8,128)(2,1)S(1)} collective-permute-done((bf16[1536,768]{1,0:T(8,128)(2,1)}, bf16[1536,768]{1,0:T(8,128)(2,1)S(1)}, u32[]{:S(2)}, u32[]{:S(2)}) %collective-permute-start.1) | collective-permute-done | bytes 2359328 | tf_op jit(solution)/shard_map/ppermute | solution.py:410
  125.4 0.0 copy-start
  125.4 1.7 copy-done
  127.0 0.5 chip_sum.1
  127.6 38.2 %all_to_all.23 = bf16[64,24,768]{2,1,0:T(8,128)(2,1)S(1)} all-to-all(bf16[64,24,768]{2,1,0:T(8,128)(2,1)S(1)} %bitcast.6), channel_id=1, replica_groups={{0,2,4,6,8,10,12,14,16,18,20,22,24,26,28,30,32,34,36,38,40,42,44,46,48,..., dimensions={0} | all-to-all | bytes 4718592 | tf_op jit(solution)/shard_map/all_to_all | solution.py:442
  165.7 1.0 slice_sum.1
Async XLA Ops:
  0.6 0.7 copy-start.1
  1.4 0.7 copy-start.2
  2.1 0.7 copy-start.3
  2.8 0.7 copy-start.4
  3.5 0.7 copy-start.5
  4.1 0.7 copy-start.6
  4.8 0.7 copy-start.7
  5.4 0.7 copy-start.8
  6.1 0.7 copy-start.9
  51.3 1.4 copy-start.10
  52.7 4.7 %collective-permute-start = (bf16[1536,768]{1,0:T(8,128)(2,1)S(1)}, bf16[1536,768]{1,0:T(8,128)(2,1)}, u32[]{:S(2)}, u32[]{:S(2)}) collective-permute-start(bf16[1536,768]{1,0:T(8,128)(2,1)S(1)} %bitcast.10), channel_id=1, source_target_pairs={{0,1},{1,0},{2,3},{3,2},{4,5},{5,4},{6,7},{7,6},{8,9},{9,8},{10,11... | collective-permute-start | bytes 7077896 | tf_op jit(solution)/shard_map/ppermute | solution.py:410
  120.6 4.7 %collective-permute-start.1 = (bf16[1536,768]{1,0:T(8,128)(2,1)}, bf16[1536,768]{1,0:T(8,128)(2,1)S(1)}, u32[]{:S(2)}, u32[]{:S(2)}) collective-permute-start(bf16[1536,768]{1,0:T(8,128)(2,1)} %get-tuple-element.27), channel_id=1, source_target_pairs={{0,1},{1,0},{2,3},{3,2},{4,5},{5,4},{6,7},{7,6},{8,9},{9,8},{10,11... | collective-permute-start | bytes 7077896 | tf_op jit(solution)/shard_map/ppermute | solution.py:410
  125.4 1.7 copy-start

commit v2 on v1

v2 whole, which is shorter than its diff:
```python
import jax
import jax.numpy as jnp
from jax import lax
from jax.experimental import pallas as pl
from jax.experimental.pallas import tpu as pltpu
from jax.sharding import PartitionSpec as P

AXES = ("dp", "fsdp")
D = 768
F = 3072
G = 4
DG = 192
QKV = 3 * DG
HEADS = 12
HEAD = 64
TOK = 512
LONG = 384
CHIPS = 64
ROWS = 24
EPS = 1e-05
BAND = 64
BANDS = D // BAND
BF = jnp.bfloat16
F32 = jnp.float32
MIB = 1 << 20

SIDE = 18
WIDE = 2 * DG
TILES = CHIPS * ROWS


def dot(left, right, over_left, over_right):
    return lax.dot_general(
        left, right, (((over_left,), (over_right,)), ((), ())), preferred_element_type=F32
    )


def iota(shape, axis):
    return lax.broadcasted_iota(jnp.int32, shape, axis)


def each(count, step, unroll=1):
    def body(i, nothing):
        step(i)
        return nothing

    lax.fori_loop(0, count, body, 0, unroll=unroll)


def part(i, size):
    return pl.ds(pl.multiple_of(i * size, size), size)


def halves(chunk):
    return jnp.sum(chunk.reshape(BAND // 8, 8, TOK), axis=0)


def means(count, bands):
    def body(i, sums):
        return tuple(kept + halves(chunk) for kept, chunk in zip(sums, bands(part(i, BAND)), strict=True))

    sums = lax.fori_loop(0, BANDS, body, (jnp.zeros((8, TOK), F32),) * count, unroll=2)
    return [jnp.sum(total, axis=0, keepdims=True) * (1.0 / D) for total in sums]


def lane_sum(chunk):
    return jnp.sum(chunk, axis=1, keepdims=True)


def pick_hidden():
    return iota((192, 128), 1) - 8 == (iota((192, 128), 0) & 3)


def arrival(core, by_device, axis):
    sorted_row = iota((192, 1) if axis == 0 else (1, 192), axis)
    if by_device:
        device = (sorted_row * 2731) >> 16
        row = sorted_row - device * ROWS
    else:
        block = (sorted_row * 1366) >> 16
        sixth = (sorted_row * 10923) >> 16
        device = sixth - block * 8
        row = block * 6 + sorted_row - sixth * 6
    return jnp.where((device & 1) == core, 0, 96) + (device >> 1) * ROWS + row


def sorter(core, by_device=False):
    return (arrival(core, by_device, 0) == iota((192, 192), 1)).astype(F32).astype(BF)


def unsorter(core, by_device=False):
    return (arrival(core, by_device, 1) == iota((192, 192), 0)).astype(F32).astype(BF)


def grower():
    return ((iota((192, 48), 0) >> 2) == iota((192, 48), 1)).astype(F32).astype(BF)


def low_lanes():
    return iota((48, 128), 1) < 64


def repeat(tile, target):
    whole = tile[...].astype(BF)
    twice = jnp.concatenate([whole, whole], axis=0)

    def copy(pair):
        target[part(pair, 2 * ROWS), :] = twice

    each(CHIPS // 2, copy, unroll=4)


def pack_attention_kernel(*refs):
    far, packed, near, (tile, square, arrive) = refs[:7], refs[7], refs[8:15], refs[15:]
    arriving = moves(zip(far, near, strict=True), arrive)
    start(*arriving)
    wait(*arriving)
    qkv, out, qv, outb, upb, gain, shift = near
    square[...] = jnp.zeros_like(square)
    for place, rows in enumerate((qv, outb, gain, shift)):
        square[2 * place : 2 * place + 2, 0:6] = rows[...].astype(F32)
    columns = square[...].T
    grown = jnp.where(iota((8, ROWS), 1) // 4 == iota((8, ROWS), 0), upb[...].astype(F32), 0.0)
    lanes = (iota((ROWS, 128), 1) - 8 == iota((ROWS, 128), 0) % 4).astype(F32)
    hidden = jnp.dot(grown, lanes, preferred_element_type=F32)
    tile[...] = jnp.zeros_like(tile)
    for block in range(4):
        rows, lanes = slice(6 * block, 6 * block + 6), slice(DG * block, DG * block + DG)
        here, there = (slice(0, DG), slice(DG, WIDE))[:: 1 - 2 * (block % 2)]
        tile[rows, here] = out[:, lanes].astype(F32)
        if block < 3:
            tile[rows, there] = qkv[:, lanes].astype(F32)
    tile[SIDE:ROWS, 0:128] = (columns[0:8] + hidden)[0:6]
    repeat(tile, packed)


def pack_feed_kernel(up_far, down_far, packed, up, down, tile, arrive):
    arriving = moves([(up_far, up), (down_far, down)], arrive)
    start(*arriving)
    wait(*arriving)
    for block in range(4):
        rows, lanes = slice(6 * block, 6 * block + 6), slice(DG * block, DG * block + DG)
        tile[rows, 0:DG] = up[:, lanes].astype(F32)
    tile[:, DG:WIDE] = down[...].astype(F32)
    repeat(tile, packed)


def turn_kernel(tokens, segments, cotangent, turn, x_t, c_t):
    ids = segments[...]
    count0 = jnp.sum((ids == 0).astype(jnp.int32))
    count1 = jnp.sum((ids == 1).astype(jnp.int32))
    start = jnp.where(count0 == LONG, 0, jnp.where(count1 == LONG, count0, count0 + count1))

    def turn_rows(i):
        place = iota((64, TOK), 1) + start
        place = jnp.where(place >= TOK, place - TOK, place)
        turn[part(i, 64), :] = jnp.where(iota((64, TOK), 0) + i * 64 == place, 1.0, 0.0).astype(BF)

    each(8, turn_rows)

    def turn_features(i):
        x_t[part(i, 256), :] = dot(tokens[:, part(i, 256)], turn[...], 0, 0).astype(BF)
        c_t[part(i, 256), :] = dot(cotangent[:, part(i, 256)], turn[...], 0, 0).astype(BF)

    each(3, turn_features)


def moves(pairs, sems):
    return [pltpu.make_async_copy(source, target, sems.at[i]) for i, (source, target) in enumerate(pairs)]


def start(*copies):
    for copy in copies:
        copy.start()


def wait(*copies):
    for copy in copies:
        copy.wait()


def own_core():
    return lax.rem(lax.axis_index("fsdp"), 2)


SPANS = (slice(0, LONG), slice(LONG, TOK))


def attention_kernel(
    segments, mine, other, x_far,
    w_qkv_far, w_out_far, side_far, q_far, k_far, v_far, ctx_far, probs_far, small_far, hat_far, scale,
    x_t, w_qkv, w_out, side, q_t, k_t, v_t, ctx_t, probs, probs_small, first, hat, arrive, leave,
):
    halves_of_hat = [(hat.at[part(i, D // 2), :], hat_far.at[part(i, D // 2), :]) for i in range(2)]
    (arriving,) = moves([(x_far, x_t)], arrive)
    leaving = moves(
        [(w_qkv, w_qkv_far), (w_out, w_out_far), (side, side_far), (q_t, q_far), (k_t, k_far), (v_t, v_far),
         (ctx_t, ctx_far), (probs, probs_far), (probs_small, small_far), *halves_of_hat],
        leave,
    )
    start(arriving)
    sort = sorter(own_core())

    def place_block(i):
        rows = part(i, 96)
        both = jnp.concatenate([mine[rows, :], other[rows, :]], axis=0)
        placed = jnp.dot(sort, both, preferred_element_type=F32).astype(BF)
        here = part(i, 48)
        blocks = [placed[48 * block : 48 * block + 48] for block in range(4)]
        for begin, target, left, right in (
            (0, w_out, 0, 1), (WIDE, w_out, 2, 3), (0, w_qkv, 1, 0), (WIDE, w_qkv, 3, 2),
        ):
            target[here, begin : begin + 128] = blocks[left][:, 0:128]
            target[here, begin + 128 : begin + 256] = jnp.where(
                low_lanes(), blocks[left][:, 128:256], blocks[right][:, 128:256]
            )
            target[here, begin + 256 : begin + 384] = blocks[right][:, 256:384]
        side[here, :] = blocks[3][:, 0:128].astype(F32)

    each(16, place_block, unroll=4)
    start(*leaving[:3])
    wait(arriving)

    ids = segments[...]
    count0 = jnp.sum((ids == 0).astype(jnp.int32))
    count1 = jnp.sum((ids == 1).astype(jnp.int32))
    count2 = TOK - count0 - count1
    border = jnp.where(count0 == LONG, count1, jnp.where(count1 == LONG, count2, count0))
    together = (iota((128, 128), 0) < border) == (iota((128, 128), 1) < border)

    def attend(g):
        rows = part(g, DG)
        packed = dot(w_qkv[rows, 0:WIDE], x_t[rows, :], 0, 0)
        k_t[rows, :] = packed[0:DG].astype(BF)
        q_t[rows, :] = ((packed[DG:WIDE] + side[rows, 0:1]).astype(BF).astype(F32) * 0.125).astype(BF)
        packed = dot(w_qkv[rows, 512:768], x_t[rows, :], 0, 0)
        v_t[rows, :] = (packed[64:256] + side[rows, 1:2]).astype(BF)
        for third in range(3):
            head = g * 3 + third
            rows = part(head, HEAD)
            for cols, kept in zip(SPANS, (probs, probs_small), strict=True):
                scores = dot(k_t[rows, cols], q_t[rows, cols], 0, 0)
                if kept is probs_small:
                    scores = jnp.where(together, scores, -1000000000.0)
                power = jnp.exp(scores - jnp.max(scores, axis=0, keepdims=True))
                share = (power * (1.0 / jnp.sum(power, axis=0, keepdims=True))).astype(BF)
                kept[head] = share
                ctx_t[rows, cols] = dot(v_t[rows, cols], share, 1, 0).astype(BF)

    each(G, attend)
    start(*leaving[3:9])

    def project(i):
        rows = part(i, 128)
        attended = dot(w_out[:, rows], ctx_t[...], 0, 0) + side[rows, 2:3]
        first[rows, :] = x_t[rows, :].astype(F32) + attended

    each(6, project)
    (mean,) = means(1, lambda rows: (first[rows, :],))
    (variance,) = means(1, lambda rows: ((first[rows, :] - mean) ** 2,))
    scale[...] = lax.rsqrt(variance + EPS)

    def norm(i):
        rows = part(i, BAND)
        hat[rows, :] = (first[rows, :] - mean) * scale[...]

    each(BANDS // 2, norm, unroll=3)
    start(leaving[9])
    each(BANDS // 2, lambda i: norm(i + BANDS // 2), unroll=3)
    start(leaving[10])
    wait(*leaving)


def feed_kernel(
    mine, other, side_far, hat_far, c_far,
    result_far, d_first_far, g_side_far, keep, send,
    side, hat, c_t, result, d_first, g_side,
    w_up, w_down, up_bias, first_low, active, slope, low_t, branch_pad, g_up, g_down, arrive, leave,
):
    arriving = moves([(side_far, side), (hat_far, hat), (c_far, c_t)], arrive)
    leaving = moves([(result, result_far), (d_first, d_first_far), (g_side, g_side_far)], leave)
    start(*arriving)
    core = own_core()
    sort, sort_devices, grow = sorter(core), sorter(core, True), grower()

    def place_block(i):
        rows = part(i, 96)
        both = jnp.concatenate([mine[rows, :], other[rows, :]], axis=0)
        placed = jnp.dot(sort, both[:, 0:256], preferred_element_type=F32).astype(BF)
        units = part(i, 192)
        w_down[units, :] = jnp.dot(sort_devices, both[:, 128:384], preferred_element_type=F32).astype(BF)
        here = part(i, 48)
        for block in range(4):
            w_up[here, DG * block : DG * block + DG] = placed[48 * block : 48 * block + 48, 0:DG]
        hidden = jnp.dot(grow, side[here, :].astype(BF), preferred_element_type=F32)
        up_bias[units, :] = lane_sum(jnp.where(pick_hidden(), hidden, 0.0))

    wait(arriving[0])
    each(16, place_block, unroll=4)
    wait(*arriving[1:])

    def first_norm(i):
        rows = part(i, BAND)
        first = hat[rows, :] * side[rows, 4:5] + side[rows, 6:7]
        d_first[rows, :] = first
        first_low[rows, :] = first.astype(BF)

    each(BANDS, first_norm, unroll=2)

    def feed(g):
        rows = part(g, DG)
        for third in range(3):
            units = part(g * 3 + third, 256)
            upper = dot(w_up[rows, 256 * third : 256 * third + 256], first_low[rows, :], 0, 0) + up_bias[units, :]
            below = 0.5 + 0.5 * lax.erf(upper * 0.7071067811865476)
            density = jnp.exp(-0.5 * upper * upper) * 0.3989422804014327
            active[units, :] = (upper * below).astype(BF)
            slope[units, :] = below + upper * density
        units = part(g, D)
        branch = dot(w_down[units, :], active[units, :], 0, 0)[64:256]
        d_first[rows, :] += branch + side[rows, 3:4]

    each(G, feed)

    (mean,) = means(1, lambda rows: (d_first[rows, :],))
    (variance,) = means(1, lambda rows: ((d_first[rows, :] - mean) ** 2,))
    scale = lax.rsqrt(variance + EPS)

    def norm(rows):
        hats = (d_first[rows, :] - mean) * scale
        d_first[rows, :] = hats
        result[rows, :] = (hats * side[rows, 5:6] + side[rows, 7:8]).astype(BF)
        slopes = c_t[rows, :].astype(F32)
        g_side[rows, :] = jnp.zeros((BAND, 128), F32)
        g_side[rows, 5:6] = lane_sum(slopes * hats)
        g_side[rows, 7:8] = lane_sum(slopes)
        slopes = slopes * side[rows, 5:6]
        return slopes, slopes * hats

    lean, tilt = means(2, norm)
    start(leaving[0])

    def norm_back(i):
        rows = part(i, BAND)
        slopes = c_t[rows, :].astype(F32) * side[rows, 5:6]
        back = scale * (slopes - lean - d_first[rows, :] * tilt)
        d_first[rows, :] = back
        low = back.astype(BF)
        g_side[rows, 3:4] = lane_sum(low.astype(F32))
        low_t[rows, :] = low

    each(BANDS, norm_back, unroll=2)
    for g in range(G):
        branch_pad[g, 0:64, :] = jnp.zeros((64, TOK), BF)
        branch_pad[g, 64:256, :] = low_t[DG * g : DG * (g + 1), :]

    def feed_back(g):
        rows = part(g, DG)
        for third in range(3):
            units = part(g * 3 + third, 256)
            span = slice(256 * third, 256 * third + 256)
            d_active = dot(w_down[units, :], branch_pad[g], 1, 0)
            d_upper = (d_active * slope[units, :]).astype(BF)
            up_bias[units, :] = lane_sum(d_upper.astype(F32))
            g_down[units, :] = dot(active[units, :], branch_pad[g], 1, 1).astype(BF)
            g_up[rows, span] = dot(first_low[rows, :], d_upper, 1, 1).astype(BF)
            active[units, :] = d_upper
        d_first[rows, :] += dot(w_up[rows, :], active[part(g, D), :], 1, 0)

    each(G, feed_back)
    start(leaving[1])
    unsort, unsort_devices = unsorter(core), unsorter(core, True)

    def tile_block(i):
        here, units, rows = part(i, 48), part(i, 192), part(i, 96)
        hidden = jnp.where(pick_hidden(), up_bias[units, :], 0.0)
        g_side[here, :] += dot(grow.astype(F32), hidden, 0, 0)
        ups = jnp.concatenate([g_up[here, DG * block : DG * block + DG] for block in range(4)], axis=0)
        ups = jnp.concatenate([ups, jnp.zeros((192, 64), BF)], axis=1)
        placed = dot(unsort, ups, 1, 0)
        downs = dot(unsort_devices, g_down[units, :], 1, 0)
        for target, begin in ((keep, 0), (send, 96)):
            span = slice(begin, begin + 96)
            target[rows, 0:128] = placed[span, 0:128].astype(BF)
            target[rows, 128:256] = (placed[span, 128:256] + downs[span, 0:128]).astype(BF)
            target[rows, 256:384] = downs[span, 128:256].astype(BF)

    each(16, tile_block, unroll=4)
    start(leaving[2])
    wait(*leaving)


def attention_back_kernel(
    d_first_far, hat_far, side_far, g_feed_far, w_out_far, ctx_far, q_far, k_far, v_far, probs_far, small_far, x_far,
    scale,
    d_sum_far, packed_far, keep, send,
    d_first, hat, side, g_feed, w_out, ctx_t, q_t, k_t, v_t, probs, probs_small, x_t,
    d_sum, packed_t, low_t, d_ctx, g_side, g_qkv, g_out, arrive, leave,
):
    arriving = moves(
        [(d_first_far, d_first), (hat_far, hat), (side_far, side), (g_feed_far, g_feed), (w_out_far, w_out),
         (ctx_far, ctx_t), (q_far, q_t), (k_far, k_t), (v_far, v_t), (probs_far, probs), (small_far, probs_small),
         (x_far, x_t)],
        arrive,
    )
    leaving = moves([(d_sum, d_sum_far), (packed_t, packed_far)], leave)
    start(*arriving)
    wait(*arriving[:4])

    def norm_sums(rows):
        slopes, hats = d_first[rows, :], hat[rows, :]
        g_side[rows, :] = g_feed[rows, :]
        g_side[rows, 4:5] = lane_sum(slopes * hats)
        g_side[rows, 6:7] = lane_sum(slopes)
        slopes = slopes * side[rows, 4:5]
        return slopes, slopes * hats

    lean, tilt = means(2, norm_sums)

    def norm_back(i):
        rows = part(i, BAND)
        back = scale[...] * (d_first[rows, :] * side[rows, 4:5] - lean - hat[rows, :] * tilt)
        d_sum[rows, :] = back
        low = back.astype(BF)
        g_side[rows, 2:3] = lane_sum(low.astype(F32))
        low_t[rows, :] = low

    each(BANDS, norm_back, unroll=2)

    start(leaving[0])
    wait(*arriving[4:6])

    def project_back(i):
        rows = part(i, 128)
        g_out[rows, :] = dot(ctx_t[rows, :], low_t[...], 1, 1).astype(BF)
        d_ctx[rows, :] = dot(w_out[rows, :], low_t[...], 1, 0).astype(BF)

    each(6, project_back)
    wait(*arriving[6:])

    def attend_back(g):
        for third in range(3):
            head = g * 3 + third
            rows = part(head, HEAD)
            at = HEAD * third
            for cols, kept in zip(SPANS, (probs, probs_small), strict=True):
                d_out = d_ctx[rows, cols]
                share_low = kept[head]
                share = share_low.astype(F32)
                d_share = dot(v_t[rows, cols], d_out, 0, 0)
                packed_t[g, 3 * DG + at : 3 * DG + at + HEAD, cols] = dot(d_out, share_low, 1, 1).astype(BF)
                d_scores = share * (d_share - jnp.sum(d_share * share, axis=0, keepdims=True))
                d_scores = d_scores.astype(BF)
                packed_t[g, DG + at : DG + at + HEAD, cols] = (0.125 * dot(k_t[rows, cols], d_scores, 1, 0)).astype(BF)
                packed_t[g, at : at + HEAD, cols] = dot(q_t[rows, cols], d_scores, 1, 1).astype(BF)
        rows = part(g, DG)
        packed_t[g, WIDE : 3 * DG, :] = jnp.zeros((DG, TOK), BF)
        g_qkv[rows, 0:WIDE] = dot(x_t[rows, :], packed_t[g, 0:WIDE, :], 1, 1).astype(BF)
        g_qkv[rows, 512:768] = dot(x_t[rows, :], packed_t[g, 512:768, :], 1, 1).astype(BF)
        g_side[rows, 0:1] = lane_sum(packed_t[g, DG:WIDE, :].astype(F32))
        g_side[rows, 1:2] = lane_sum(packed_t[g, 3 * DG :, :].astype(F32))

    each(G, attend_back)
    start(leaving[1])
    unsort = unsorter(own_core())

    def tile_block(i):
        here, rows = part(i, 48), part(i, 96)
        blocks = []
        for begin in (0, WIDE):
            mixed_out, mixed_qkv = g_out[here, begin + 128 : begin + 256], g_qkv[here, begin + 128 : begin + 256]
            blocks.append(
                [
                    g_out[here, begin : begin + 128],
                    jnp.where(low_lanes(), mixed_out, mixed_qkv),
                    g_qkv[here, begin + 256 : begin + 384],
                ]
            )
            blocks.append(
                [
                    g_qkv[here, 0:128] if begin == 0 else g_side[here, :].astype(BF),
                    jnp.where(low_lanes(), mixed_qkv, mixed_out),
                    g_out[here, begin + 256 : begin + 384],
                ]
            )
        both = jnp.concatenate([jnp.concatenate(block, axis=1) for block in blocks], axis=0)
        placed = dot(unsort, both, 1, 0).astype(BF)
        keep[rows, :] = placed[0:96]
        send[rows, :] = placed[96:192]

    each(16, tile_block, unroll=4)
    wait(*leaving)


def token_kernel(w_qkv, packed_t, d_sum, turn, result, grad_tokens, output, high, low):
    def total(g):
        rows = part(g, DG)
        back = dot(w_qkv[rows, 0:WIDE], packed_t[g, 0:WIDE, :], 1, 0)
        whole = d_sum[rows, :] + back + dot(w_qkv[rows, 512:768], packed_t[g, 512:768, :], 1, 0)
        high[rows, :] = whole.astype(BF)
        low[rows, :] = (whole - high[rows, :].astype(F32)).astype(BF)

    each(G, total)

    def write(i):
        rows = part(i, 256)
        grad_tokens[:, rows] = dot(turn[...], high[rows, :], 1, 1) + dot(turn[...], low[rows, :], 1, 1)
        output[:, rows] = dot(turn[...], result[rows, :], 1, 1).astype(BF)

    each(3, write)


def add_kernel(left, right, total):
    total[...] = (left[...].astype(F32) + right[...].astype(F32)).astype(BF)


def tile_sum(parts):
    total = jnp.zeros((2 * ROWS, WIDE), F32)
    for pair in range(CHIPS // 2):
        total += parts[2 * ROWS * pair : 2 * ROWS * (pair + 1), :].astype(F32)
    return total[0:ROWS] + total[ROWS:]


def sum_feed_kernel(parts, up, down):
    total = tile_sum(parts)
    for block in range(4):
        up[:, DG * block : DG * block + DG] = total[6 * block : 6 * block + 6, 0:DG]
    down[...] = total[:, DG:WIDE]


def sum_attention_kernel(parts, qkv, out, qv, outb, upb, gain, shift, square):
    total = tile_sum(parts)
    for block in range(4):
        rows, lanes = slice(6 * block, 6 * block + 6), slice(DG * block, DG * block + DG)
        here, there = (slice(0, DG), slice(DG, WIDE))[:: 1 - 2 * (block % 2)]
        out[:, lanes] = total[rows, here]
        if block < 3:
            qkv[:, lanes] = total[rows, there]
    square[...] = jnp.zeros_like(square)
    square[0:6, :] = total[SIDE:ROWS, 0:128]
    columns = square[...].T
    for place, rows in enumerate((qv, outb, gain, shift)):
        rows[...] = columns[2 * place : 2 * place + 2, 0:6]
    lanes = (iota((128, ROWS), 0) - 8 == iota((128, ROWS), 1) % 4).astype(F32)
    grown = jnp.dot(square[0:8, :], lanes, preferred_element_type=F32, precision=lax.Precision.HIGHEST)
    grown = jnp.where(iota((8, ROWS), 1) // 4 == iota((8, ROWS), 0), grown, 0.0)
    upb[...] = jnp.sum(grown, axis=0, keepdims=True)


FAR = pl.BlockSpec(memory_space=pl.ANY)
NEAR = pl.BlockSpec(memory_space=pltpu.VMEM)


def call(kernel, shapes, scratch, name, limit, flops=0, near=(), sems=()):
    scratch = [pltpu.VMEM(*shape) for shape in scratch] + [pltpu.SemaphoreType.DMA((count,)) for count in sems]

    def specs(count, base):
        return [NEAR if not sems or base + i in near else FAR for i in range(count)]

    def run(*inputs):
        if sems:
            inputs = [x if i in near else pltpu.with_memory_space_constraint(x, pltpu.HBM) for i, x in enumerate(inputs)]
        return pl.pallas_call(
            kernel,
            in_specs=specs(len(inputs), 0),
            out_specs=specs(len(shapes), len(inputs)),
            out_shape=[
                pltpu.HBM(*shape) if sems and len(inputs) + i not in near else jax.ShapeDtypeStruct(*shape)
                for i, shape in enumerate(shapes)
            ],
            scratch_shapes=scratch,
            compiler_params=pltpu.CompilerParams(vmem_limit_bytes=limit * MIB),
            cost_estimate=pl.CostEstimate(flops=flops, bytes_accessed=0, transcendentals=0),
            name=name,
        )(*inputs)

    return run


def exchange(array):
    groups = [[y * 32 + i for y in range(4) for i in range(core, 32, 2)] for core in range(2)]
    return lax.all_to_all(array, AXES, 0, 0, axis_index_groups=groups, tiled=True)


def swap(array):
    return lax.ppermute(array, "fsdp", [(i, i ^ 1) for i in range(32)])


def local(
    tokens, segment_ids, qkv_weight, out_weight, up_weight, down_weight,
    qv_bias, out_bias, up_bias, norm_gain, norm_shift, cotangent,
):
    tile, probs = ((TILES, WIDE), BF), ((HEADS, LONG, LONG), BF)
    full, low, square, side = ((D, TOK), F32), ((D, TOK), BF), ((D, D), BF), ((D, 128), F32)
    small, packed, row = ((HEADS, 128, 128), BF), ((G, D, TOK), BF), ((1, TOK), F32)
    one_tile = ((ROWS, WIDE), F32)
    shards = (qkv_weight, out_weight, qv_bias, out_bias, up_bias.reshape(1, ROWS), norm_gain, norm_shift)
    pack_a = call(
        pack_attention_kernel, [tile], [*((x.shape, x.dtype) for x in shards), one_tile, ((128, 128), F32)],
        "pack_attention", 12, near=(7,), sems=(7,),
    )(*shards)[0]
    mine_a = exchange(pack_a)
    pack_f = call(
        pack_feed_kernel, [tile], [((6, D), BF), ((ROWS, DG), BF), one_tile],
        "pack_feed", 12, flops=10**9, near=(2,), sems=(2,),
    )(up_weight, down_weight)[0]
    turn, x_t, c_t = call(
        turn_kernel, [((TOK, TOK), BF), low, low], [], "turn", 60, flops=2 * 2 * TOK * TOK * D
    )(tokens, segment_ids, cotangent)
    mine_a, pack_f, x_t = lax.optimization_barrier((mine_a, pack_f, x_t))
    mine_f = exchange(pack_f)
    w_qkv, w_out, sides, q_t, k_t, v_t, ctx_t, shares, shares_small, hat, scale = call(
        attention_kernel,
        [square, square, side, low, low, low, low, probs, small, full, row],
        [low, square, square, side, low, low, low, low, probs, small, full, full],
        "attention", 44, flops=15 * 10**9, near=(0, 1, 2, 14), sems=(1, 11),
    )(segment_ids, mine_a, swap(mine_a), x_t)
    mine_f, hat = lax.optimization_barrier((mine_f, hat))
    result, d_first, g_side, keep_f, send_f = call(
        feed_kernel,
        [low, full, side, tile, tile],
        [side, full, low, low, full, side,
         square, ((F, 256), BF), ((F, 1), F32), low, ((F, TOK), BF), ((F, TOK), F32), low,
         ((G, 256, TOK), BF), square, ((F, 256), BF)],
        "feed", 44, flops=20 * 10**9, near=(0, 1, 8, 9), sems=(3, 3),
    )(mine_f, swap(mine_f), sides, hat, c_t)
    chip_f = call(add_kernel, [tile], [], "chip_sum_feed", 12)(keep_f, swap(send_f))[0]
    chip_f, d_first = lax.optimization_barrier((chip_f, d_first))
    parts_f = exchange(chip_f)
    d_sum, d_packed, keep_a, send_a = call(
        attention_back_kernel,
        [full, packed, tile, tile],
        [full, full, side, side, square, low, low, low, low, probs, small, low,
         full, packed, low, low, side, square, square],
        "attention_back", 44, flops=20 * 10**9, near=(12, 15, 16), sems=(12, 2),
    )(d_first, hat, sides, g_side, w_out, ctx_t, q_t, k_t, v_t, shares, shares_small, x_t, scale)
    keep_a, send_a, parts_f = lax.optimization_barrier((keep_a, send_a, parts_f))
    chip_a = call(add_kernel, [tile], [], "chip_sum_attention", 12)(keep_a, swap(send_a))[0]
    chip_a, d_sum, parts_f = lax.optimization_barrier((chip_a, d_sum, parts_f))
    parts_a = exchange(chip_a)
    grad_tokens, output = call(
        token_kernel, [((TOK, D), F32), ((TOK, D), BF)], [low, low], "token_gradient", 60, flops=4 * 2 * TOK * TOK * D
    )(w_qkv, d_packed, d_sum, turn, result)
    up, down = call(sum_feed_kernel, [((6, D), F32), ((ROWS, DG), F32)], [], "sum_feed", 12, flops=10**9)(parts_f)
    qkv, out, qv, outb, upb, gain, shift = call(
        sum_attention_kernel,
        [((6, QKV), F32), ((6, D), F32), ((2, 6), F32), ((2, 6), F32), ((1, ROWS), F32), ((2, 6), F32), ((2, 6), F32)],
        [((128, 128), F32)], "sum_attention", 12,
    )(parts_a)
    return output, grad_tokens, qkv, out, up, down, qv, outb, upb.reshape(ROWS), gain, shift


def solution(mesh):
    rows, columns, flat = P(AXES, None), P(None, AXES), P(AXES)
    in_specs = (rows, rows, rows, rows, rows, rows, columns, columns, flat, columns, columns, rows)
    out_specs = (rows, rows, rows, rows, rows, rows, columns, columns, flat, columns, columns)
    return jax.shard_map(local, mesh=mesh, in_specs=in_specs, out_specs=out_specs, check_vma=False)
```

time: 167 us -> 147 us (0.88)
  blocking collectives: 82.5 us -> 0 us
  waiting for transfers between devices: 9.27 us -> 44.2 us
  starting transfers between devices: 0.14 us -> 29.5 us
  local copies, waits for them, and re-layouts: 9.18 us -> 0.01 us
  Pallas kernels: 64.9 us -> 72.1 us
    all_to_all x2 -> x0, blocking collectives: 82.5 us -> none  [the longest x1 44.3 us: local(): lax.all_to_all(packed, AXES, 0, 0, axis_index_groups=groups, tiled=True)]
    all_to_all x0 -> x4, waiting for transfers between devices: none -> 35.8 us  [exchange(): lax.all_to_all(array, AXES, 0, 0, axis_index_groups=groups, tiled=True)]
    all_to_all x0 -> x4, starting transfers between devices: none -> 29.2 us  [exchange(): lax.all_to_all(array, AXES, 0, 0, axis_index_groups=groups, tiled=True)]
    unnamed x22 -> x2, local copies, waits for them, and re-layouts: 9.18 us -> 0.01 us
    pallas_call x4 -> x11, Pallas kernels: 64.9 us -> 72.1 us  [run(): pl.pallas_call(kernel, in_specs=specs(len(inputs), 0), out_specs=specs(le...]
    ppermute x2 -> x4, waiting for transfers between devices: 9.27 us -> 8.4 us  [swap(): return lax.ppermute(array, 'fsdp', [(i, i ^ 1) for i in range(32)])]
  transfers between devices with their start and end apart: 2 -> 8, of which waited for: 2 -> 7; matrix products, arithmetic and copies ran while one was open for 0% -> 0% of each run, Pallas kernels for 0% -> 31%
where the time goes in v2:
time: 147 us
  Pallas kernels  72.1 us (49%)
  waiting for transfers between devices  44.2 us (30%)
  starting transfers between devices  29.5 us (20%)
    pallas_call x11, Pallas kernels, run(): pl.pallas_call(kernel, in_specs=specs(len(inputs), 0), out_specs=specs(le...  72.1 us
    all_to_all x4, waiting for transfers between devices, exchange(): lax.all_to_all(array, AXES, 0, 0, axis_index_groups=groups, tiled=True)  35.8 us
    all_to_all x4, starting transfers between devices, exchange(): lax.all_to_all(array, AXES, 0, 0, axis_index_groups=groups, tiled=True)  29.2 us
    ppermute x4, waiting for transfers between devices, swap(): return lax.ppermute(array, 'fsdp', [(i, i ^ 1) for i in range(32)])  8.4 us
  transfers between devices with their start and end apart: 8, of which 7 were waited for; matrix products, arithmetic and copies ran while one was open for 0% of the time, Pallas kernels for 31%

profile of v2, /device:TPU:0, one launch (start us, length us, event | category | flops | bytes accessed | tf_op | source)
XLA Modules:
  0.0 146.6 jit_solution(9208293594678920793)
XLA Ops:
  0.6 2.1 %pack_attention.1 = bf16[1536,384]{1,0:T(8,128)(2,1)} custom-call(bf16[6,576]{1,0:T(8,128)(2,1)} %refs_0_.1, bf16[6,768]{1,0:T(8,128)(2,1)} %refs_1_.1, bf16[2,6]{1,0:T(2,128)(2,1)} %refs_2_.1, bf16[2,6]{1,0:T(2,128)(2,1)} %refs_3_.1, bf16[1,24]{1,0:T(2,128)(2,1)} %bitcast.16, bf16[2,6]{1,0:T(2,128)(2,1)} %refs_5_.1, bf16[2,6]{1,0:T(2,128)(2,1)} %refs_6_.1), custom_call_target="tpu_custom_call" | custom-call | tf_op jit(solution)/shard_map/pack_attention/pallas_call | solution.py:563
  2.7 11.5 %all-to-all-start = ((bf16[64,24,384]{2,1,0:T(8,128)(2,1)}), bf16[64,24,384]{2,1,0:T(8,128)(2,1)S(1)}, u32[]{:S(2)}, u32[]{:S(2)}) async-start(bf16[64,24,384]{2,1,0:T(8,128)(2,1)} %bitcast.1), calls=%async_computation | async-start | bytes 2359296 | tf_op jit(solution)/shard_map/all_to_all | solution.py:582
  14.3 4.1 %turn.1 = (bf16[512,512]{1,0:T(8,128)(2,1)}, bf16[768,512]{1,0:T(8,128)(2,1)}, bf16[768,512]{1,0:T(8,128)(2,1)}) custom-call(bf16[512,768]{1,0:T(8,128)(2,1)} %tokens.1, s32[1,512]{1,0:T(1,128)} %segments.3, bf16[512,768]{1,0:T(8,128)(2,1)} %cotangent.1), custom_call_target="tpu_custom_call" | custom-call | flops 805306368 | tf_op jit(solution)/shard_map/turn/pallas_call | solution.py:563
  18.4 2.0 %pack_feed.1 = bf16[1536,384]{1,0:T(8,128)(2,1)} custom-call(bf16[6,768]{1,0:T(8,128)(2,1)} %up_far.1, bf16[24,192]{1,0:T(8,128)(2,1)} %down_far.1), custom_call_target="tpu_custom_call" | custom-call | flops 1000000000 | tf_op jit(solution)/shard_map/pack_feed/pallas_call | solution.py:563
  20.4 14.0 %all-to-all-done = bf16[64,24,384]{2,1,0:T(8,128)(2,1)S(1)} async-done(((bf16[64,24,384]{2,1,0:T(8,128)(2,1)}), bf16[64,24,384]{2,1,0:T(8,128)(2,1)S(1)}, u32[]{:S(2)}, u32[]{:S(2)}) %all-to-all-start) | async-done | bytes 1179680 | tf_op jit(solution)/shard_map/all_to_all | solution.py:582
  34.3 0.0 collective-permute-start
  34.3 0.0 copy-start
  34.3 4.9 %all-to-all-start.1 = ((bf16[64,24,384]{2,1,0:T(8,128)(2,1)}), bf16[64,24,384]{2,1,0:T(8,128)(2,1)S(1)}, u32[]{:S(2)}, u32[]{:S(2)}) async-start(bf16[64,24,384]{2,1,0:T(8,128)(2,1)} %bitcast.3), calls=%async_computation.1 | async-start | bytes 2359296 | tf_op jit(solution)/shard_map/all_to_all | solution.py:582
  39.2 0.0 collective-permute-done.other
  39.2 0.0 copy-done
  39.2 13.6 %attention.1 = (bf16[768,768]{1,0:T(8,128)(2,1)}, bf16[768,768]{1,0:T(8,128)(2,1)}, f32[768,128]{1,0:T(8,128)}, bf16[768,512]{1,0:T(8,128)(2,1)}, bf16[768,512]{...) custom-call(s32[1,512]{1,0:T(1,128)S(1)} %copy-done, ...), custom_call_target="tpu_custom_call" | custom-call | flops 15000000512 | tf_op jit(solution)/shard_map/attention/pallas_call | solution.py:563
  52.8 7.4 %all-to-all-done.1 = bf16[64,24,384]{2,1,0:T(8,128)(2,1)S(1)} async-done(((bf16[64,24,384]{2,1,0:T(8,128)(2,1)}), bf16[64,24,384]{2,1,0:T(8,128)(2,1)S(1)}, u32[]{:S(2)}, u32[]{:S(2)}) %all-to-all-start.1) | async-done | bytes 1179680 | tf_op jit(solution)/shard_map/all_to_all | solution.py:582
  60.2 0.0 collective-permute-start.1
  60.2 2.8 %collective-permute-done.1.other = bf16[1536,384]{1,0:T(8,128)(2,1)S(1)} collective-permute-done((bf16[1536,384]{1,0:T(8,128)(2,1)S(1)}, bf16[1536,384]{1,0:T(8,128)(2,1)S(1)}, u32[]{:S(2)}, u32[]{:S(2)}) %collective-permute-start.1) | collective-permute-done | bytes 1179680 | tf_op jit(solution)/shard_map/ppermute | solution.py:586
  63.0 20.7 %feed.1 = (bf16[768,512]{1,0:T(8,128)(2,1)}, f32[768,512]{1,0:T(8,128)}, f32[768,128]{1,0:T(8,128)}, bf16[1536,384]{1,0:T(8,128)(2,1)S(1)}, bf16[1536,384]{1,0:T(8,128)(2,1)S(1)}) custom-call(bf16[1536,384]{1,0:T(8,128)(2,1)S(1)} %bitcast.13, bf16[1536,384]{1,0:T(8,128)(2,1)S(1)} %collective-permute-done.1.other, f32[768,128]{1,0:T(8,128)} %get-tuple-element.65.side_far, ...), custom_call_target="tpu_custom_call" | custom-call | flops 20000000000 | tf_op jit(solution)/shard_map/feed/pallas_call | solution.py:563
  83.7 0.2 collective-permute-start.2
  83.9 2.7 %collective-permute-done.2.right = bf16[1536,384]{1,0:T(8,128)(2,1)S(1)} collective-permute-done((bf16[1536,384]{1,0:T(8,128)(2,1)S(1)}, bf16[1536,384]{1,0:T(8,128)(2,1)S(1)}, u32[]{:S(2)}, u32[]{:S(2)}) %collective-permute-start.2) | collective-permute-done | bytes 1179680 | tf_op jit(solution)/shard_map/ppermute | solution.py:586
  86.6 1.4 chip_sum_feed.1
  88.0 5.2 %all-to-all-start.2 = ((bf16[64,24,384]{2,1,0:T(8,128)(2,1)}), bf16[64,24,384]{2,1,0:T(8,128)(2,1)S(1)}, u32[]{:S(2)}, u32[]{:S(2)}) async-start(bf16[64,24,384]{2,1,0:T(8,128)(2,1)} %bitcast.5), calls=%async_computation.2 | async-start | bytes 2359296 | tf_op jit(solution)/shard_map/all_to_all | solution.py:582
  93.2 17.7 %attention_back.1 = (f32[768,512]{1,0:T(8,128)}, bf16[4,768,512]{2,1,0:T(8,128)(2,1)}, bf16[1536,384]{1,0:T(8,128)(2,1)S(1)}, bf16[1536,384]{1,0:T(8,128)(2,1)S(1)}) custom-call(f32[768,512]{1,0:T(8,128)} %get-tuple-element.71.d_first_far, f32[768,512]{1,0:T(8,128)} %get-tuple-element.66.hat_far, f32[768,128]{1,0:T(8,128)} %get-tuple-element.65.side_far, ...), custom_call_target="tpu_custom_call" | custom-call | flops 20000000000 | tf_op jit(solution)/shard_map/attention_back/pallas_call | solution.py:563
  110.8 2.6 %all-to-all-done.2 = bf16[64,24,384]{2,1,0:T(8,128)(2,1)S(1)} async-done(((bf16[64,24,384]{2,1,0:T(8,128)(2,1)}), bf16[64,24,384]{2,1,0:T(8,128)(2,1)S(1)}, u32[]{:S(2)}, u32[]{:S(2)}) %all-to-all-start.2) | async-done | bytes 1179680 | tf_op jit(solution)/shard_map/all_to_all | solution.py:582
  113.4 0.0 collective-permute-start.3
  113.4 2.8 %collective-permute-done.3.right = bf16[1536,384]{1,0:T(8,128)(2,1)S(1)} collective-permute-done((bf16[1536,384]{1,0:T(8,128)(2,1)S(1)}, bf16[1536,384]{1,0:T(8,128)(2,1)S(1)}, u32[]{:S(2)}, u32[]{:S(2)}) %collective-permute-start.3) | collective-permute-done | bytes 1179680 | tf_op jit(solution)/shard_map/ppermute | solution.py:586
  116.2 1.4 chip_sum_attention.1
  117.6 7.7 %all-to-all-start.3 = ((bf16[64,24,384]{2,1,0:T(8,128)(2,1)}), bf16[64,24,384]{2,1,0:T(8,128)(2,1)S(1)}, u32[]{:S(2)}, u32[]{:S(2)}) async-start(bf16[64,24,384]{2,1,0:T(8,128)(2,1)} %bitcast.7), calls=%async_computation.3 | async-start | bytes 2359296 | tf_op jit(solution)/shard_map/all_to_all | solution.py:582
  125.3 0.8 sum_feed.1
  126.2 7.6 %token_gradient.1 = (f32[512,768]{1,0:T(8,128)}, bf16[512,768]{1,0:T(8,128)(2,1)}) custom-call(bf16[768,768]{1,0:T(8,128)(2,1)} %get-tuple-element.61.w_qkv, bf16[4,768,512]{2,1,0:T(8,128)(2,1)} %get-tuple-element.81.packed_t, f32[768,512]{1,0:T(8,128)} %get-tuple-element.89.d_sum, bf16[512,512]{1,0:T(8,128)(2,1)} %get-tuple-element.90.turn, ...), custom_call_target="tpu_custom_call" | custom-call | flops 1610612736 | tf_op jit(solution)/shard_map/token_gradient/pallas_call | solution.py:563
  133.7 12.0 %all-to-all-done.3 = bf16[64,24,384]{2,1,0:T(8,128)(2,1)S(1)} async-done(((bf16[64,24,384]{2,1,0:T(8,128)(2,1)}), bf16[64,24,384]{2,1,0:T(8,128)(2,1)S(1)}, u32[]{:S(2)}, u32[]{:S(2)}) %all-to-all-start.3) | async-done | bytes 1179680 | tf_op jit(solution)/shard_map/all_to_all | solution.py:582
  145.7 0.9 sum_attention.1
Async XLA Ops:
  2.7 31.6 %all-to-all-start = ((bf16[64,24,384]{2,1,0:T(8,128)(2,1)}), bf16[64,24,384]{2,1,0:T(8,128)(2,1)S(1)}, u32[]{:S(2)}, u32[]{:S(2)}) async-start(bf16[64,24,384]{2,1,0:T(8,128)(2,1)} %bitcast.1), calls=%async_computation | async-start | bytes 2359296 | tf_op jit(solution)/shard_map/all_to_all | solution.py:582
  34.3 4.9 %collective-permute-start = (bf16[1536,384]{1,0:T(8,128)(2,1)S(1)}, bf16[1536,384]{1,0:T(8,128)(2,1)S(1)}, u32[]{:S(2)}, u32[]{:S(2)}) collective-permute-start(bf16[1536,384]{1,0:T(8,128)(2,1)S(1)} %bitcast.14), channel_id=1, source_target_pairs={{0,1},{1,0},{2,3},{3,2},{4,5},{5,4},{6,7},{7,6},{8,9},{9,8},{10,11... | collective-permute-start | bytes 3538952 | tf_op jit(solution)/shard_map/ppermute | solution.py:586
  34.3 4.9 %copy-start = (s32[1,512]{1,0:T(1,128)S(1)}, s32[1,512]{1,0:T(1,128)}, u32[]{:S(2)}) copy-start(s32[1,512]{1,0:T(1,128)} %segments.3) | copy-start | bytes 6148
  34.3 25.8 %all-to-all-start.1 = ((bf16[64,24,384]{2,1,0:T(8,128)(2,1)}), bf16[64,24,384]{2,1,0:T(8,128)(2,1)S(1)}, u32[]{:S(2)}, u32[]{:S(2)}) async-start(bf16[64,24,384]{2,1,0:T(8,128)(2,1)} %bitcast.3), calls=%async_computation.1 | async-start | bytes 2359296 | tf_op jit(solution)/shard_map/all_to_all | solution.py:582
  60.2 2.8 %collective-permute-start.1 = (bf16[1536,384]{1,0:T(8,128)(2,1)S(1)}, bf16[1536,384]{1,0:T(8,128)(2,1)S(1)}, u32[]{:S(2)}, u32[]{:S(2)}) collective-permute-start(bf16[1536,384]{1,0:T(8,128)(2,1)S(1)} %bitcast.12), channel_id=1, source_target_pairs={{0,1},{1,0},{2,3},{3,2},{4,5},{5,4},{6,7},{7,6},{8,9},{9,8},{10,11... | collective-permute-start | bytes 3538952 | tf_op jit(solution)/shard_map/ppermute | solution.py:586
  83.7 2.9 %collective-permute-start.2 = (bf16[1536,384]{1,0:T(8,128)(2,1)S(1)}, bf16[1536,384]{1,0:T(8,128)(2,1)S(1)}, u32[]{:S(2)}, u32[]{:S(2)}) collective-permute-start(bf16[1536,384]{1,0:T(8,128)(2,1)S(1)} %get-tuple-element.69), channel_id=1, source_target_pairs={{0,1},{1,0},{2,3},{3,2},{4,5},{5,4},{6,7},{7,6},{8,9},{9,8},{10,11... | collective-permute-start | bytes 3538952 | tf_op jit(solution)/shard_map/ppermute | solution.py:586
  88.0 25.4 %all-to-all-start.2 = ((bf16[64,24,384]{2,1,0:T(8,128)(2,1)}), bf16[64,24,384]{2,1,0:T(8,128)(2,1)S(1)}, u32[]{:S(2)}, u32[]{:S(2)}) async-start(bf16[64,24,384]{2,1,0:T(8,128)(2,1)} %bitcast.5), calls=%async_computation.2 | async-start | bytes 2359296 | tf_op jit(solution)/shard_map/all_to_all | solution.py:582
  113.4 2.8 %collective-permute-start.3 = (bf16[1536,384]{1,0:T(8,128)(2,1)S(1)}, bf16[1536,384]{1,0:T(8,128)(2,1)S(1)}, u32[]{:S(2)}, u32[]{:S(2)}) collective-permute-start(bf16[1536,384]{1,0:T(8,128)(2,1)S(1)} %get-tuple-element.86), channel_id=1, source_target_pairs={{0,1},{1,0},{2,3},{3,2},{4,5},{5,4},{6,7},{7,6},{8,9},{9,8},{10,11... | collective-permute-start | bytes 3538952 | tf_op jit(solution)/shard_map/ppermute | solution.py:586
  117.6 28.1 %all-to-all-start.3 = ((bf16[64,24,384]{2,1,0:T(8,128)(2,1)}), bf16[64,24,384]{2,1,0:T(8,128)(2,1)S(1)}, u32[]{:S(2)}, u32[]{:S(2)}) async-start(bf16[64,24,384]{2,1,0:T(8,128)(2,1)} %bitcast.7), calls=%async_computation.3 | async-start | bytes 2359296 | tf_op jit(solution)/shard_map/all_to_all | solution.py:582

commit v3 on v2

v3 whole, which is shorter than its diff:
```python
import jax
import jax.numpy as jnp
from jax import lax
from jax.experimental import pallas as pl
from jax.experimental.pallas import tpu as pltpu
from jax.sharding import PartitionSpec as P

AXES = ("dp", "fsdp")
D = 768
F = 3072
G = 4
DG = 192
QKV = 3 * DG
HEADS = 12
HEAD = 64
TOK = 512
LONG = 384
CHIPS = 64
ROWS = 24
EPS = 1e-05
BAND = 64
BANDS = D // BAND
BF = jnp.bfloat16
F32 = jnp.float32
MIB = 1 << 20

SIDE = 18
WIDE = 2 * DG
TILES = CHIPS * ROWS


def dot(left, right, over_left, over_right):
    return lax.dot_general(
        left, right, (((over_left,), (over_right,)), ((), ())), preferred_element_type=F32
    )


def iota(shape, axis):
    return lax.broadcasted_iota(jnp.int32, shape, axis)


def each(count, step):
    for i in range(count):
        step(i)


def part(i, size):
    return slice(i * size, (i + 1) * size)


def halves(chunk):
    return jnp.sum(chunk.reshape(BAND // 8, 8, TOK), axis=0)


def means(count, bands):
    sums = [jnp.zeros((8, TOK), F32)] * count
    for i in range(BANDS):
        sums = [kept + halves(chunk) for kept, chunk in zip(sums, bands(part(i, BAND)), strict=True)]
    return [jnp.sum(total, axis=0, keepdims=True) * (1.0 / D) for total in sums]


def lane_sum(chunk):
    return jnp.sum(chunk, axis=1, keepdims=True)


def pick_hidden():
    return iota((192, 128), 1) - 8 == (iota((192, 128), 0) & 3)


def arrival(core, by_device, axis):
    sorted_row = iota((192, 1) if axis == 0 else (1, 192), axis)
    if by_device:
        device = (sorted_row * 2731) >> 16
        row = sorted_row - device * ROWS
    else:
        block = (sorted_row * 1366) >> 16
        sixth = (sorted_row * 10923) >> 16
        device = sixth - block * 8
        row = block * 6 + sorted_row - sixth * 6
    return jnp.where((device & 1) == core, 0, 96) + (device >> 1) * ROWS + row


def sorter(core, by_device=False):
    return (arrival(core, by_device, 0) == iota((192, 192), 1)).astype(F32).astype(BF)


def unsorter(core, by_device=False):
    return (arrival(core, by_device, 1) == iota((192, 192), 0)).astype(F32).astype(BF)


def grower():
    return ((iota((192, 48), 0) >> 2) == iota((192, 48), 1)).astype(F32).astype(BF)


def low_lanes():
    return iota((48, 128), 1) < 64


def pack_kernel(*refs):
    far, packed, near, (tile, square, twice, arrive, leave) = refs[:9], refs[9], refs[10:19], refs[19:]
    arriving = moves(zip(far, near, strict=True), arrive)
    start(*arriving)
    wait(*arriving)
    qkv, out, up, down, qv, outb, upb, gain, shift = near
    square[...] = jnp.zeros_like(square)
    for place, rows in enumerate((qv, outb, gain, shift)):
        square[2 * place : 2 * place + 2, 0:6] = rows[...].astype(F32)
    columns = square[...].T
    grown = jnp.where(iota((8, ROWS), 1) // 4 == iota((8, ROWS), 0), upb[...].astype(F32), 0.0)
    lanes = (iota((ROWS, 128), 1) - 8 == iota((ROWS, 128), 0) % 4).astype(F32)
    hidden = jnp.dot(grown, lanes, preferred_element_type=F32)
    tile[...] = jnp.zeros_like(tile)
    for block in range(4):
        rows, lanes = slice(6 * block, 6 * block + 6), slice(DG * block, DG * block + DG)
        here, there = (slice(0, DG), slice(DG, WIDE))[:: 1 - 2 * (block % 2)]
        tile[rows, here] = out[:, lanes].astype(F32)
        if block < 3:
            tile[rows, there] = qkv[:, lanes].astype(F32)
        tile[rows, WIDE : WIDE + DG] = up[:, lanes].astype(F32)
    tile[SIDE:ROWS, 0:128] = (columns[0:8] + hidden)[0:6]
    tile[:, WIDE + DG : D] = down[...].astype(F32)
    twice[0:ROWS, :] = tile[...].astype(BF)
    twice[ROWS:, :] = tile[...].astype(BF)
    pairs = [(twice, packed.at[2 * ROWS * pair : 2 * ROWS * (pair + 1), :]) for pair in range(CHIPS // 2)]
    leaving = moves(pairs, leave)
    start(*leaving)
    wait(*leaving)


def turn_kernel(tokens, segments, cotangent, turn, x_t, c_t):
    ids = segments[...]
    count0 = jnp.sum((ids == 0).astype(jnp.int32))
    count1 = jnp.sum((ids == 1).astype(jnp.int32))
    start = jnp.where(count0 == LONG, 0, jnp.where(count1 == LONG, count0, count0 + count1))

    def turn_rows(i):
        place = iota((64, TOK), 1) + start
        place = jnp.where(place >= TOK, place - TOK, place)
        turn[part(i, 64), :] = jnp.where(iota((64, TOK), 0) + i * 64 == place, 1.0, 0.0).astype(BF)

    each(8, turn_rows)

    def turn_features(i):
        x_t[part(i, 256), :] = dot(tokens[:, part(i, 256)], turn[...], 0, 0).astype(BF)
        c_t[part(i, 256), :] = dot(cotangent[:, part(i, 256)], turn[...], 0, 0).astype(BF)

    each(3, turn_features)


def moves(pairs, sems):
    return [pltpu.make_async_copy(source, target, sems.at[i]) for i, (source, target) in enumerate(pairs)]


def start(*copies):
    for copy in copies:
        copy.start()


def wait(*copies):
    for copy in copies:
        copy.wait()


def own_core():
    return lax.rem(lax.axis_index("fsdp"), 2)


SPANS = (slice(0, LONG), slice(LONG, TOK))


def layer_kernel(
    segments, mine_far, other, x_far, c_far,
    w_qkv_far, result_far, d_sum_far, packed_far, keep_far, send_far,
    mine, send, x_t, c_t, w_qkv, w_out, w_up, w_down, side, up_bias, q_t, k_t, v_t, ctx_t, probs, probs_small,
    first_low, hat, hat_two, active, slope, stream, d_first, d_upper, d_ctx, result, low_t, branch_pad, packed_t,
    g_qkv, g_out, g_up, g_down, g_side, arrive, leave,
):
    core = own_core()
    quarters = [slice(TILES // 4 * i, TILES // 4 * (i + 1)) for i in range(4)]
    arriving = moves(
        [(mine_far.at[rows, :], mine.at[rows, :]) for rows in quarters] + [(x_far, x_t), (c_far, c_t)],
        arrive,
    )
    leaving = moves(
        [(w_qkv, w_qkv_far), (result, result_far), (stream, d_sum_far)]
        + [(packed_t.at[g], packed_far.at[g]) for g in range(G)]
        + [
            (near.at[rows, :], far.at[rows, :])
            for rows in quarters
            for near, far in ((mine, keep_far), (send, send_far))
        ],
        leave,
    )
    start(*arriving)
    sort, sort_devices, grow = sorter(core), sorter(core, True), grower()

    def both(i, lanes):
        rows = part(i, 96)
        return jnp.concatenate([mine[rows, lanes], other[rows, lanes]], axis=0)

    def place_attention(i):
        here = part(i, 48)
        placed = jnp.dot(sort, both(i, slice(0, WIDE)), preferred_element_type=F32).astype(BF)
        blocks = [placed[48 * block : 48 * block + 48] for block in range(4)]
        for begin, target, left, right in (
            (0, w_out, 0, 1), (WIDE, w_out, 2, 3), (0, w_qkv, 1, 0), (WIDE, w_qkv, 3, 2),
        ):
            target[here, begin : begin + 128] = blocks[left][:, 0:128]
            target[here, begin + 128 : begin + 256] = jnp.where(
                low_lanes(), blocks[left][:, 128:256], blocks[right][:, 128:256]
            )
            target[here, begin + 256 : begin + 384] = blocks[right][:, 256:384]
        side[here, :] = blocks[3][:, 0:128].astype(F32)

    def place_feed(i):
        here, units = part(i, 48), part(i, 192)
        placed = jnp.dot(sort, both(i, slice(WIDE, WIDE + 256)), preferred_element_type=F32).astype(BF)
        for block in range(4):
            w_up[here, DG * block : DG * block + DG] = placed[48 * block : 48 * block + 48, 0:DG]
        rows = jnp.dot(sort_devices, both(i, slice(512, 768)), preferred_element_type=F32)
        w_down[units, :] = rows.astype(BF)
        hidden = jnp.dot(grow, side[here, :].astype(BF), preferred_element_type=F32)
        up_bias[units, :] = lane_sum(jnp.where(pick_hidden(), hidden, 0.0))

    for quarter in range(4):
        wait(arriving[quarter])
        each(4, lambda i, quarter=quarter: place_attention(i + 4 * quarter))
    start(leaving[0])
    wait(arriving[4])

    ids = segments[...]
    count0 = jnp.sum((ids == 0).astype(jnp.int32))
    count1 = jnp.sum((ids == 1).astype(jnp.int32))
    count2 = TOK - count0 - count1
    border = jnp.where(count0 == LONG, count1, jnp.where(count1 == LONG, count2, count0))
    together = (iota((128, 128), 0) < border) == (iota((128, 128), 1) < border)

    def attend(g):
        rows = part(g, DG)
        packed = dot(w_qkv[rows, 0:WIDE], x_t[rows, :], 0, 0)
        k_t[rows, :] = packed[0:DG].astype(BF)
        q_t[rows, :] = ((packed[DG:WIDE] + side[rows, 0:1]).astype(BF).astype(F32) * 0.125).astype(BF)
        packed = dot(w_qkv[rows, 512:768], x_t[rows, :], 0, 0)
        v_t[rows, :] = (packed[64:256] + side[rows, 1:2]).astype(BF)
        for third in range(3):
            head = g * 3 + third
            rows = part(head, HEAD)
            for cols, kept in zip(SPANS, (probs, probs_small), strict=True):
                scores = dot(k_t[rows, cols], q_t[rows, cols], 0, 0)
                if kept is probs_small:
                    scores = jnp.where(together, scores, -1000000000.0)
                power = jnp.exp(scores - jnp.max(scores, axis=0, keepdims=True))
                share = (power * (1.0 / jnp.sum(power, axis=0, keepdims=True))).astype(BF)
                kept[head] = share
                ctx_t[rows, cols] = dot(v_t[rows, cols], share, 1, 0).astype(BF)

    each(G, attend)

    def project(i):
        rows = part(i, 128)
        attended = dot(w_out[:, rows], ctx_t[...], 0, 0) + side[rows, 2:3]
        stream[rows, :] = x_t[rows, :].astype(F32) + attended

    each(6, project)
    (mean_one,) = means(1, lambda rows: (stream[rows, :],))

    def spread_one(rows):
        place_feed(rows.start // BAND)
        return ((stream[rows, :] - mean_one) ** 2,)

    (variance,) = means(1, spread_one)
    scale_one = lax.rsqrt(variance + EPS)

    def norm_one(i):
        rows = part(i, BAND)
        hats = (stream[rows, :] - mean_one) * scale_one
        hat[rows, :] = hats
        first = hats * side[rows, 4:5] + side[rows, 6:7]
        stream[rows, :] = first
        first_low[rows, :] = first.astype(BF)
        if i % 3 == 0:
            place_feed(BANDS + i // 3)

    each(BANDS, norm_one)

    def feed(g):
        rows = part(g, DG)
        for third in range(3):
            units = part(g * 3 + third, 256)
            upper = dot(w_up[rows, 256 * third : 256 * third + 256], first_low[rows, :], 0, 0) + up_bias[units, :]
            below = 0.5 + 0.5 * lax.erf(upper * 0.7071067811865476)
            density = jnp.exp(-0.5 * upper * upper) * 0.3989422804014327
            active[units, :] = (upper * below).astype(BF)
            slope[units, :] = below + upper * density
        units = part(g, D)
        branch = dot(w_down[units, :], active[units, :], 0, 0)[64:256]
        stream[rows, :] += branch + side[rows, 3:4]

    each(G, feed)
    wait(arriving[5])

    (mean_two,) = means(1, lambda rows: (stream[rows, :],))
    (variance,) = means(1, lambda rows: ((stream[rows, :] - mean_two) ** 2,))
    scale_two = lax.rsqrt(variance + EPS)

    def norm_two(rows):
        hats = (stream[rows, :] - mean_two) * scale_two
        hat_two[rows, :] = hats
        result[rows, :] = (hats * side[rows, 5:6] + side[rows, 7:8]).astype(BF)
        slopes = c_t[rows, :].astype(F32) * side[rows, 5:6]
        return slopes, slopes * hats

    lean_two, tilt_two = means(2, norm_two)
    start(leaving[1])
    for g in range(G):
        branch_pad[g, 0:64, :] = jnp.zeros((64, TOK), BF)

    def norm_two_back(i):
        rows = part(i, BAND)
        slopes = c_t[rows, :].astype(F32) * side[rows, 5:6]
        back = scale_two * (slopes - lean_two - hat_two[rows, :] * tilt_two)
        stream[rows, :] = back
        branch_pad[i // 3, 64 + BAND * (i % 3) : 128 + BAND * (i % 3), :] = back.astype(BF)

    each(BANDS, norm_two_back)

    def feed_back(g):
        rows = part(g, DG)
        for third in range(3):
            units = part(g * 3 + third, 256)
            d_active = dot(w_down[units, :], branch_pad[g], 1, 0)
            d_upper[units, :] = (d_active * slope[units, :]).astype(BF)
        d_first[rows, :] = stream[rows, :] + dot(w_up[rows, :], d_upper[part(g, D), :], 1, 0)

    each(G, feed_back)

    def norm_one_sums(rows):
        i = rows.start // BAND
        units = part(i, 256)
        g_down[units, :] = dot(active[units, :], branch_pad[i // 3], 1, 1).astype(BF)
        slopes = d_first[rows, :] * side[rows, 4:5]
        return slopes, slopes * hat[rows, :]

    lean_one, tilt_one = means(2, norm_one_sums)

    def norm_one_back(i):
        rows, units = part(i, BAND), part(i, 256)
        back = scale_one * (d_first[rows, :] * side[rows, 4:5] - lean_one - hat[rows, :] * tilt_one)
        stream[rows, :] = back
        low_t[rows, :] = back.astype(BF)
        span = slice(256 * (i % 3), 256 * (i % 3) + 256)
        g_up[part(i // 3, DG), span] = dot(first_low[part(i // 3, DG), :], d_upper[units, :], 1, 1).astype(BF)

    each(BANDS, norm_one_back)
    start(leaving[2])

    def project_back(i):
        rows = part(i, 128)
        d_ctx[rows, :] = dot(w_out[rows, :], low_t[...], 1, 0).astype(BF)
        g_out[rows, :] = dot(ctx_t[rows, :], low_t[...], 1, 1).astype(BF)

    each(6, project_back)

    unsort, unsort_devices = unsorter(core), unsorter(core, True)

    def side_sums(i):
        rows = part(i, BAND)
        g_side[rows, :] = jnp.zeros((BAND, 128), F32)
        slopes = c_t[rows, :].astype(F32)
        g_side[rows, 5:6] = lane_sum(slopes * hat_two[rows, :])
        g_side[rows, 7:8] = lane_sum(slopes)
        slopes = d_first[rows, :]
        g_side[rows, 4:5] = lane_sum(slopes * hat[rows, :])
        g_side[rows, 6:7] = lane_sum(slopes)
        g_side[rows, 2:3] = lane_sum(low_t[rows, :].astype(F32))
        branch = branch_pad[i // 3, 64 + BAND * (i % 3) : 128 + BAND * (i % 3), :]
        g_side[rows, 3:4] = lane_sum(branch.astype(F32))
        units = part(i, 256)
        up_bias[units, :] = lane_sum(d_upper[units, :].astype(F32))

    def tile_feed(i):
        here, units, rows = part(i, 48), part(i, 192), part(i, 96)
        zero = jnp.zeros((48, 64), BF)
        ups = [jnp.concatenate([g_up[here, DG * block : DG * block + DG], zero], axis=1) for block in range(4)]
        placed = dot(unsort, jnp.concatenate(ups, axis=0), 1, 0)
        downs = dot(unsort_devices, g_down[units, :], 1, 0)
        for target, begin in ((mine, 0), (send, 96)):
            span = slice(begin, begin + 96)
            target[rows, 384:512] = placed[span, 0:128].astype(BF)
            target[rows, 512:640] = (placed[span, 128:256] + downs[span, 0:128]).astype(BF)
            target[rows, 640:768] = downs[span, 128:256].astype(BF)

    def attend_back(g):
        for third in range(3):
            head = g * 3 + third
            rows = part(head, HEAD)
            at = HEAD * third
            for cols, kept in zip(SPANS, (probs, probs_small), strict=True):
                d_out = d_ctx[rows, cols]
                share_low = kept[head]
                share = share_low.astype(F32)
                d_share = dot(v_t[rows, cols], d_out, 0, 0)
                packed_t[g, 3 * DG + at : 3 * DG + at + HEAD, cols] = dot(d_out, share_low, 1, 1).astype(BF)
                d_scores = share * (d_share - jnp.sum(d_share * share, axis=0, keepdims=True))
                d_scores = d_scores.astype(BF)
                packed_t[g, DG + at : DG + at + HEAD, cols] = (0.125 * dot(k_t[rows, cols], d_scores, 1, 0)).astype(BF)
                packed_t[g, at : at + HEAD, cols] = dot(q_t[rows, cols], d_scores, 1, 1).astype(BF)
            side_sums(head)
            tile_feed(head)
        rows = part(g, DG)
        packed_t[g, WIDE : 3 * DG, :] = jnp.zeros((DG, TOK), BF)
        start(leaving[3 + g])
        g_qkv[rows, 0:WIDE] = dot(x_t[rows, :], packed_t[g, 0:WIDE, :], 1, 1).astype(BF)
        g_qkv[rows, 512:768] = dot(x_t[rows, :], packed_t[g, 512:768, :], 1, 1).astype(BF)
        g_side[rows, 0:1] = lane_sum(packed_t[g, DG:WIDE, :].astype(F32))
        g_side[rows, 1:2] = lane_sum(packed_t[g, 3 * DG :, :].astype(F32))
        tile_feed(12 + g)

    each(G, attend_back)

    def tile_attention(i):
        here, units, rows = part(i, 48), part(i, 192), part(i, 96)
        hidden = jnp.where(pick_hidden(), up_bias[units, :], 0.0).astype(BF)
        bias = (g_side[here, :] + dot(grow, hidden, 0, 0)).astype(BF)
        blocks = []
        for begin in (0, WIDE):
            mixed_out, mixed_qkv = g_out[here, begin + 128 : begin + 256], g_qkv[here, begin + 128 : begin + 256]
            for odd in range(2):
                first = (g_qkv[here, 0:128] if begin == 0 else bias) if odd else g_out[here, begin : begin + 128]
                left, right = (mixed_qkv, mixed_out) if odd else (mixed_out, mixed_qkv)
                last = (g_out if odd else g_qkv)[here, begin + 256 : begin + 384]
                blocks.append(jnp.concatenate([first, jnp.where(low_lanes(), left, right), last], axis=1))
        placed = dot(unsort, jnp.concatenate(blocks, axis=0), 1, 0).astype(BF)
        mine[rows, 0:WIDE] = placed[0:96]
        send[rows, 0:WIDE] = placed[96:192]

    for quarter in range(4):
        each(4, lambda i, quarter=quarter: tile_attention(i + 4 * quarter))
        start(*leaving[7 + 2 * quarter : 9 + 2 * quarter])
    wait(*leaving)


def token_kernel(w_qkv, packed_t, d_sum, turn, result, grad_tokens, output, high, low):
    def total(g):
        rows = part(g, DG)
        back = dot(w_qkv[rows, 0:WIDE], packed_t[g, 0:WIDE, :], 1, 0)
        whole = d_sum[rows, :] + back + dot(w_qkv[rows, 512:768], packed_t[g, 512:768, :], 1, 0)
        high[rows, :] = whole.astype(BF)
        low[rows, :] = (whole - high[rows, :].astype(F32)).astype(BF)

    each(G, total)

    def write(i):
        rows = part(i, 256)
        grad_tokens[:, rows] = dot(turn[...], high[rows, :], 1, 1) + dot(turn[...], low[rows, :], 1, 1)
        output[:, rows] = dot(turn[...], result[rows, :], 1, 1).astype(BF)

    each(3, write)


def add_kernel(left_far, right, total_far, left, total, arrive, leave):
    count = 8
    size = TILES // count
    rows = [part(i, size) for i in range(count)]
    arriving = moves([(left_far.at[span, :], left.at[span, :]) for span in rows], arrive)
    leaving = moves([(total.at[span, :], total_far.at[span, :]) for span in rows], leave)
    start(*arriving)
    for i, span in enumerate(rows):
        wait(arriving[i])
        total[span, :] = (left[span, :].astype(F32) + right[span, :].astype(F32)).astype(BF)
        start(leaving[i])
    wait(*leaving)


def sum_kernel(parts, qkv, out, up, down, qv, outb, upb, gain, shift, square):
    total = jnp.zeros((2 * ROWS, D), F32)
    for pair in range(CHIPS // 2):
        total += parts[part(pair, 2 * ROWS), :].astype(F32)
    total = total[0:ROWS] + total[ROWS:]
    for block in range(4):
        rows, lanes = slice(6 * block, 6 * block + 6), slice(DG * block, DG * block + DG)
        here, there = (slice(0, DG), slice(DG, WIDE))[:: 1 - 2 * (block % 2)]
        out[:, lanes] = total[rows, here]
        if block < 3:
            qkv[:, lanes] = total[rows, there]
        up[:, lanes] = total[rows, WIDE : WIDE + DG]
    down[...] = total[:, WIDE + DG : D]
    square[...] = jnp.zeros_like(square)
    square[0:6, :] = total[SIDE:ROWS, 0:128]
    columns = square[...].T
    for place, rows in enumerate((qv, outb, gain, shift)):
        rows[...] = columns[2 * place : 2 * place + 2, 0:6]
    lanes = (iota((128, ROWS), 0) - 8 == iota((128, ROWS), 1) % 4).astype(F32)
    grown = jnp.dot(square[0:8, :], lanes, preferred_element_type=F32, precision=lax.Precision.HIGHEST)
    grown = jnp.where(iota((8, ROWS), 1) // 4 == iota((8, ROWS), 0), grown, 0.0)
    upb[...] = jnp.sum(grown, axis=0, keepdims=True)


FAR = pl.BlockSpec(memory_space=pl.ANY)
NEAR = pl.BlockSpec(memory_space=pltpu.VMEM)


def call(kernel, shapes, scratch, name, limit, flops=0, near=(), sems=(), aliases=()):
    scratch = [pltpu.VMEM(*shape) for shape in scratch] + [pltpu.SemaphoreType.DMA((count,)) for count in sems]

    def specs(count, base):
        return [NEAR if not sems or base + i in near else FAR for i in range(count)]

    def run(*inputs):
        if sems:
            inputs = [x if i in near else pltpu.with_memory_space_constraint(x, pltpu.HBM) for i, x in enumerate(inputs)]
        return pl.pallas_call(
            kernel,
            in_specs=specs(len(inputs), 0),
            out_specs=specs(len(shapes), len(inputs)),
            out_shape=[
                pltpu.HBM(*shape) if sems and len(inputs) + i not in near else jax.ShapeDtypeStruct(*shape)
                for i, shape in enumerate(shapes)
            ],
            scratch_shapes=scratch,
            input_output_aliases=dict(aliases),
            compiler_params=pltpu.CompilerParams(vmem_limit_bytes=limit * MIB),
            cost_estimate=pl.CostEstimate(flops=flops, bytes_accessed=0, transcendentals=0),
            name=name,
        )(*inputs)

    return run


def exchange(array):
    groups = [[y * 32 + i for y in range(4) for i in range(core, 32, 2)] for core in range(2)]
    return lax.all_to_all(array, AXES, 0, 0, axis_index_groups=groups, tiled=True)


def swap(array):
    return lax.ppermute(array, "fsdp", [(i, i ^ 1) for i in range(32)])


def local(
    tokens, segment_ids, qkv_weight, out_weight, up_weight, down_weight,
    qv_bias, out_bias, up_bias, norm_gain, norm_shift, cotangent,
):
    tile, full, low, square, side = ((TILES, D), BF), ((D, TOK), F32), ((D, TOK), BF), ((D, D), BF), ((D, 128), F32)
    probs, small, packed = ((HEADS, LONG, LONG), BF), ((HEADS, 128, 128), BF), ((G, D, TOK), BF)
    units = ((F, 256), BF)
    shards = (
        qkv_weight, out_weight, up_weight, down_weight, qv_bias, out_bias, up_bias.reshape(1, ROWS),
        norm_gain, norm_shift,
    )
    gathered = call(
        pack_kernel, [tile], [*((x.shape, x.dtype) for x in shards), ((ROWS, D), F32), ((128, 128), F32), ((2 * ROWS, D), BF)],
        "pack", 12, sems=(9, CHIPS // 2),
    )(*shards)[0]
    mine = exchange(gathered)
    turn, x_t, c_t = call(
        turn_kernel, [((TOK, TOK), BF), low, low], [], "turn", 60, flops=2 * 2 * TOK * TOK * D
    )(tokens, segment_ids, cotangent)
    mine, x_t = lax.optimization_barrier((mine, x_t))
    w_qkv, result, d_sum, d_packed, keep, send = call(
        layer_kernel,
        [square, low, full, packed, tile, tile],
        [tile, tile, low, low, square, square, square, units, side, ((F, 1), F32), low, low, low, low, probs, small,
         low, full, full, ((F, TOK), BF), ((F, TOK), F32), full, full, ((F, TOK), BF), low, low, low,
         ((G, 256, TOK), BF), packed,
         square, square, square, units, side],
        "layer", 53, flops=40 * 10**9, near=(0, 2), sems=(6, 15),
    )(segment_ids, mine, pltpu.with_memory_space_constraint(swap(mine), pltpu.VMEM), x_t, c_t)
    chip = call(add_kernel, [tile], [tile, tile], "chip_sum", 20, near=(1,), sems=(8, 8))(keep, swap(send))[0]
    chip, d_packed = lax.optimization_barrier((chip, d_packed))
    parts = exchange(chip)
    grad_tokens, output = call(
        token_kernel, [((TOK, D), F32), ((TOK, D), BF)], [low, low], "token_gradient", 60,
        flops=4 * 2 * TOK * TOK * D,
    )(w_qkv, d_packed, d_sum, turn, result)
    qkv, out, up, down, qv, outb, upb, gain, shift = call(
        sum_kernel,
        [((6, QKV), F32), ((6, D), F32), ((6, D), F32), ((ROWS, DG), F32), ((2, 6), F32), ((2, 6), F32),
         ((1, ROWS), F32), ((2, 6), F32), ((2, 6), F32)],
        [((128, 128), F32)], "slice_sum", 12,
    )(parts)
    return output, grad_tokens, qkv, out, up, down, qv, outb, upb.reshape(ROWS), gain, shift


def solution(mesh):
    rows, columns, flat = P(AXES, None), P(None, AXES), P(AXES)
    in_specs = (rows, rows, rows, rows, rows, rows, columns, columns, flat, columns, columns, rows)
    out_specs = (rows, rows, rows, rows, rows, rows, columns, columns, flat, columns, columns)
    return jax.shard_map(local, mesh=mesh, in_specs=in_specs, out_specs=out_specs, check_vma=False)
```

time: 147 us -> 137 us (0.932)
  waiting for transfers between devices: 44.2 us -> 64.1 us
  Pallas kernels: 72.1 us -> 54 us
  starting transfers between devices: 29.5 us -> 17.6 us
    all_to_all x4 -> x2, waiting for transfers between devices: 35.8 us -> 54.9 us  [exchange(): lax.all_to_all(array, AXES, 0, 0, axis_index_groups=groups, tiled=True)]
    pallas_call x11 -> x6, Pallas kernels: 72.1 us -> 54 us  [run(): pl.pallas_call(kernel, in_specs=specs(len(inputs), 0), out_specs=specs(le...]
    all_to_all x4 -> x2, starting transfers between devices: 29.2 us -> 17.4 us  [exchange(): lax.all_to_all(array, AXES, 0, 0, axis_index_groups=groups, tiled=True)]
    ppermute x4 -> x2, waiting for transfers between devices: 8.4 us -> 9.14 us  [swap(): return lax.ppermute(array, 'fsdp', [(i, i ^ 1) for i in range(32)])]
  transfers between devices with their start and end apart: 8 -> 4, of which waited for: 7 -> 4; matrix products, arithmetic and copies ran while one was open for 0% -> 0% of each run, Pallas kernels for 31% -> 7%
where the time goes in v3:
time: 137 us; the launch traced here: 136 us
  waiting for transfers between devices  64.1 us (47%)
  Pallas kernels  54 us (39%)
  starting transfers between devices  17.6 us (13%)
    all_to_all x2, waiting for transfers between devices, exchange(): lax.all_to_all(array, AXES, 0, 0, axis_index_groups=groups, tiled=True)  54.9 us
    pallas_call x6, Pallas kernels, run(): pl.pallas_call(kernel, in_specs=specs(len(inputs), 0), out_specs=specs(le...  54 us
    all_to_all x2, starting transfers between devices, exchange(): lax.all_to_all(array, AXES, 0, 0, axis_index_groups=groups, tiled=True)  17.4 us
    ppermute x2, waiting for transfers between devices, swap(): return lax.ppermute(array, 'fsdp', [(i, i ^ 1) for i in range(32)])  9.14 us
  transfers between devices with their start and end apart: 4, of which 4 were waited for; matrix products, arithmetic and copies ran while one was open for 0% of the time, Pallas kernels for 7%

profile of v3, /device:TPU:0, one launch (start us, length us, event | category | flops | bytes accessed | tf_op | source)
XLA Modules:
  0.0 136.3 jit_solution(3973663750575888442)
XLA Ops:
  0.6 2.7 %pack.1 = bf16[1536,768]{1,0:T(8,128)(2,1)} custom-call(bf16[6,576]{1,0:T(8,128)(2,1)} %refs_0_.1, bf16[6,768]{1,0:T(8,128)(2,1)} %refs_1_.1, bf16[6,768]{1,0:T(8,128)(2,1)} %refs_2_.1, bf16[24,192]{1,0:T(8,128)(2,1)} %refs_3_.1, bf16[2,6]{1,0:T(2,128)(2,1)} %refs_4_.1, bf16[2,6]{1,0:T(2,128)(2,1)} %refs_5_.1, bf16[1,24]{1,0:T(2,128)(2,1)} %bitcast.11, ...), custom_call_target="tpu_custom_call" | custom-call | tf_op jit(solution)/shard_map/pack/pallas_call | solution.py:512
  3.3 11.5 %all-to-all-start = ((bf16[64,24,768]{2,1,0:T(8,128)(2,1)}), bf16[64,24,768]{2,1,0:T(8,128)(2,1)S(1)}, u32[]{:S(2)}, u32[]{:S(2)}) async-start(bf16[64,24,768]{2,1,0:T(8,128)(2,1)} %bitcast.8), calls=%async_computation | async-start | bytes 4718592 | tf_op jit(solution)/shard_map/all_to_all | solution.py:532
  14.9 3.5 %turn.1 = (bf16[512,512]{1,0:T(8,128)(2,1)}, bf16[768,512]{1,0:T(8,128)(2,1)}, bf16[768,512]{1,0:T(8,128)(2,1)}) custom-call(bf16[512,768]{1,0:T(8,128)(2,1)} %tokens.1, s32[1,512]{1,0:T(1,128)} %segments.3, bf16[512,768]{1,0:T(8,128)(2,1)} %cotangent.1), custom_call_target="tpu_custom_call" | custom-call | flops 805306368 | tf_op jit(solution)/shard_map/turn/pallas_call | solution.py:512
  18.4 28.8 %all-to-all-done = bf16[64,24,768]{2,1,0:T(8,128)(2,1)S(1)} async-done(((bf16[64,24,768]{2,1,0:T(8,128)(2,1)}), bf16[64,24,768]{2,1,0:T(8,128)(2,1)S(1)}, u32[]{:S(2)}, u32[]{:S(2)}) %all-to-all-start) | async-done | bytes 2359328 | tf_op jit(solution)/shard_map/all_to_all | solution.py:532
  47.2 0.0 copy-start
  47.2 0.0 collective-permute-start
  47.2 4.5 %collective-permute-done.other = bf16[1536,768]{1,0:T(8,128)(2,1)S(1)} collective-permute-done((bf16[1536,768]{1,0:T(8,128)(2,1)S(1)}, bf16[1536,768]{1,0:T(8,128)(2,1)S(1)}, u32[]{:S(2)}, u32[]{:S(2)}) %collective-permute-start) | collective-permute-done | bytes 2359328 | tf_op jit(solution)/shard_map/ppermute | solution.py:536
  51.7 0.0 copy-done
  51.7 37.6 %layer.1 = (bf16[768,768]{1,0:T(8,128)(2,1)}, bf16[768,512]{1,0:T(8,128)(2,1)}, f32[768,512]{1,0:T(8,128)}, bf16[4,768,512]{2,1,0:T(8,128)(2,1)}, bf16[1536,768]{1,0:T(8,128)(2,1)}, /*index=5*/bf16[1536,768]{1,0:T(8,128)(2,1)}) custom-call(s32[1,512]{1,0:T(1,128)} %segments.3, bf16[1536,768]{1,0:T(8,128)(2,1)} %bitcast.10, ...), custom_call_target="tpu_custom_call" | custom-call | flops 40000000000 | tf_op jit(solution)/shard_map/layer/pallas_call | solution.py:512
  89.4 0.2 collective-permute-start.1
  89.6 4.6 %collective-permute-done.1.right = bf16[1536,768]{1,0:T(8,128)(2,1)S(1)} collective-permute-done((bf16[1536,768]{1,0:T(8,128)(2,1)}, bf16[1536,768]{1,0:T(8,128)(2,1)S(1)}, u32[]{:S(2)}, u32[]{:S(2)}) %collective-permute-start.1) | collective-permute-done | bytes 2359328 | tf_op jit(solution)/shard_map/ppermute | solution.py:536
  94.2 2.6 %chip_sum.1 = bf16[1536,768]{1,0:T(8,128)(2,1)} custom-call(bf16[1536,768]{1,0:T(8,128)(2,1)} %get-tuple-element.40.left_far, bf16[1536,768]{1,0:T(8,128)(2,1)S(1)} %collective-permute-done.1.right), custom_call_target="tpu_custom_call" | custom-call | tf_op jit(solution)/shard_map/chip_sum/pallas_call | solution.py:512
  96.8 5.9 %all-to-all-start.1 = ((bf16[64,24,768]{2,1,0:T(8,128)(2,1)}), bf16[64,24,768]{2,1,0:T(8,128)(2,1)S(1)}, u32[]{:S(2)}, u32[]{:S(2)}) async-start(bf16[64,24,768]{2,1,0:T(8,128)(2,1)} %bitcast.7), calls=%async_computation.1 | async-start | bytes 4718592 | tf_op jit(solution)/shard_map/all_to_all | solution.py:532
  102.6 6.5 %token_gradient.1 = (f32[512,768]{1,0:T(8,128)}, bf16[512,768]{1,0:T(8,128)(2,1)}) custom-call(bf16[768,768]{1,0:T(8,128)(2,1)} %get-tuple-element.39.w_qkv, bf16[4,768,512]{2,1,0:T(8,128)(2,1)} %get-tuple-element.43.packed_t, f32[768,512]{1,0:T(8,128)} %get-tuple-element.44.d_sum, bf16[512,512]{1,0:T(8,128)(2,1)} %get-tuple-element.45.turn, ...), custom_call_target="tpu_custom_call" | custom-call | flops 1610612736 | tf_op jit(solution)/shard_map/token_gradient/pallas_call | solution.py:512
  109.1 26.1 %all-to-all-done.1 = bf16[64,24,768]{2,1,0:T(8,128)(2,1)S(1)} async-done(((bf16[64,24,768]{2,1,0:T(8,128)(2,1)}), bf16[64,24,768]{2,1,0:T(8,128)(2,1)S(1)}, u32[]{:S(2)}, u32[]{:S(2)}) %all-to-all-start.1) | async-done | bytes 2359328 | tf_op jit(solution)/shard_map/all_to_all | solution.py:532
  135.3 1.0 slice_sum.1
Async XLA Ops:
  3.3 43.8 %all-to-all-start = ((bf16[64,24,768]{2,1,0:T(8,128)(2,1)}), bf16[64,24,768]{2,1,0:T(8,128)(2,1)S(1)}, u32[]{:S(2)}, u32[]{:S(2)}) async-start(bf16[64,24,768]{2,1,0:T(8,128)(2,1)} %bitcast.8), calls=%async_computation | async-start | bytes 4718592 | tf_op jit(solution)/shard_map/all_to_all | solution.py:532
  47.2 4.5 %copy-start = (bf16[64,24,768]{2,1,0:T(8,128)(2,1)}, bf16[64,24,768]{2,1,0:T(8,128)(2,1)S(1)}, u32[]{:S(2)}) copy-start(bf16[64,24,768]{2,1,0:T(8,128)(2,1)S(1)} %all-to-all-done) | copy-start | bytes 7077892
  47.2 4.5 %collective-permute-start = (bf16[1536,768]{1,0:T(8,128)(2,1)S(1)}, bf16[1536,768]{1,0:T(8,128)(2,1)S(1)}, u32[]{:S(2)}, u32[]{:S(2)}) collective-permute-start(bf16[1536,768]{1,0:T(8,128)(2,1)S(1)} %bitcast.9), channel_id=1, source_target_pairs={{0,1},{1,0},{2,3},{3,2},{4,5},{5,4},{6,7},{7,6},{8,9},{9,8},{10,11... | collective-permute-start | bytes 7077896 | tf_op jit(solution)/shard_map/ppermute | solution.py:536
  89.4 4.8 %collective-permute-start.1 = (bf16[1536,768]{1,0:T(8,128)(2,1)}, bf16[1536,768]{1,0:T(8,128)(2,1)S(1)}, u32[]{:S(2)}, u32[]{:S(2)}) collective-permute-start(bf16[1536,768]{1,0:T(8,128)(2,1)} %get-tuple-element.41), channel_id=1, source_target_pairs={{0,1},{1,0},{2,3},{3,2},{4,5},{5,4},{6,7},{7,6},{8,9},{9,8},{10,11... | collective-permute-start | bytes 7077896 | tf_op jit(solution)/shard_map/ppermute | solution.py:536
  96.8 38.5 %all-to-all-start.1 = ((bf16[64,24,768]{2,1,0:T(8,128)(2,1)}), bf16[64,24,768]{2,1,0:T(8,128)(2,1)S(1)}, u32[]{:S(2)}, u32[]{:S(2)}) async-start(bf16[64,24,768]{2,1,0:T(8,128)(2,1)} %bitcast.7), calls=%async_computation.1 | async-start | bytes 4718592 | tf_op jit(solution)/shard_map/all_to_all | solution.py:532

commit v4 on v3

--- a/solution.py
+++ b/solution.py
@@ -49,7 +49,7 @@
 
 
 def halves(chunk):
-    return jnp.sum(chunk.reshape(BAND // 8, 8, TOK), axis=0)
+    return jnp.sum(chunk.reshape(chunk.shape[0] // 8, 8, TOK), axis=0)
 
 
 def means(count, bands):
@@ -57,6 +57,19 @@
     for i in range(BANDS):
         sums = [kept + halves(chunk) for kept, chunk in zip(sums, bands(part(i, BAND)), strict=True)]
     return [jnp.sum(total, axis=0, keepdims=True) * (1.0 / D) for total in sums]
+
+
+class Moments:
+    def add(self, chunk):
+        if not hasattr(self, "near"):
+            self.near = jnp.mean(chunk, axis=0, keepdims=True)
+            self.sums = [jnp.zeros((8, TOK), F32)] * 2
+        off = chunk - self.near
+        self.sums = [self.sums[0] + halves(off), self.sums[1] + halves(off * off)]
+
+    def result(self):
+        off, square = (jnp.sum(total, axis=0, keepdims=True) * (1.0 / D) for total in self.sums)
+        return self.near + off, lax.rsqrt(square - off * off + EPS)
 
 
 def lane_sum(chunk):
@@ -161,6 +174,14 @@
         copy.wait()
 
 
+def start_behind(core, *copies):
+    def body(i, nothing):
+        start(*copies)
+        return nothing
+
+    lax.fori_loop(0, 1 + (core >> 1), body, 0)
+
+
 def own_core():
     return lax.rem(lax.axis_index("fsdp"), 2)
 
@@ -173,7 +194,7 @@
     w_qkv_far, result_far, d_sum_far, packed_far, keep_far, send_far,
     mine, send, x_t, c_t, w_qkv, w_out, w_up, w_down, side, up_bias, q_t, k_t, v_t, ctx_t, probs, probs_small,
     first_low, hat, hat_two, active, slope, stream, d_first, d_upper, d_ctx, result, low_t, branch_pad, packed_t,
-    g_qkv, g_out, g_up, g_down, g_side, arrive, leave,
+    g_qkv, g_out, g_up, g_down, g_side, scores, d_scores, d_few, work, arrive, leave,
 ):
     core = own_core()
     quarters = [slice(TILES // 4 * i, TILES // 4 * (i + 1)) for i in range(4)]
@@ -222,10 +243,8 @@
         hidden = jnp.dot(grow, side[here, :].astype(BF), preferred_element_type=F32)
         up_bias[units, :] = lane_sum(jnp.where(pick_hidden(), hidden, 0.0))
 
-    for quarter in range(4):
-        wait(arriving[quarter])
-        each(4, lambda i, quarter=quarter: place_attention(i + 4 * quarter))
-    start(leaving[0])
+    wait(arriving[0])
+    each(4, place_attention)
     wait(arriving[4])
 
     ids = segments[...]
@@ -235,41 +254,61 @@
     border = jnp.where(count0 == LONG, count1, jnp.where(count1 == LONG, count2, count0))
     together = (iota((128, 128), 0) < border) == (iota((128, 128), 1) < border)
 
-    def attend(g):
+    def project_in(g):
         rows = part(g, DG)
         packed = dot(w_qkv[rows, 0:WIDE], x_t[rows, :], 0, 0)
         k_t[rows, :] = packed[0:DG].astype(BF)
         q_t[rows, :] = ((packed[DG:WIDE] + side[rows, 0:1]).astype(BF).astype(F32) * 0.125).astype(BF)
         packed = dot(w_qkv[rows, 512:768], x_t[rows, :], 0, 0)
         v_t[rows, :] = (packed[64:256] + side[rows, 1:2]).astype(BF)
+
+    def score(head):
+        if head % 3 == 0:
+            project_in(head // 3)
+        rows = part(head, HEAD)
+        scores[head % 2] = dot(k_t[rows, 0:LONG], q_t[rows, 0:LONG], 0, 0)
+
+    def shares(logits):
+        power = jnp.exp(logits - jnp.max(logits, axis=0, keepdims=True))
+        return (power * (1.0 / jnp.sum(power, axis=0, keepdims=True))).astype(BF)
+
+    def attend(head):
         for third in range(3):
-            head = g * 3 + third
-            rows = part(head, HEAD)
-            for cols, kept in zip(SPANS, (probs, probs_small), strict=True):
-                scores = dot(k_t[rows, cols], q_t[rows, cols], 0, 0)
-                if kept is probs_small:
-                    scores = jnp.where(together, scores, -1000000000.0)
-                power = jnp.exp(scores - jnp.max(scores, axis=0, keepdims=True))
-                share = (power * (1.0 / jnp.sum(power, axis=0, keepdims=True))).astype(BF)
-                kept[head] = share
-                ctx_t[rows, cols] = dot(v_t[rows, cols], share, 1, 0).astype(BF)
-
-    each(G, attend)
+            cols = part(third, 128)
+            probs[head, :, cols] = shares(scores[head % 2, :, cols])
+        rows = part(head, HEAD)
+        few = dot(k_t[rows, LONG:TOK], q_t[rows, LONG:TOK], 0, 0)
+        probs_small[head] = shares(jnp.where(together, few, -1000000000.0))
+
+    def mix(head):
+        rows = part(head, HEAD)
+        ctx_t[rows, 0:LONG] = dot(v_t[rows, 0:LONG], probs[head], 1, 0).astype(BF)
+        ctx_t[rows, LONG:TOK] = dot(v_t[rows, LONG:TOK], probs_small[head], 1, 0).astype(BF)
+
+    meanwhile = ((4, 5), (6, 7), (8,), (9,), (10, 11), (12,), (13,), (14, 15), (), (), (), ())
+    score(0)
+    for head in range(HEADS):
+        if head + 1 < HEADS:
+            score(head + 1)
+        if head > 0:
+            mix(head - 1)
+        attend(head)
+        if head in (0, 2, 5):
+            wait(arriving[(head + 4) // 3])
+        each(len(meanwhile[head]), lambda i, blocks=meanwhile[head]: place_attention(blocks[i]))
+    mix(HEADS - 1)
+
+    moments_one = Moments()
 
     def project(i):
         rows = part(i, 128)
         attended = dot(w_out[:, rows], ctx_t[...], 0, 0) + side[rows, 2:3]
-        stream[rows, :] = x_t[rows, :].astype(F32) + attended
+        total = x_t[rows, :].astype(F32) + attended
+        stream[rows, :] = total
+        moments_one.add(total)
 
     each(6, project)
-    (mean_one,) = means(1, lambda rows: (stream[rows, :],))
-
-    def spread_one(rows):
-        place_feed(rows.start // BAND)
-        return ((stream[rows, :] - mean_one) ** 2,)
-
-    (variance,) = means(1, spread_one)
-    scale_one = lax.rsqrt(variance + EPS)
+    mean_one, scale_one = moments_one.result()
 
     def norm_one(i):
         rows = part(i, BAND)
@@ -278,30 +317,45 @@
         first = hats * side[rows, 4:5] + side[rows, 6:7]
         stream[rows, :] = first
         first_low[rows, :] = first.astype(BF)
-        if i % 3 == 0:
+        place_feed(i)
+        if i % 3 == 2:
             place_feed(BANDS + i // 3)
 
     each(BANDS, norm_one)
 
-    def feed(g):
+    def raise_up(i):
+        g, third = i // 3, i % 3
         rows = part(g, DG)
-        for third in range(3):
-            units = part(g * 3 + third, 256)
-            upper = dot(w_up[rows, 256 * third : 256 * third + 256], first_low[rows, :], 0, 0) + up_bias[units, :]
+        work[i % 2] = dot(w_up[rows, 256 * third : 256 * third + 256], first_low[rows, :], 0, 0)
+
+    def activate(i):
+        for quarter in range(4):
+            units = part(4 * i + quarter, 64)
+            upper = work[i % 2, part(quarter, 64), :] + up_bias[units, :]
             below = 0.5 + 0.5 * lax.erf(upper * 0.7071067811865476)
             density = jnp.exp(-0.5 * upper * upper) * 0.3989422804014327
             active[units, :] = (upper * below).astype(BF)
             slope[units, :] = below + upper * density
-        units = part(g, D)
+
+    def bring_down(g):
+        rows, units = part(g, DG), part(g, D)
         branch = dot(w_down[units, :], active[units, :], 0, 0)[64:256]
-        stream[rows, :] += branch + side[rows, 3:4]
-
-    each(G, feed)
+        total = stream[rows, :] + branch + side[rows, 3:4]
+        stream[rows, :] = total
+        moments_two.add(total)
+
+    moments_two = Moments()
+    raise_up(0)
+    for i in range(12):
+        if i + 1 < 12:
+            raise_up(i + 1)
+        if i % 3 == 0 and i > 0:
+            bring_down(i // 3 - 1)
+        activate(i)
+    bring_down(3)
     wait(arriving[5])
 
-    (mean_two,) = means(1, lambda rows: (stream[rows, :],))
-    (variance,) = means(1, lambda rows: ((stream[rows, :] - mean_two) ** 2,))
-    scale_two = lax.rsqrt(variance + EPS)
+    mean_two, scale_two = moments_two.result()
 
     def norm_two(rows):
         hats = (stream[rows, :] - mean_two) * scale_two
@@ -311,7 +365,6 @@
         return slopes, slopes * hats
 
     lean_two, tilt_two = means(2, norm_two)
-    start(leaving[1])
     for g in range(G):
         branch_pad[g, 0:64, :] = jnp.zeros((64, TOK), BF)
 
@@ -324,24 +377,32 @@
 
     each(BANDS, norm_two_back)
 
-    def feed_back(g):
+    def raise_back(i):
+        work[i % 2] = dot(w_down[part(i, 256), :], branch_pad[i // 3], 1, 0)
+
+    def activate_back(i):
+        for quarter in range(4):
+            units = part(4 * i + quarter, 64)
+            d_upper[units, :] = (work[i % 2, part(quarter, 64), :] * slope[units, :]).astype(BF)
+
+    def bring_back(g):
         rows = part(g, DG)
-        for third in range(3):
-            units = part(g * 3 + third, 256)
-            d_active = dot(w_down[units, :], branch_pad[g], 1, 0)
-            d_upper[units, :] = (d_active * slope[units, :]).astype(BF)
-        d_first[rows, :] = stream[rows, :] + dot(w_up[rows, :], d_upper[part(g, D), :], 1, 0)
-
-    each(G, feed_back)
-
-    def norm_one_sums(rows):
-        i = rows.start // BAND
-        units = part(i, 256)
-        g_down[units, :] = dot(active[units, :], branch_pad[i // 3], 1, 1).astype(BF)
-        slopes = d_first[rows, :] * side[rows, 4:5]
-        return slopes, slopes * hat[rows, :]
-
-    lean_one, tilt_one = means(2, norm_one_sums)
+        slopes = stream[rows, :] + dot(w_up[rows, :], d_upper[part(g, D), :], 1, 0)
+        d_first[rows, :] = slopes
+        slopes = slopes * side[rows, 4:5]
+        sums_one[:] = [sums_one[0] + halves(slopes), sums_one[1] + halves(slopes * hat[rows, :])]
+
+    sums_one = [jnp.zeros((8, TOK), F32)] * 2
+    raise_back(0)
+    for i in range(12):
+        if i + 1 < 12:
+            raise_back(i + 1)
+        if i % 3 == 0 and i > 0:
+            bring_back(i // 3 - 1)
+        activate_back(i)
+    bring_back(3)
+
+    lean_one, tilt_one = (jnp.sum(total, axis=0, keepdims=True) * (1.0 / D) for total in sums_one)
 
     def norm_one_back(i):
         rows, units = part(i, BAND), part(i, 256)
@@ -350,9 +411,10 @@
         low_t[rows, :] = back.astype(BF)
         span = slice(256 * (i % 3), 256 * (i % 3) + 256)
         g_up[part(i // 3, DG), span] = dot(first_low[part(i // 3, DG), :], d_upper[units, :], 1, 1).astype(BF)
+        g_down[units, :] = dot(active[units, :], branch_pad[i // 3], 1, 1).astype(BF)
 
     each(BANDS, norm_one_back)
-    start(leaving[2])
+    start_behind(core, *leaving[0:3])
 
     def project_back(i):
         rows = part(i, 128)
@@ -390,33 +452,42 @@
             target[rows, 512:640] = (placed[span, 128:256] + downs[span, 0:128]).astype(BF)
             target[rows, 640:768] = downs[span, 128:256].astype(BF)
 
-    def attend_back(g):
+    def score_back(head):
+        rows = part(head, HEAD)
+        scores[head % 2] = dot(v_t[rows, 0:LONG], d_ctx[rows, 0:LONG], 0, 0)
+
+    def shares_back(share, d_share):
+        return (share * (d_share - jnp.sum(d_share * share, axis=0, keepdims=True))).astype(BF)
+
+    def attend_back(head):
+        rows = part(head, HEAD)
         for third in range(3):
-            head = g * 3 + third
-            rows = part(head, HEAD)
-            at = HEAD * third
-            for cols, kept in zip(SPANS, (probs, probs_small), strict=True):
-                d_out = d_ctx[rows, cols]
-                share_low = kept[head]
-                share = share_low.astype(F32)
-                d_share = dot(v_t[rows, cols], d_out, 0, 0)
-                packed_t[g, 3 * DG + at : 3 * DG + at + HEAD, cols] = dot(d_out, share_low, 1, 1).astype(BF)
-                d_scores = share * (d_share - jnp.sum(d_share * share, axis=0, keepdims=True))
-                d_scores = d_scores.astype(BF)
-                packed_t[g, DG + at : DG + at + HEAD, cols] = (0.125 * dot(k_t[rows, cols], d_scores, 1, 0)).astype(BF)
-                packed_t[g, at : at + HEAD, cols] = dot(q_t[rows, cols], d_scores, 1, 1).astype(BF)
-            side_sums(head)
-            tile_feed(head)
+            cols = part(third, 128)
+            d_scores[head % 2, :, cols] = shares_back(probs[head, :, cols].astype(F32), scores[head % 2, :, cols])
+        few = dot(v_t[rows, LONG:TOK], d_ctx[rows, LONG:TOK], 0, 0)
+        d_few[head % 2] = shares_back(probs_small[head].astype(F32), few)
+
+    def mix_back(head):
+        rows = part(head, HEAD)
+        g, at = head // 3, HEAD * (head % 3)
+        for cols, share, d_score in (
+            (slice(0, LONG), probs[head], d_scores[head % 2]),
+            (slice(LONG, TOK), probs_small[head], d_few[head % 2]),
+        ):
+            packed_t[g, 3 * DG + at : 3 * DG + at + HEAD, cols] = dot(d_ctx[rows, cols], share, 1, 1).astype(BF)
+            packed_t[g, DG + at : DG + at + HEAD, cols] = (0.125 * dot(k_t[rows, cols], d_score, 1, 0)).astype(BF)
+            packed_t[g, at : at + HEAD, cols] = dot(q_t[rows, cols], d_score, 1, 1).astype(BF)
+        side_sums(head)
+        tile_feed(head)
+
+    def project_in_back(g):
         rows = part(g, DG)
         packed_t[g, WIDE : 3 * DG, :] = jnp.zeros((DG, TOK), BF)
-        start(leaving[3 + g])
         g_qkv[rows, 0:WIDE] = dot(x_t[rows, :], packed_t[g, 0:WIDE, :], 1, 1).astype(BF)
         g_qkv[rows, 512:768] = dot(x_t[rows, :], packed_t[g, 512:768, :], 1, 1).astype(BF)
         g_side[rows, 0:1] = lane_sum(packed_t[g, DG:WIDE, :].astype(F32))
         g_side[rows, 1:2] = lane_sum(packed_t[g, 3 * DG :, :].astype(F32))
         tile_feed(12 + g)
-
-    each(G, attend_back)
 
     def tile_attention(i):
         here, units, rows = part(i, 48), part(i, 192), part(i, 96)
@@ -434,9 +505,27 @@
         mine[rows, 0:WIDE] = placed[0:96]
         send[rows, 0:WIDE] = placed[96:192]
 
-    for quarter in range(4):
-        each(4, lambda i, quarter=quarter: tile_attention(i + 4 * quarter))
-        start(*leaving[7 + 2 * quarter : 9 + 2 * quarter])
+    score_back(0)
+    for head in range(HEADS):
+        if head + 1 < HEADS:
+            score_back(head + 1)
+        if head > 0:
+            mix_back(head - 1)
+            if head % 3 == 0:
+                project_in_back(head // 3 - 1)
+        attend_back(head)
+        if head > 2:
+            block = (head // 3 - 1) * 4 + head % 3
+            tile_attention(block)
+            if head % 3 == 2:
+                tile_attention(block + 1)
+        if head == 7:
+            start_behind(core, *leaving[3:5], *leaving[7:9])
+    mix_back(HEADS - 1)
+    project_in_back(G - 1)
+    start_behind(core, *leaving[5:7], *leaving[9:13])
+    each(4, lambda i: tile_attention(12 + i))
+    start_behind(core, *leaving[13:15])
     wait(*leaving)
 
 
@@ -562,8 +651,9 @@
         [tile, tile, low, low, square, square, square, units, side, ((F, 1), F32), low, low, low, low, probs, small,
          low, full, full, ((F, TOK), BF), ((F, TOK), F32), full, full, ((F, TOK), BF), low, low, low,
          ((G, 256, TOK), BF), packed,
-         square, square, square, units, side],
-        "layer", 53, flops=40 * 10**9, near=(0, 2), sems=(6, 15),
+         square, square, square, units, side, ((2, LONG, LONG), F32), ((2, LONG, LONG), BF),
+         ((2, 128, 128), BF), ((2, 256, TOK), F32)],
+        "layer", 56, flops=40 * 10**9, near=(0, 2), sems=(6, 15),
     )(segment_ids, mine, pltpu.with_memory_space_constraint(swap(mine), pltpu.VMEM), x_t, c_t)
     chip = call(add_kernel, [tile], [tile, tile], "chip_sum", 20, near=(1,), sems=(8, 8))(keep, swap(send))[0]
     chip, d_packed = lax.optimization_barrier((chip, d_packed))

time: 137 us -> 133 us (0.971)
  Pallas kernels: 54 us -> 50 us
    pallas_call x6, Pallas kernels: 54 us -> 50 us  [run(): pl.pallas_call(kernel, in_specs=specs(len(inputs), 0), out_specs=specs(le...]
  transfers between devices with their start and end apart: 4 -> 4, of which waited for: 4 -> 4; matrix products, arithmetic and copies ran while one was open for 0% -> 0% of each run, Pallas kernels for 7% -> 8%
where the time goes in v4:
time: 133 us; the launch traced here: 132 us
  waiting for transfers between devices  64.1 us (48%)
  Pallas kernels  50 us (38%)
  starting transfers between devices  17.6 us (13%)
    all_to_all x2, waiting for transfers between devices, exchange(): lax.all_to_all(array, AXES, 0, 0, axis_index_groups=groups, tiled=True)  54.9 us
    pallas_call x6, Pallas kernels, run(): pl.pallas_call(kernel, in_specs=specs(len(inputs), 0), out_specs=specs(le...  50 us
    all_to_all x2, starting transfers between devices, exchange(): lax.all_to_all(array, AXES, 0, 0, axis_index_groups=groups, tiled=True)  17.4 us
    ppermute x2, waiting for transfers between devices, swap(): return lax.ppermute(array, 'fsdp', [(i, i ^ 1) for i in range(32)])  9.14 us
  transfers between devices with their start and end apart: 4, of which 4 were waited for; matrix products, arithmetic and copies ran while one was open for 0% of the time, Pallas kernels for 8%

profile of v4, /device:TPU:0, one launch (start us, length us, event | category | flops | bytes accessed | tf_op | source)
XLA Modules:
  0.0 132.4 jit_solution(15905557933787208074)
XLA Ops:
  0.6 2.7 %pack.1 = bf16[1536,768]{1,0:T(8,128)(2,1)} custom-call(bf16[6,576]{1,0:T(8,128)(2,1)} %refs_0_.1, bf16[6,768]{1,0:T(8,128)(2,1)} %refs_1_.1, bf16[6,768]{1,0:T(8,128)(2,1)} %refs_2_.1, bf16[24,192]{1,0:T(8,128)(2,1)} %refs_3_.1, bf16[2,6]{1,0:T(2,128)(2,1)} %refs_4_.1, bf16[2,6]{1,0:T(2,128)(2,1)} %refs_5_.1, bf16[1,24]{1,0:T(2,128)(2,1)} %bitcast.11, ...), custom_call_target="tpu_custom_call" | custom-call | tf_op jit(solution)/shard_map/pack/pallas_call | solution.py:601
  3.3 11.5 %all-to-all-start = ((bf16[64,24,768]{2,1,0:T(8,128)(2,1)}), bf16[64,24,768]{2,1,0:T(8,128)(2,1)S(1)}, u32[]{:S(2)}, u32[]{:S(2)}) async-start(bf16[64,24,768]{2,1,0:T(8,128)(2,1)} %bitcast.8), calls=%async_computation | async-start | bytes 4718592 | tf_op jit(solution)/shard_map/all_to_all | solution.py:621
  14.9 3.5 %turn.1 = (bf16[512,512]{1,0:T(8,128)(2,1)}, bf16[768,512]{1,0:T(8,128)(2,1)}, bf16[768,512]{1,0:T(8,128)(2,1)}) custom-call(bf16[512,768]{1,0:T(8,128)(2,1)} %tokens.1, s32[1,512]{1,0:T(1,128)} %segments.3, bf16[512,768]{1,0:T(8,128)(2,1)} %cotangent.1), custom_call_target="tpu_custom_call" | custom-call | flops 805306368 | tf_op jit(solution)/shard_map/turn/pallas_call | solution.py:601
  18.4 28.8 %all-to-all-done = bf16[64,24,768]{2,1,0:T(8,128)(2,1)S(1)} async-done(((bf16[64,24,768]{2,1,0:T(8,128)(2,1)}), bf16[64,24,768]{2,1,0:T(8,128)(2,1)S(1)}, u32[]{:S(2)}, u32[]{:S(2)}) %all-to-all-start) | async-done | bytes 2359328 | tf_op jit(solution)/shard_map/all_to_all | solution.py:621
  47.2 0.0 copy-start
  47.2 0.0 collective-permute-start
  47.2 4.5 %collective-permute-done.other = bf16[1536,768]{1,0:T(8,128)(2,1)S(1)} collective-permute-done((bf16[1536,768]{1,0:T(8,128)(2,1)S(1)}, bf16[1536,768]{1,0:T(8,128)(2,1)S(1)}, u32[]{:S(2)}, u32[]{:S(2)}) %collective-permute-start) | collective-permute-done | bytes 2359328 | tf_op jit(solution)/shard_map/ppermute | solution.py:625
  51.7 0.0 copy-done
  51.7 33.7 %layer.1 = (bf16[768,768]{1,0:T(8,128)(2,1)}, bf16[768,512]{1,0:T(8,128)(2,1)}, f32[768,512]{1,0:T(8,128)}, bf16[4,768,512]{2,1,0:T(8,128)(2,1)}, bf16[1536,768]{1,0:T(8,128)(2,1)}, /*index=5*/bf16[1536,768]{1,0:T(8,128)(2,1)}) custom-call(s32[1,512]{1,0:T(1,128)} %segments.3, bf16[1536,768]{1,0:T(8,128)(2,1)} %bitcast.10, ...), custom_call_target="tpu_custom_call" | custom-call | flops 40000000000 | tf_op jit(solution)/shard_map/layer/pallas_call | solution.py:601
  85.4 0.2 collective-permute-start.1
  85.6 4.6 %collective-permute-done.1.right = bf16[1536,768]{1,0:T(8,128)(2,1)S(1)} collective-permute-done((bf16[1536,768]{1,0:T(8,128)(2,1)}, bf16[1536,768]{1,0:T(8,128)(2,1)S(1)}, u32[]{:S(2)}, u32[]{:S(2)}) %collective-permute-start.1) | collective-permute-done | bytes 2359328 | tf_op jit(solution)/shard_map/ppermute | solution.py:625
  90.2 2.6 %chip_sum.1 = bf16[1536,768]{1,0:T(8,128)(2,1)} custom-call(bf16[1536,768]{1,0:T(8,128)(2,1)} %get-tuple-element.40.left_far, bf16[1536,768]{1,0:T(8,128)(2,1)S(1)} %collective-permute-done.1.right), custom_call_target="tpu_custom_call" | custom-call | tf_op jit(solution)/shard_map/chip_sum/pallas_call | solution.py:601
  92.8 5.8 %all-to-all-start.1 = ((bf16[64,24,768]{2,1,0:T(8,128)(2,1)}), bf16[64,24,768]{2,1,0:T(8,128)(2,1)S(1)}, u32[]{:S(2)}, u32[]{:S(2)}) async-start(bf16[64,24,768]{2,1,0:T(8,128)(2,1)} %bitcast.7), calls=%async_computation.1 | async-start | bytes 4718592 | tf_op jit(solution)/shard_map/all_to_all | solution.py:621
  98.7 6.5 %token_gradient.1 = (f32[512,768]{1,0:T(8,128)}, bf16[512,768]{1,0:T(8,128)(2,1)}) custom-call(bf16[768,768]{1,0:T(8,128)(2,1)} %get-tuple-element.39.w_qkv, bf16[4,768,512]{2,1,0:T(8,128)(2,1)} %get-tuple-element.43.packed_t, f32[768,512]{1,0:T(8,128)} %get-tuple-element.44.d_sum, bf16[512,512]{1,0:T(8,128)(2,1)} %get-tuple-element.45.turn, ...), custom_call_target="tpu_custom_call" | custom-call | flops 1610612736 | tf_op jit(solution)/shard_map/token_gradient/pallas_call | solution.py:601
  105.2 26.1 %all-to-all-done.1 = bf16[64,24,768]{2,1,0:T(8,128)(2,1)S(1)} async-done(((bf16[64,24,768]{2,1,0:T(8,128)(2,1)}), bf16[64,24,768]{2,1,0:T(8,128)(2,1)S(1)}, u32[]{:S(2)}, u32[]{:S(2)}) %all-to-all-start.1) | async-done | bytes 2359328 | tf_op jit(solution)/shard_map/all_to_all | solution.py:621
  131.3 1.0 slice_sum.1
Async XLA Ops:
  3.3 43.8 %all-to-all-start = ((bf16[64,24,768]{2,1,0:T(8,128)(2,1)}), bf16[64,24,768]{2,1,0:T(8,128)(2,1)S(1)}, u32[]{:S(2)}, u32[]{:S(2)}) async-start(bf16[64,24,768]{2,1,0:T(8,128)(2,1)} %bitcast.8), calls=%async_computation | async-start | bytes 4718592 | tf_op jit(solution)/shard_map/all_to_all | solution.py:621
  47.2 4.5 %copy-start = (bf16[64,24,768]{2,1,0:T(8,128)(2,1)}, bf16[64,24,768]{2,1,0:T(8,128)(2,1)S(1)}, u32[]{:S(2)}) copy-start(bf16[64,24,768]{2,1,0:T(8,128)(2,1)S(1)} %all-to-all-done) | copy-start | bytes 7077892
  47.2 4.5 %collective-permute-start = (bf16[1536,768]{1,0:T(8,128)(2,1)S(1)}, bf16[1536,768]{1,0:T(8,128)(2,1)S(1)}, u32[]{:S(2)}, u32[]{:S(2)}) collective-permute-start(bf16[1536,768]{1,0:T(8,128)(2,1)S(1)} %bitcast.9), channel_id=1, source_target_pairs={{0,1},{1,0},{2,3},{3,2},{4,5},{5,4},{6,7},{7,6},{8,9},{9,8},{10,11... | collective-permute-start | bytes 7077896 | tf_op jit(solution)/shard_map/ppermute | solution.py:625
  85.4 4.8 %collective-permute-start.1 = (bf16[1536,768]{1,0:T(8,128)(2,1)}, bf16[1536,768]{1,0:T(8,128)(2,1)S(1)}, u32[]{:S(2)}, u32[]{:S(2)}) collective-permute-start(bf16[1536,768]{1,0:T(8,128)(2,1)} %get-tuple-element.41), channel_id=1, source_target_pairs={{0,1},{1,0},{2,3},{3,2},{4,5},{5,4},{6,7},{7,6},{8,9},{9,8},{10,11... | collective-permute-start | bytes 7077896 | tf_op jit(solution)/shard_map/ppermute | solution.py:625
  92.8 38.5 %all-to-all-start.1 = ((bf16[64,24,768]{2,1,0:T(8,128)(2,1)}), bf16[64,24,768]{2,1,0:T(8,128)(2,1)S(1)}, u32[]{:S(2)}, u32[]{:S(2)}) async-start(bf16[64,24,768]{2,1,0:T(8,128)(2,1)} %bitcast.7), calls=%async_computation.1 | async-start | bytes 4718592 | tf_op jit(solution)/shard_map/all_to_all | solution.py:621

commit v5 on v4

--- a/solution.py
+++ b/solution.py
@@ -191,8 +191,8 @@
 
 def layer_kernel(
     segments, mine_far, other, x_far, c_far,
-    w_qkv_far, result_far, d_sum_far, packed_far, keep_far, send_far,
-    mine, send, x_t, c_t, w_qkv, w_out, w_up, w_down, side, up_bias, q_t, k_t, v_t, ctx_t, probs, probs_small,
+    w_qkv_far, result_far, d_sum_far, packed_far, keep, send,
+    mine, x_t, c_t, w_qkv, w_out, w_up, w_down, side, up_bias, q_t, k_t, v_t, ctx_t, probs, probs_small,
     first_low, hat, hat_two, active, slope, stream, d_first, d_upper, d_ctx, result, low_t, branch_pad, packed_t,
     g_qkv, g_out, g_up, g_down, g_side, scores, d_scores, d_few, work, arrive, leave,
 ):
@@ -204,12 +204,7 @@
     )
     leaving = moves(
         [(w_qkv, w_qkv_far), (result, result_far), (stream, d_sum_far)]
-        + [(packed_t.at[g], packed_far.at[g]) for g in range(G)]
-        + [
-            (near.at[rows, :], far.at[rows, :])
-            for rows in quarters
-            for near, far in ((mine, keep_far), (send, send_far))
-        ],
+        + [(packed_t.at[g], packed_far.at[g]) for g in range(G)],
         leave,
     )
     start(*arriving)
@@ -288,13 +283,15 @@
     meanwhile = ((4, 5), (6, 7), (8,), (9,), (10, 11), (12,), (13,), (14, 15), (), (), (), ())
     score(0)
     for head in range(HEADS):
-        if head + 1 < HEADS:
-            score(head + 1)
         if head > 0:
             mix(head - 1)
         attend(head)
+        if head + 1 < HEADS:
+            score(head + 1)
         if head in (0, 2, 5):
             wait(arriving[(head + 4) // 3])
+        if head >= 8:
+            each(4, lambda i, head=head: place_feed(4 * (head - 8) + i))
         each(len(meanwhile[head]), lambda i, blocks=meanwhile[head]: place_attention(blocks[i]))
     mix(HEADS - 1)
 
@@ -317,9 +314,6 @@
         first = hats * side[rows, 4:5] + side[rows, 6:7]
         stream[rows, :] = first
         first_low[rows, :] = first.astype(BF)
-        place_feed(i)
-        if i % 3 == 2:
-            place_feed(BANDS + i // 3)
 
     each(BANDS, norm_one)
 
@@ -446,7 +440,7 @@
         ups = [jnp.concatenate([g_up[here, DG * block : DG * block + DG], zero], axis=1) for block in range(4)]
         placed = dot(unsort, jnp.concatenate(ups, axis=0), 1, 0)
         downs = dot(unsort_devices, g_down[units, :], 1, 0)
-        for target, begin in ((mine, 0), (send, 96)):
+        for target, begin in ((keep, 0), (send, 96)):
             span = slice(begin, begin + 96)
             target[rows, 384:512] = placed[span, 0:128].astype(BF)
             target[rows, 512:640] = (placed[span, 128:256] + downs[span, 0:128]).astype(BF)
@@ -502,7 +496,7 @@
                 last = (g_out if odd else g_qkv)[here, begin + 256 : begin + 384]
                 blocks.append(jnp.concatenate([first, jnp.where(low_lanes(), left, right), last], axis=1))
         placed = dot(unsort, jnp.concatenate(blocks, axis=0), 1, 0).astype(BF)
-        mine[rows, 0:WIDE] = placed[0:96]
+        keep[rows, 0:WIDE] = placed[0:96]
         send[rows, 0:WIDE] = placed[96:192]
 
     score_back(0)
@@ -520,12 +514,11 @@
             if head % 3 == 2:
                 tile_attention(block + 1)
         if head == 7:
-            start_behind(core, *leaving[3:5], *leaving[7:9])
+            start_behind(core, *leaving[3:5])
     mix_back(HEADS - 1)
     project_in_back(G - 1)
-    start_behind(core, *leaving[5:7], *leaving[9:13])
+    start_behind(core, *leaving[5:7])
     each(4, lambda i: tile_attention(12 + i))
-    start_behind(core, *leaving[13:15])
     wait(*leaving)
 
 
@@ -547,17 +540,12 @@
     each(3, write)
 
 
-def add_kernel(left_far, right, total_far, left, total, arrive, leave):
-    count = 8
-    size = TILES // count
-    rows = [part(i, size) for i in range(count)]
-    arriving = moves([(left_far.at[span, :], left.at[span, :]) for span in rows], arrive)
+def add_kernel(left, right, total_far, total, leave):
+    rows = [part(i, TILES // 4) for i in range(4)]
     leaving = moves([(total.at[span, :], total_far.at[span, :]) for span in rows], leave)
-    start(*arriving)
     for i, span in enumerate(rows):
-        wait(arriving[i])
         total[span, :] = (left[span, :].astype(F32) + right[span, :].astype(F32)).astype(BF)
-        start(leaving[i])
+        start_behind(own_core(), leaving[i])
     wait(*leaving)
 
 
@@ -589,7 +577,7 @@
 NEAR = pl.BlockSpec(memory_space=pltpu.VMEM)
 
 
-def call(kernel, shapes, scratch, name, limit, flops=0, near=(), sems=(), aliases=()):
+def call(kernel, shapes, scratch, name, limit, flops=0, near=(), held=(), sems=()):
     scratch = [pltpu.VMEM(*shape) for shape in scratch] + [pltpu.SemaphoreType.DMA((count,)) for count in sems]
 
     def specs(count, base):
@@ -603,11 +591,12 @@
             in_specs=specs(len(inputs), 0),
             out_specs=specs(len(shapes), len(inputs)),
             out_shape=[
-                pltpu.HBM(*shape) if sems and len(inputs) + i not in near else jax.ShapeDtypeStruct(*shape)
+                (pltpu.VMEM if len(inputs) + i in held else pltpu.HBM)(*shape)
+                if sems and (len(inputs) + i in held or len(inputs) + i not in near)
+                else jax.ShapeDtypeStruct(*shape)
                 for i, shape in enumerate(shapes)
             ],
             scratch_shapes=scratch,
-            input_output_aliases=dict(aliases),
             compiler_params=pltpu.CompilerParams(vmem_limit_bytes=limit * MIB),
             cost_estimate=pl.CostEstimate(flops=flops, bytes_accessed=0, transcendentals=0),
             name=name,
@@ -648,14 +637,14 @@
     w_qkv, result, d_sum, d_packed, keep, send = call(
         layer_kernel,
         [square, low, full, packed, tile, tile],
-        [tile, tile, low, low, square, square, square, units, side, ((F, 1), F32), low, low, low, low, probs, small,
+        [tile, low, low, square, square, square, units, side, ((F, 1), F32), low, low, low, low, probs, small,
          low, full, full, ((F, TOK), BF), ((F, TOK), F32), full, full, ((F, TOK), BF), low, low, low,
          ((G, 256, TOK), BF), packed,
          square, square, square, units, side, ((2, LONG, LONG), F32), ((2, LONG, LONG), BF),
          ((2, 128, 128), BF), ((2, 256, TOK), F32)],
-        "layer", 56, flops=40 * 10**9, near=(0, 2), sems=(6, 15),
+        "layer", 53, flops=40 * 10**9, near=(0, 2, 9, 10), held=(9, 10), sems=(6, 7),
     )(segment_ids, mine, pltpu.with_memory_space_constraint(swap(mine), pltpu.VMEM), x_t, c_t)
-    chip = call(add_kernel, [tile], [tile, tile], "chip_sum", 20, near=(1,), sems=(8, 8))(keep, swap(send))[0]
+    chip = call(add_kernel, [tile], [tile], "chip_sum", 20, near=(0, 1), sems=(4,))(keep, swap(send))[0]
     chip, d_packed = lax.optimization_barrier((chip, d_packed))
     parts = exchange(chip)
     grad_tokens, output = call(

time: 133 us -> 129 us (0.970)
  Pallas kernels: 50 us -> 46.6 us
    pallas_call x6, Pallas kernels: 50 us -> 46.6 us  [run(): pl.pallas_call(kernel, in_specs=specs(len(inputs), 0), out_specs=specs(le...]
where the time goes in v5:
time: 129 us
  waiting for transfers between devices  63.9 us (50%)
  Pallas kernels  46.6 us (36%)
  starting transfers between devices  17.6 us (14%)
    all_to_all x2, waiting for transfers between devices, exchange(): lax.all_to_all(array, AXES, 0, 0, axis_index_groups=groups, tiled=True)  54.9 us
    pallas_call x6, Pallas kernels, run(): pl.pallas_call(kernel, in_specs=specs(len(inputs), 0), out_specs=specs(le...  46.6 us
    all_to_all x2, starting transfers between devices, exchange(): lax.all_to_all(array, AXES, 0, 0, axis_index_groups=groups, tiled=True)  17.4 us
    ppermute x2, waiting for transfers between devices, swap(): return lax.ppermute(array, 'fsdp', [(i, i ^ 1) for i in range(32)])  8.93 us
  transfers between devices with their start and end apart: 4, of which 4 were waited for; matrix products, arithmetic and copies ran while one was open for 0% of the time, Pallas kernels for 8%

profile of v5, /device:TPU:0, one launch (start us, length us, event | category | flops | bytes accessed | tf_op | source)
XLA Modules:
  0.0 128.8 jit_solution(17422758763035412121)
XLA Ops:
  0.6 2.7 %pack.1 = bf16[1536,768]{1,0:T(8,128)(2,1)} custom-call(bf16[6,576]{1,0:T(8,128)(2,1)} %refs_0_.1, bf16[6,768]{1,0:T(8,128)(2,1)} %refs_1_.1, bf16[6,768]{1,0:T(8,128)(2,1)} %refs_2_.1, bf16[24,192]{1,0:T(8,128)(2,1)} %refs_3_.1, bf16[2,6]{1,0:T(2,128)(2,1)} %refs_4_.1, bf16[2,6]{1,0:T(2,128)(2,1)} %refs_5_.1, bf16[1,24]{1,0:T(2,128)(2,1)} %bitcast.11, ...), custom_call_target="tpu_custom_call" | custom-call | tf_op jit(solution)/shard_map/pack/pallas_call | solution.py:589
  3.3 11.5 %all-to-all-start = ((bf16[64,24,768]{2,1,0:T(8,128)(2,1)}), bf16[64,24,768]{2,1,0:T(8,128)(2,1)S(1)}, u32[]{:S(2)}, u32[]{:S(2)}) async-start(bf16[64,24,768]{2,1,0:T(8,128)(2,1)} %bitcast.8), calls=%async_computation | async-start | bytes 4718592 | tf_op jit(solution)/shard_map/all_to_all | solution.py:610
  14.9 3.5 %turn.1 = (bf16[512,512]{1,0:T(8,128)(2,1)}, bf16[768,512]{1,0:T(8,128)(2,1)}, bf16[768,512]{1,0:T(8,128)(2,1)}) custom-call(bf16[512,768]{1,0:T(8,128)(2,1)} %tokens.1, s32[1,512]{1,0:T(1,128)} %segments.3, bf16[512,768]{1,0:T(8,128)(2,1)} %cotangent.1), custom_call_target="tpu_custom_call" | custom-call | flops 805306368 | tf_op jit(solution)/shard_map/turn/pallas_call | solution.py:589
  18.4 28.8 %all-to-all-done = bf16[64,24,768]{2,1,0:T(8,128)(2,1)S(1)} async-done(((bf16[64,24,768]{2,1,0:T(8,128)(2,1)}), bf16[64,24,768]{2,1,0:T(8,128)(2,1)S(1)}, u32[]{:S(2)}, u32[]{:S(2)}) %all-to-all-start) | async-done | bytes 2359328 | tf_op jit(solution)/shard_map/all_to_all | solution.py:610
  47.2 0.0 copy-start
  47.2 0.0 collective-permute-start
  47.2 4.5 %collective-permute-done.other = bf16[1536,768]{1,0:T(8,128)(2,1)S(1)} collective-permute-done((bf16[1536,768]{1,0:T(8,128)(2,1)S(1)}, bf16[1536,768]{1,0:T(8,128)(2,1)S(1)}, u32[]{:S(2)}, u32[]{:S(2)}) %collective-permute-start) | collective-permute-done | bytes 2359328 | tf_op jit(solution)/shard_map/ppermute | solution.py:614
  51.7 0.0 copy-done
  51.7 31.2 %layer.1 = (bf16[768,768]{1,0:T(8,128)(2,1)}, bf16[768,512]{1,0:T(8,128)(2,1)}, f32[768,512]{1,0:T(8,128)}, bf16[4,768,512]{2,1,0:T(8,128)(2,1)}, bf16[1536,768]...) custom-call(s32[1,512]{1,0:T(1,128)} %segments.3, bf16[1536,768]{1,0:T(8,128)(2,1)} %bitcast.10, ...), custom_call_target="tpu_custom_call" | custom-call | flops 40000000000 | tf_op jit(solution)/shard_map/layer/pallas_call | solution.py:589
  82.9 0.2 collective-permute-start.1
  83.1 4.4 %collective-permute-done.1.right = bf16[1536,768]{1,0:T(8,128)(2,1)S(1)} collective-permute-done((bf16[1536,768]{1,0:T(8,128)(2,1)S(1)}, bf16[1536,768]{1,0:T(8,128)(2,1)S(1)}, u32[]{:S(2)}, u32[]{:S(2)}) %collective-permute-start.1) | collective-permute-done | bytes 2359328 | tf_op jit(solution)/shard_map/ppermute | solution.py:614
  87.5 1.7 %chip_sum.1 = bf16[1536,768]{1,0:T(8,128)(2,1)} custom-call(bf16[1536,768]{1,0:T(8,128)(2,1)S(1)} %get-tuple-element.40.left, bf16[1536,768]{1,0:T(8,128)(2,1)S(1)} %collective-permute-done.1.right), custom_call_target="tpu_custom_call" | custom-call | tf_op jit(solution)/shard_map/chip_sum/pallas_call | solution.py:589
  89.2 5.9 %all-to-all-start.1 = ((bf16[64,24,768]{2,1,0:T(8,128)(2,1)}), bf16[64,24,768]{2,1,0:T(8,128)(2,1)S(1)}, u32[]{:S(2)}, u32[]{:S(2)}) async-start(bf16[64,24,768]{2,1,0:T(8,128)(2,1)} %bitcast.7), calls=%async_computation.1 | async-start | bytes 4718592 | tf_op jit(solution)/shard_map/all_to_all | solution.py:610
  95.1 6.5 %token_gradient.1 = (f32[512,768]{1,0:T(8,128)}, bf16[512,768]{1,0:T(8,128)(2,1)}) custom-call(bf16[768,768]{1,0:T(8,128)(2,1)} %get-tuple-element.39.w_qkv, bf16[4,768,512]{2,1,0:T(8,128)(2,1)} %get-tuple-element.43.packed_t, f32[768,512]{1,0:T(8,128)} %get-tuple-element.44.d_sum, bf16[512,512]{1,0:T(8,128)(2,1)} %get-tuple-element.45.turn, ...), custom_call_target="tpu_custom_call" | custom-call | flops 1610612736 | tf_op jit(solution)/shard_map/token_gradient/pallas_call | solution.py:589
  101.6 26.1 %all-to-all-done.1 = bf16[64,24,768]{2,1,0:T(8,128)(2,1)S(1)} async-done(((bf16[64,24,768]{2,1,0:T(8,128)(2,1)}), bf16[64,24,768]{2,1,0:T(8,128)(2,1)S(1)}, u32[]{:S(2)}, u32[]{:S(2)}) %all-to-all-start.1) | async-done | bytes 2359328 | tf_op jit(solution)/shard_map/all_to_all | solution.py:610
  127.7 1.0 slice_sum.1
Async XLA Ops:
  3.3 43.8 %all-to-all-start = ((bf16[64,24,768]{2,1,0:T(8,128)(2,1)}), bf16[64,24,768]{2,1,0:T(8,128)(2,1)S(1)}, u32[]{:S(2)}, u32[]{:S(2)}) async-start(bf16[64,24,768]{2,1,0:T(8,128)(2,1)} %bitcast.8), calls=%async_computation | async-start | bytes 4718592 | tf_op jit(solution)/shard_map/all_to_all | solution.py:610
  47.2 4.5 %copy-start = (bf16[64,24,768]{2,1,0:T(8,128)(2,1)}, bf16[64,24,768]{2,1,0:T(8,128)(2,1)S(1)}, u32[]{:S(2)}) copy-start(bf16[64,24,768]{2,1,0:T(8,128)(2,1)S(1)} %all-to-all-done) | copy-start | bytes 7077892
  47.2 4.5 %collective-permute-start = (bf16[1536,768]{1,0:T(8,128)(2,1)S(1)}, bf16[1536,768]{1,0:T(8,128)(2,1)S(1)}, u32[]{:S(2)}, u32[]{:S(2)}) collective-permute-start(bf16[1536,768]{1,0:T(8,128)(2,1)S(1)} %bitcast.9), channel_id=1, source_target_pairs={{0,1},{1,0},{2,3},{3,2},{4,5},{5,4},{6,7},{7,6},{8,9},{9,8},{10,11... | collective-permute-start | bytes 7077896 | tf_op jit(solution)/shard_map/ppermute | solution.py:614
  82.9 4.6 %collective-permute-start.1 = (bf16[1536,768]{1,0:T(8,128)(2,1)S(1)}, bf16[1536,768]{1,0:T(8,128)(2,1)S(1)}, u32[]{:S(2)}, u32[]{:S(2)}) collective-permute-start(bf16[1536,768]{1,0:T(8,128)(2,1)S(1)} %get-tuple-element.41), channel_id=1, source_target_pairs={{0,1},{1,0},{2,3},{3,2},{4,5},{5,4},{6,7},{7,6},{8,9},{9,8},{10,11... | collective-permute-start | bytes 7077896 | tf_op jit(solution)/shard_map/ppermute | solution.py:614
  89.2 38.5 %all-to-all-start.1 = ((bf16[64,24,768]{2,1,0:T(8,128)(2,1)}), bf16[64,24,768]{2,1,0:T(8,128)(2,1)S(1)}, u32[]{:S(2)}, u32[]{:S(2)}) async-start(bf16[64,24,768]{2,1,0:T(8,128)(2,1)} %bitcast.7), calls=%async_computation.1 | async-start | bytes 4718592 | tf_op jit(solution)/shard_map/all_to_all | solution.py:610

commit v6 on v5

--- a/solution.py
+++ b/solution.py
@@ -136,7 +136,7 @@
     twice[ROWS:, :] = tile[...].astype(BF)
     pairs = [(twice, packed.at[2 * ROWS * pair : 2 * ROWS * (pair + 1), :]) for pair in range(CHIPS // 2)]
     leaving = moves(pairs, leave)
-    start(*leaving)
+    start_behind(own_core(), *leaving)
     wait(*leaving)
 
 
@@ -413,6 +413,9 @@
     def project_back(i):
         rows = part(i, 128)
         d_ctx[rows, :] = dot(w_out[rows, :], low_t[...], 1, 0).astype(BF)
+
+    def out_gradient(i):
+        rows = part(i, 128)
         g_out[rows, :] = dot(ctx_t[rows, :], low_t[...], 1, 1).astype(BF)
 
     each(6, project_back)
@@ -508,6 +511,8 @@
             if head % 3 == 0:
                 project_in_back(head // 3 - 1)
         attend_back(head)
+        if head < 3:
+            each(2, lambda i, head=head: out_gradient(2 * head + i))
         if head > 2:
             block = (head // 3 - 1) * 4 + head % 3
             tile_attention(block)

time: 129 us -> 129 us (level)
  no operation moved by 1% of the time
where the time goes in v6:
time: 129 us
  waiting for transfers between devices  63.9 us (50%)
  Pallas kernels  46.4 us (36%)
  starting transfers between devices  17.6 us (14%)
    all_to_all x2, waiting for transfers between devices, exchange(): lax.all_to_all(array, AXES, 0, 0, axis_index_groups=groups, tiled=True)  54.9 us
    pallas_call x6, Pallas kernels, run(): pl.pallas_call(kernel, in_specs=specs(len(inputs), 0), out_specs=specs(le...  46.4 us
    all_to_all x2, starting transfers between devices, exchange(): lax.all_to_all(array, AXES, 0, 0, axis_index_groups=groups, tiled=True)  17.4 us
    ppermute x2, waiting for transfers between devices, swap(): return lax.ppermute(array, 'fsdp', [(i, i ^ 1) for i in range(32)])  8.93 us
  transfers between devices with their start and end apart: 4, of which 4 were waited for; matrix products, arithmetic and copies ran while one was open for 0% of the time, Pallas kernels for 8%

profile of v6, /device:TPU:0, one launch (start us, length us, event | category | flops | bytes accessed | tf_op | source)
XLA Modules:
  0.0 128.6 jit_solution(11449499453810196346)
XLA Ops:
  0.6 2.7 %pack.1 = bf16[1536,768]{1,0:T(8,128)(2,1)} custom-call(bf16[6,576]{1,0:T(8,128)(2,1)} %refs_0_.1, bf16[6,768]{1,0:T(8,128)(2,1)} %refs_1_.1, bf16[6,768]{1,0:T(8,128)(2,1)} %refs_2_.1, bf16[24,192]{1,0:T(8,128)(2,1)} %refs_3_.1, bf16[2,6]{1,0:T(2,128)(2,1)} %refs_4_.1, bf16[2,6]{1,0:T(2,128)(2,1)} %refs_5_.1, bf16[1,24]{1,0:T(2,128)(2,1)} %bitcast.11, ...), custom_call_target="tpu_custom_call" | custom-call | tf_op jit(solution)/shard_map/pack/pallas_call | solution.py:594
  3.3 11.5 %all-to-all-start = ((bf16[64,24,768]{2,1,0:T(8,128)(2,1)}), bf16[64,24,768]{2,1,0:T(8,128)(2,1)S(1)}, u32[]{:S(2)}, u32[]{:S(2)}) async-start(bf16[64,24,768]{2,1,0:T(8,128)(2,1)} %bitcast.8), calls=%async_computation | async-start | bytes 4718592 | tf_op jit(solution)/shard_map/all_to_all | solution.py:615
  14.9 3.5 %turn.1 = (bf16[512,512]{1,0:T(8,128)(2,1)}, bf16[768,512]{1,0:T(8,128)(2,1)}, bf16[768,512]{1,0:T(8,128)(2,1)}) custom-call(bf16[512,768]{1,0:T(8,128)(2,1)} %tokens.1, s32[1,512]{1,0:T(1,128)} %segments.3, bf16[512,768]{1,0:T(8,128)(2,1)} %cotangent.1), custom_call_target="tpu_custom_call" | custom-call | flops 805306368 | tf_op jit(solution)/shard_map/turn/pallas_call | solution.py:594
  18.4 28.8 %all-to-all-done = bf16[64,24,768]{2,1,0:T(8,128)(2,1)S(1)} async-done(((bf16[64,24,768]{2,1,0:T(8,128)(2,1)}), bf16[64,24,768]{2,1,0:T(8,128)(2,1)S(1)}, u32[]{:S(2)}, u32[]{:S(2)}) %all-to-all-start) | async-done | bytes 2359328 | tf_op jit(solution)/shard_map/all_to_all | solution.py:615
  47.2 0.0 copy-start
  47.2 0.0 collective-permute-start
  47.2 4.5 %collective-permute-done.other = bf16[1536,768]{1,0:T(8,128)(2,1)S(1)} collective-permute-done((bf16[1536,768]{1,0:T(8,128)(2,1)S(1)}, bf16[1536,768]{1,0:T(8,128)(2,1)S(1)}, u32[]{:S(2)}, u32[]{:S(2)}) %collective-permute-start) | collective-permute-done | bytes 2359328 | tf_op jit(solution)/shard_map/ppermute | solution.py:619
  51.7 0.0 copy-done
  51.7 31.0 %layer.1 = (bf16[768,768]{1,0:T(8,128)(2,1)}, bf16[768,512]{1,0:T(8,128)(2,1)}, f32[768,512]{1,0:T(8,128)}, bf16[4,768,512]{2,1,0:T(8,128)(2,1)}, bf16[1536,768]...) custom-call(s32[1,512]{1,0:T(1,128)} %segments.3, bf16[1536,768]{1,0:T(8,128)(2,1)} %bitcast.10, ...), custom_call_target="tpu_custom_call" | custom-call | flops 40000000000 | tf_op jit(solution)/shard_map/layer/pallas_call | solution.py:594
  82.7 0.2 collective-permute-start.1
  83.0 4.4 %collective-permute-done.1.right = bf16[1536,768]{1,0:T(8,128)(2,1)S(1)} collective-permute-done((bf16[1536,768]{1,0:T(8,128)(2,1)S(1)}, bf16[1536,768]{1,0:T(8,128)(2,1)S(1)}, u32[]{:S(2)}, u32[]{:S(2)}) %collective-permute-start.1) | collective-permute-done | bytes 2359328 | tf_op jit(solution)/shard_map/ppermute | solution.py:619
  87.3 1.7 %chip_sum.1 = bf16[1536,768]{1,0:T(8,128)(2,1)} custom-call(bf16[1536,768]{1,0:T(8,128)(2,1)S(1)} %get-tuple-element.40.left, bf16[1536,768]{1,0:T(8,128)(2,1)S(1)} %collective-permute-done.1.right), custom_call_target="tpu_custom_call" | custom-call | tf_op jit(solution)/shard_map/chip_sum/pallas_call | solution.py:594
  89.0 5.9 %all-to-all-start.1 = ((bf16[64,24,768]{2,1,0:T(8,128)(2,1)}), bf16[64,24,768]{2,1,0:T(8,128)(2,1)S(1)}, u32[]{:S(2)}, u32[]{:S(2)}) async-start(bf16[64,24,768]{2,1,0:T(8,128)(2,1)} %bitcast.7), calls=%async_computation.1 | async-start | bytes 4718592 | tf_op jit(solution)/shard_map/all_to_all | solution.py:615
  94.9 6.5 %token_gradient.1 = (f32[512,768]{1,0:T(8,128)}, bf16[512,768]{1,0:T(8,128)(2,1)}) custom-call(bf16[768,768]{1,0:T(8,128)(2,1)} %get-tuple-element.39.w_qkv, bf16[4,768,512]{2,1,0:T(8,128)(2,1)} %get-tuple-element.43.packed_t, f32[768,512]{1,0:T(8,128)} %get-tuple-element.44.d_sum, bf16[512,512]{1,0:T(8,128)(2,1)} %get-tuple-element.45.turn, ...), custom_call_target="tpu_custom_call" | custom-call | flops 1610612736 | tf_op jit(solution)/shard_map/token_gradient/pallas_call | solution.py:594
  101.4 26.1 %all-to-all-done.1 = bf16[64,24,768]{2,1,0:T(8,128)(2,1)S(1)} async-done(((bf16[64,24,768]{2,1,0:T(8,128)(2,1)}), bf16[64,24,768]{2,1,0:T(8,128)(2,1)S(1)}, u32[]{:S(2)}, u32[]{:S(2)}) %all-to-all-start.1) | async-done | bytes 2359328 | tf_op jit(solution)/shard_map/all_to_all | solution.py:615
  127.5 1.0 slice_sum.1
Async XLA Ops:
  3.3 43.8 %all-to-all-start = ((bf16[64,24,768]{2,1,0:T(8,128)(2,1)}), bf16[64,24,768]{2,1,0:T(8,128)(2,1)S(1)}, u32[]{:S(2)}, u32[]{:S(2)}) async-start(bf16[64,24,768]{2,1,0:T(8,128)(2,1)} %bitcast.8), calls=%async_computation | async-start | bytes 4718592 | tf_op jit(solution)/shard_map/all_to_all | solution.py:615
  47.2 4.5 %copy-start = (bf16[64,24,768]{2,1,0:T(8,128)(2,1)}, bf16[64,24,768]{2,1,0:T(8,128)(2,1)S(1)}, u32[]{:S(2)}) copy-start(bf16[64,24,768]{2,1,0:T(8,128)(2,1)S(1)} %all-to-all-done) | copy-start | bytes 7077892
  47.2 4.5 %collective-permute-start = (bf16[1536,768]{1,0:T(8,128)(2,1)S(1)}, bf16[1536,768]{1,0:T(8,128)(2,1)S(1)}, u32[]{:S(2)}, u32[]{:S(2)}) collective-permute-start(bf16[1536,768]{1,0:T(8,128)(2,1)S(1)} %bitcast.9), channel_id=1, source_target_pairs={{0,1},{1,0},{2,3},{3,2},{4,5},{5,4},{6,7},{7,6},{8,9},{9,8},{10,11... | collective-permute-start | bytes 7077896 | tf_op jit(solution)/shard_map/ppermute | solution.py:619
  82.7 4.6 %collective-permute-start.1 = (bf16[1536,768]{1,0:T(8,128)(2,1)S(1)}, bf16[1536,768]{1,0:T(8,128)(2,1)S(1)}, u32[]{:S(2)}, u32[]{:S(2)}) collective-permute-start(bf16[1536,768]{1,0:T(8,128)(2,1)S(1)} %get-tuple-element.41), channel_id=1, source_target_pairs={{0,1},{1,0},{2,3},{3,2},{4,5},{5,4},{6,7},{7,6},{8,9},{9,8},{10,11... | collective-permute-start | bytes 7077896 | tf_op jit(solution)/shard_map/ppermute | solution.py:619
  89.0 38.5 %all-to-all-start.1 = ((bf16[64,24,768]{2,1,0:T(8,128)(2,1)}), bf16[64,24,768]{2,1,0:T(8,128)(2,1)S(1)}, u32[]{:S(2)}, u32[]{:S(2)}) async-start(bf16[64,24,768]{2,1,0:T(8,128)(2,1)} %bitcast.7), calls=%async_computation.1 | async-start | bytes 4718592 | tf_op jit(solution)/shard_map/all_to_all | solution.py:615

commit v7 on v6

--- a/solution.py
+++ b/solution.py
@@ -190,16 +190,15 @@
 
 
 def layer_kernel(
-    segments, mine_far, other, x_far, c_far,
+    segments, mine, other, x_far, c_far,
     w_qkv_far, result_far, d_sum_far, packed_far, keep, send,
-    mine, x_t, c_t, w_qkv, w_out, w_up, w_down, side, up_bias, q_t, k_t, v_t, ctx_t, probs, probs_small,
+    x_t, c_t, w_qkv, w_out, w_up, w_down, side, up_bias, q_t, k_t, v_t, ctx_t, probs, probs_small,
     first_low, hat, hat_two, active, slope, stream, d_first, d_upper, d_ctx, result, low_t, branch_pad, packed_t,
     g_qkv, g_out, g_up, g_down, g_side, scores, d_scores, d_few, work, arrive, leave,
 ):
     core = own_core()
-    quarters = [slice(TILES // 4 * i, TILES // 4 * (i + 1)) for i in range(4)]
     arriving = moves(
-        [(mine_far.at[rows, :], mine.at[rows, :]) for rows in quarters] + [(x_far, x_t), (c_far, c_t)],
+        [(x_far, x_t), (c_far, c_t)],
         arrive,
     )
     leaving = moves(
@@ -238,9 +237,8 @@
         hidden = jnp.dot(grow, side[here, :].astype(BF), preferred_element_type=F32)
         up_bias[units, :] = lane_sum(jnp.where(pick_hidden(), hidden, 0.0))
 
+    each(4, place_attention)
     wait(arriving[0])
-    each(4, place_attention)
-    wait(arriving[4])
 
     ids = segments[...]
     count0 = jnp.sum((ids == 0).astype(jnp.int32))
@@ -288,8 +286,6 @@
         attend(head)
         if head + 1 < HEADS:
             score(head + 1)
-        if head in (0, 2, 5):
-            wait(arriving[(head + 4) // 3])
         if head >= 8:
             each(4, lambda i, head=head: place_feed(4 * (head - 8) + i))
         each(len(meanwhile[head]), lambda i, blocks=meanwhile[head]: place_attention(blocks[i]))
@@ -347,7 +343,7 @@
             bring_down(i // 3 - 1)
         activate(i)
     bring_down(3)
-    wait(arriving[5])
+    wait(arriving[1])
 
     mean_two, scale_two = moments_two.result()
 
@@ -642,13 +638,13 @@
     w_qkv, result, d_sum, d_packed, keep, send = call(
         layer_kernel,
         [square, low, full, packed, tile, tile],
-        [tile, low, low, square, square, square, units, side, ((F, 1), F32), low, low, low, low, probs, small,
+        [low, low, square, square, square, units, side, ((F, 1), F32), low, low, low, low, probs, small,
          low, full, full, ((F, TOK), BF), ((F, TOK), F32), full, full, ((F, TOK), BF), low, low, low,
          ((G, 256, TOK), BF), packed,
          square, square, square, units, side, ((2, LONG, LONG), F32), ((2, LONG, LONG), BF),
          ((2, 128, 128), BF), ((2, 256, TOK), F32)],
-        "layer", 53, flops=40 * 10**9, near=(0, 2, 9, 10), held=(9, 10), sems=(6, 7),
-    )(segment_ids, mine, pltpu.with_memory_space_constraint(swap(mine), pltpu.VMEM), x_t, c_t)
+        "layer", 51, flops=40 * 10**9, near=(0, 1, 2, 9, 10), held=(9, 10), sems=(2, 7),
+    )(segment_ids, *(pltpu.with_memory_space_constraint(x, pltpu.VMEM) for x in (mine, swap(mine))), x_t, c_t)
     chip = call(add_kernel, [tile], [tile], "chip_sum", 20, near=(0, 1), sems=(4,))(keep, swap(send))[0]
     chip, d_packed = lax.optimization_barrier((chip, d_packed))
     parts = exchange(chip)

time: 129 us -> 128 us (level)
  no operation moved by 1% of the time
where the time goes in v7:
time: 128 us
  waiting for transfers between devices  63.9 us (50%)
  Pallas kernels  45.4 us (35%)
  starting transfers between devices  17.6 us (14%)
    all_to_all x2, waiting for transfers between devices, exchange(): lax.all_to_all(array, AXES, 0, 0, axis_index_groups=groups, tiled=True)  54.9 us
    pallas_call x6, Pallas kernels, run(): pl.pallas_call(kernel, in_specs=specs(len(inputs), 0), out_specs=specs(le...  45.4 us
    all_to_all x2, starting transfers between devices, exchange(): lax.all_to_all(array, AXES, 0, 0, axis_index_groups=groups, tiled=True)  17.4 us
    ppermute x2, waiting for transfers between devices, swap(): return lax.ppermute(array, 'fsdp', [(i, i ^ 1) for i in range(32)])  8.94 us
  transfers between devices with their start and end apart: 4, of which 4 were waited for; matrix products, arithmetic and copies ran while one was open for 0% of the time, Pallas kernels for 8%

profile of v7, /device:TPU:0, one launch (start us, length us, event | category | flops | bytes accessed | tf_op | source)
XLA Modules:
  0.0 127.6 jit_solution(2526885229808281303)
XLA Ops:
  0.6 2.7 %pack.1 = bf16[1536,768]{1,0:T(8,128)(2,1)} custom-call(bf16[6,576]{1,0:T(8,128)(2,1)} %refs_0_.1, bf16[6,768]{1,0:T(8,128)(2,1)} %refs_1_.1, bf16[6,768]{1,0:T(8,128)(2,1)} %refs_2_.1, bf16[24,192]{1,0:T(8,128)(2,1)} %refs_3_.1, bf16[2,6]{1,0:T(2,128)(2,1)} %refs_4_.1, bf16[2,6]{1,0:T(2,128)(2,1)} %refs_5_.1, bf16[1,24]{1,0:T(2,128)(2,1)} %bitcast.11, ...), custom_call_target="tpu_custom_call" | custom-call | tf_op jit(solution)/shard_map/pack/pallas_call | solution.py:590
  3.3 11.5 %all-to-all-start = ((bf16[64,24,768]{2,1,0:T(8,128)(2,1)}), bf16[64,24,768]{2,1,0:T(8,128)(2,1)S(1)}, u32[]{:S(2)}, u32[]{:S(2)}) async-start(bf16[64,24,768]{2,1,0:T(8,128)(2,1)} %bitcast.10), calls=%async_computation | async-start | bytes 4718592 | tf_op jit(solution)/shard_map/all_to_all | solution.py:611
  14.9 3.5 %turn.1 = (bf16[512,512]{1,0:T(8,128)(2,1)}, bf16[768,512]{1,0:T(8,128)(2,1)}, bf16[768,512]{1,0:T(8,128)(2,1)}) custom-call(bf16[512,768]{1,0:T(8,128)(2,1)} %tokens.1, s32[1,512]{1,0:T(1,128)} %segments.3, bf16[512,768]{1,0:T(8,128)(2,1)} %cotangent.1), custom_call_target="tpu_custom_call" | custom-call | flops 805306368 | tf_op jit(solution)/shard_map/turn/pallas_call | solution.py:590
  18.4 28.8 %all-to-all-done = bf16[64,24,768]{2,1,0:T(8,128)(2,1)S(1)} async-done(((bf16[64,24,768]{2,1,0:T(8,128)(2,1)}), bf16[64,24,768]{2,1,0:T(8,128)(2,1)S(1)}, u32[]{:S(2)}, u32[]{:S(2)}) %all-to-all-start) | async-done | bytes 2359328 | tf_op jit(solution)/shard_map/all_to_all | solution.py:611
  47.2 0.0 collective-permute-start
  47.2 4.5 %collective-permute-done.other = bf16[1536,768]{1,0:T(8,128)(2,1)S(1)} collective-permute-done((bf16[1536,768]{1,0:T(8,128)(2,1)S(1)}, bf16[1536,768]{1,0:T(8,128)(2,1)S(1)}, u32[]{:S(2)}, u32[]{:S(2)}) %collective-permute-start) | collective-permute-done | bytes 2359328 | tf_op jit(solution)/shard_map/ppermute | solution.py:615
  51.7 30.0 %layer.1 = (bf16[768,768]{1,0:T(8,128)(2,1)}, bf16[768,512]{1,0:T(8,128)(2,1)}, f32[768,512]{1,0:T(8,128)}, bf16[4,768,512]{2,1,0:T(8,128)(2,1)}, bf16[1536,768]...) custom-call(s32[1,512]{1,0:T(1,128)} %segments.3, bf16[1536,768]{1,0:T(8,128)(2,1)S(1)} %bitcast.8, ...), custom_call_target="tpu_custom_call" | custom-call | flops 40000000000 | tf_op jit(solution)/shard_map/layer/pallas_call | solution.py:590
  81.7 0.2 collective-permute-start.1
  82.0 4.4 %collective-permute-done.1.right = bf16[1536,768]{1,0:T(8,128)(2,1)S(1)} collective-permute-done((bf16[1536,768]{1,0:T(8,128)(2,1)S(1)}, bf16[1536,768]{1,0:T(8,128)(2,1)S(1)}, u32[]{:S(2)}, u32[]{:S(2)}) %collective-permute-start.1) | collective-permute-done | bytes 2359328 | tf_op jit(solution)/shard_map/ppermute | solution.py:615
  86.4 1.7 %chip_sum.1 = bf16[1536,768]{1,0:T(8,128)(2,1)} custom-call(bf16[1536,768]{1,0:T(8,128)(2,1)S(1)} %get-tuple-element.40.left, bf16[1536,768]{1,0:T(8,128)(2,1)S(1)} %collective-permute-done.1.right), custom_call_target="tpu_custom_call" | custom-call | tf_op jit(solution)/shard_map/chip_sum/pallas_call | solution.py:590
  88.0 5.8 %all-to-all-start.1 = ((bf16[64,24,768]{2,1,0:T(8,128)(2,1)}), bf16[64,24,768]{2,1,0:T(8,128)(2,1)S(1)}, u32[]{:S(2)}, u32[]{:S(2)}) async-start(bf16[64,24,768]{2,1,0:T(8,128)(2,1)} %bitcast.9), calls=%async_computation.1 | async-start | bytes 4718592 | tf_op jit(solution)/shard_map/all_to_all | solution.py:611
  93.9 6.5 %token_gradient.1 = (f32[512,768]{1,0:T(8,128)}, bf16[512,768]{1,0:T(8,128)(2,1)}) custom-call(bf16[768,768]{1,0:T(8,128)(2,1)} %get-tuple-element.39.w_qkv, bf16[4,768,512]{2,1,0:T(8,128)(2,1)} %get-tuple-element.43.packed_t, f32[768,512]{1,0:T(8,128)} %get-tuple-element.44.d_sum, bf16[512,512]{1,0:T(8,128)(2,1)} %get-tuple-element.45.turn, ...), custom_call_target="tpu_custom_call" | custom-call | flops 1610612736 | tf_op jit(solution)/shard_map/token_gradient/pallas_call | solution.py:590
  100.4 26.1 %all-to-all-done.1 = bf16[64,24,768]{2,1,0:T(8,128)(2,1)S(1)} async-done(((bf16[64,24,768]{2,1,0:T(8,128)(2,1)}), bf16[64,24,768]{2,1,0:T(8,128)(2,1)S(1)}, u32[]{:S(2)}, u32[]{:S(2)}) %all-to-all-start.1) | async-done | bytes 2359328 | tf_op jit(solution)/shard_map/all_to_all | solution.py:611
  126.5 1.0 slice_sum.1
Async XLA Ops:
  3.3 43.8 %all-to-all-start = ((bf16[64,24,768]{2,1,0:T(8,128)(2,1)}), bf16[64,24,768]{2,1,0:T(8,128)(2,1)S(1)}, u32[]{:S(2)}, u32[]{:S(2)}) async-start(bf16[64,24,768]{2,1,0:T(8,128)(2,1)} %bitcast.10), calls=%async_computation | async-start | bytes 4718592 | tf_op jit(solution)/shard_map/all_to_all | solution.py:611
  47.2 4.5 %collective-permute-start = (bf16[1536,768]{1,0:T(8,128)(2,1)S(1)}, bf16[1536,768]{1,0:T(8,128)(2,1)S(1)}, u32[]{:S(2)}, u32[]{:S(2)}) collective-permute-start(bf16[1536,768]{1,0:T(8,128)(2,1)S(1)} %bitcast.7), channel_id=1, source_target_pairs={{0,1},{1,0},{2,3},{3,2},{4,5},{5,4},{6,7},{7,6},{8,9},{9,8},{10,11... | collective-permute-start | bytes 7077896 | tf_op jit(solution)/shard_map/ppermute | solution.py:615
  81.7 4.6 %collective-permute-start.1 = (bf16[1536,768]{1,0:T(8,128)(2,1)S(1)}, bf16[1536,768]{1,0:T(8,128)(2,1)S(1)}, u32[]{:S(2)}, u32[]{:S(2)}) collective-permute-start(bf16[1536,768]{1,0:T(8,128)(2,1)S(1)} %get-tuple-element.41), channel_id=1, source_target_pairs={{0,1},{1,0},{2,3},{3,2},{4,5},{5,4},{6,7},{7,6},{8,9},{9,8},{10,11... | collective-permute-start | bytes 7077896 | tf_op jit(solution)/shard_map/ppermute | solution.py:615
  88.0 38.5 %all-to-all-start.1 = ((bf16[64,24,768]{2,1,0:T(8,128)(2,1)}), bf16[64,24,768]{2,1,0:T(8,128)(2,1)S(1)}, u32[]{:S(2)}, u32[]{:S(2)}) async-start(bf16[64,24,768]{2,1,0:T(8,128)(2,1)} %bitcast.9), calls=%async_computation.1 | async-start | bytes 4718592 | tf_op jit(solution)/shard_map/all_to_all | solution.py:611
